TPU v7x, 256 devices: a whole 4x4x8 slice. The times are simulated.
256 devices in a mesh: tm: 16 (over x, y), pts: 16 (over z, core).
Axes of the slice: x: 4, y: 4, z: 8, core: 2. Of those that a mesh axis runs over, the one named last changes fastest.
Arguments:
- feats: bfloat16 [16, 4096, 256], P('tm', 'pts'), may hold values from -24 to 24
- query_frame: int32 [16384], P('pts'), may hold values from 0 to 15
- query_pos: int32 [16384], P('pts'), may hold values from 0 to 4095
- time_mix: float32 [16, 16], replicated, may hold values from -1.5 to 1.5
- w_up: bfloat16 [512, 2048], replicated, may hold values from -0.25 to 0.25
- w_down: bfloat16 [2048, 512], replicated, may hold values from -0.125 to 0.125
- w_query: bfloat16 [512, 256], replicated, may hold values from -0.25 to 0.25
Outputs:
- track_x: float32 [16, 16384], P('tm', 'pts')
- track_y: float32 [16, 16384], P('tm', 'pts')
All inputs are finite; a program needn't handle non-finite values.
Results may differ from a plain program's by a relative error of at most 0.04.
Values may be sent and summed in bfloat16 or wider, within the bound.
No kernel may reach another device: no remote copies, remote signals or barrier semaphores. Data moves between devices by JAX's collectives and lax.ppermute only.
A program may use at most 64 MiB of HBM per device.

v0:
```python
import functools

import jax
import jax.numpy as jnp
from jax import lax
from jax.experimental import pallas as pl
from jax.experimental.pallas import tpu as pltpu
from jax.sharding import PartitionSpec as P

GRID = 64
LOG2E = 1.4426950408889634
IN_VMEM = pl.BlockSpec(memory_space=pltpu.VMEM)
NT = (((1,), (1,)), ((), ()))


def params(megabytes):
    return pltpu.CompilerParams(vmem_limit_bytes=megabytes << 20)


def cost(macs, nbytes):
    return pl.CostEstimate(flops=2 * macs, bytes_accessed=nbytes, transcendentals=0)


def tile_bases(aways, rows):
    chips = lax.axis_size("pts") // 2
    place = lax.axis_index("pts")
    core = lax.rem(place, 2)
    bases = []
    for away in aways:
        chip = lax.rem(place // 2 + (away + chips) % chips, chips)
        bases += [(chip * 2 + core) * rows, (chip * 2 + 1 - core) * rows]
    return bases


def pick_kernel(aways, frame_ref, pos_ref, *refs):
    count = 2 * len(aways)
    tiles, before, out = refs[:count], refs[count:-1], refs[-1]
    points = pos_ref.shape[1]
    want = jnp.where(frame_ref[...] == lax.axis_index("tm"), pos_ref[...], -1)
    spread = []
    for first in range(0, points, 128):
        row = jnp.broadcast_to(want[:, first : first + 128], (128, 128))
        spread.append(jnp.transpose(row))
    want = jnp.concatenate(spread, axis=0)
    lane = lax.broadcasted_iota(jnp.int32, (1, 128), 1)
    total = None
    for tile, base in zip(tiles, tile_bases(aways, tiles[0].shape[0])):
        hot = jnp.concatenate(
            [
                (want == lane + (base + first)).astype(jnp.float32).astype(jnp.bfloat16)
                for first in range(0, tile.shape[0], 128)
            ],
            axis=1,
        )
        part = jnp.dot(hot, tile[...], preferred_element_type=jnp.float32)
        total = part if total is None else total + part
    for other in before:
        total = total + other[...].astype(jnp.float32)
    out[...] = total.astype(jnp.bfloat16)


def pick(query_frame, query_pos, aways, tiles, before=()):
    points, width = query_pos.shape[1], tiles[0].shape[1]
    count = len(tiles)
    return pl.pallas_call(
        functools.partial(pick_kernel, aways),
        out_shape=jax.ShapeDtypeStruct((points, width), jnp.bfloat16),
        in_specs=[IN_VMEM] * (2 + count + len(before)),
        out_specs=IN_VMEM,
        compiler_params=params(12),
        cost_estimate=cost(points * count * tiles[0].size, 2 * count * tiles[0].size),
        name="pick",
    )(query_frame, query_pos, *tiles, *before)


def join_kernel(parts_ref, query_ref, copies_ref):
    query = jnp.sum(parts_ref[...].astype(jnp.float32), axis=0).astype(jnp.bfloat16)
    query_ref[...] = query
    for n in range(copies_ref.shape[0]):
        copies_ref[n] = query


def join(parts):
    return pl.pallas_call(
        join_kernel,
        out_shape=[
            jax.ShapeDtypeStruct(parts.shape[1:], parts.dtype),
            jax.ShapeDtypeStruct(parts.shape, parts.dtype),
        ],
        in_specs=[IN_VMEM],
        out_specs=[IN_VMEM] * 2,
        compiler_params=params(6),
        cost_estimate=cost(parts.size, 4 * parts.size),
        name="join",
    )(parts)


def match_kernel(count, block, factor, q_ref, *refs):
    tiles, out, bufs = refs[:count], refs[count], refs[count + 1 :]
    rows = tiles[0].shape[0]
    blocks = q_ref.shape[0] // block

    def score(i, t, top):
        s = lax.dot_general(
            q_ref[i * block : (i + 1) * block],
            tiles[t][...],
            NT,
            preferred_element_type=jnp.float32,
        )
        bufs[i % 2][:, t * rows : (t + 1) * rows] = s
        for h in range(0, rows, 128):
            top = s[:, h : h + 128] if top is None else jnp.maximum(top, s[:, h : h + 128])
        return top

    top = None
    for t in range(count):
        top = score(0, t, top)
    for i in range(blocks):
        high = jnp.max(top, axis=1, keepdims=True) * factor
        top = acc = sums = None
        for t in range(count):
            if i + 1 < blocks:
                top = score(i + 1, t, top)
            expo = jnp.exp2(bufs[i % 2][:, t * rows : (t + 1) * rows] * factor - high)
            for h in range(0, rows, 128):
                sums = expo[:, h : h + 128] if sums is None else sums + expo[:, h : h + 128]
            part = jnp.dot(
                expo.astype(jnp.bfloat16), tiles[t][...], preferred_element_type=jnp.float32
            )
            acc = part if acc is None else acc + part
        total = jnp.sum(sums, axis=1, keepdims=True)
        out[i * block : (i + 1) * block] = (acc / total).astype(jnp.bfloat16)


def match(query, tiles, block=256):
    points, width = query.shape
    count = len(tiles)
    places = count * tiles[0].shape[0]
    return pl.pallas_call(
        functools.partial(match_kernel, count, block, LOG2E * width**-0.5),
        out_shape=jax.ShapeDtypeStruct(query.shape, jnp.bfloat16),
        in_specs=[IN_VMEM] * (1 + count),
        out_specs=IN_VMEM,
        scratch_shapes=[pltpu.VMEM((block, places), jnp.float32)] * 2,
        compiler_params=params(18),
        cost_estimate=cost(2 * points * places * width, 2 * places * width),
        name="match",
    )(query, *tiles)


def rematch_kernel(aways, block, factor, q_ref, *refs):
    tiles, out_x, out_y = refs[:-2], refs[-2], refs[-1]
    count = len(tiles)
    rows = tiles[0].shape[0]
    bases = tile_bases(aways, rows)
    sub = lax.broadcasted_iota(jnp.int32, (8, 1), 0)
    columns = [(2 * (sub + at) + 1).astype(jnp.float32) / GRID - 1.0 for at in range(0, GRID, 8)]
    work = [(i, t) for i in range(q_ref.shape[0] // block) for t in range(count)]

    def score(i, t):
        return lax.dot_general(
            tiles[t][...],
            q_ref[i * block : (i + 1) * block],
            NT,
            preferred_element_type=jnp.float32,
        ).reshape(rows // 8, 8, block)

    ahead = score(*work[0])
    for n, (i, t) in enumerate(work):
        s = ahead
        if n + 1 < len(work):
            ahead = score(*work[n + 1])
        if t == 0:
            top = None
            sums = [None] * len(columns)
            sum_y = jnp.zeros((8, block), jnp.float32)
        high = jnp.max(s, axis=0)
        if top is not None:
            high = jnp.maximum(high, top)
            shrink = jnp.exp2((top - high) * factor)
            sum_y = sum_y * shrink
            sums = [value * shrink for value in sums]
        top = high
        high = high * factor
        first = bases[t] // GRID
        for line in range(rows // GRID):
            y = (2 * (first + line) + 1).astype(jnp.float32) / GRID - 1.0
            here = None
            for c in range(len(columns)):
                expo = jnp.exp2(s[line * len(columns) + c] * factor - high)
                sums[c] = expo if sums[c] is None else sums[c] + expo
                here = expo if here is None else here + expo
            sum_y = sum_y + here * y
        if t == count - 1:
            total = sums[0]
            sum_x = sums[0] * columns[0]
            for value, x in zip(sums[1:], columns[1:]):
                total = total + value
                sum_x = sum_x + value * x
            weight = jnp.exp2((top - jnp.max(top, axis=0, keepdims=True)) * factor)
            total = jnp.sum(total * weight, axis=0, keepdims=True)
            here = slice(i * block, (i + 1) * block)
            out_x[:, here] = jnp.sum(sum_x * weight, axis=0, keepdims=True) / total
            out_y[:, here] = jnp.sum(sum_y * weight, axis=0, keepdims=True) / total


def rematch(refined, aways, tiles, block=256):
    points, width = refined.shape
    count = len(tiles)
    places = count * tiles[0].shape[0]
    return pl.pallas_call(
        functools.partial(rematch_kernel, aways, block, LOG2E * width**-0.5),
        out_shape=[jax.ShapeDtypeStruct((1, points), jnp.float32)] * 2,
        in_specs=[IN_VMEM] * (1 + count),
        out_specs=[IN_VMEM] * 2,
        compiler_params=params(12),
        cost_estimate=cost(points * places * width, 2 * places * width),
        name="rematch",
    )(refined, *tiles)


def prep_kernel(mix_ref, down_ref, to_query_ref, mixes_ref, folded_ref):
    frames = mix_ref.shape[0]
    side = mixes_ref.shape[1]
    repeat = side // frames

    def iota(shape, axis):
        return lax.broadcasted_iota(jnp.int32, shape, axis)

    spread = iota((side, frames), 0) // repeat == iota((side, frames), 1)
    spread = spread.astype(jnp.float32).astype(jnp.bfloat16)
    same = iota((side, side), 0) % repeat == iota((side, side), 1) % repeat
    rest = mix_ref[...]
    for part in range(mixes_ref.shape[0]):
        now = rest.astype(jnp.bfloat16)
        rest = rest - now.astype(jnp.float32)
        rows = jnp.dot(spread, now, preferred_element_type=jnp.float32).astype(jnp.bfloat16)
        full = lax.dot_general(rows, spread, NT, preferred_element_type=jnp.float32)
        mixes_ref[part] = jnp.where(same, full, 0.0).astype(jnp.bfloat16)
    folded_ref[...] = jnp.dot(
        down_ref[...], to_query_ref[...], preferred_element_type=jnp.float32
    ).astype(jnp.bfloat16)


def prep(time_mix, w_down, w_query, side=256, parts=2):
    hidden, width = w_down.shape
    return pl.pallas_call(
        prep_kernel,
        out_shape=[
            jax.ShapeDtypeStruct((parts, side, side), jnp.bfloat16),
            jax.ShapeDtypeStruct((hidden, w_query.shape[1]), jnp.bfloat16),
        ],
        in_specs=[IN_VMEM] * 3,
        out_specs=[IN_VMEM] * 2,
        compiler_params=params(10),
        cost_estimate=cost(w_down.size * w_query.shape[1], 2 * w_down.size),
        name="prep",
    )(time_mix, w_down, w_query)


def mixer_kernel(step, m_ref, q_ref, mixes_ref, up_ref, folded_ref, tq_ref, out_ref):
    frames, points, width = m_ref.shape
    side = mixes_ref.shape[1]
    repeat = side // frames
    hidden = up_ref.shape[1]
    for j in range(points // repeat):
        here = slice(j * repeat, (j + 1) * repeat)
        query = q_ref[here]
        matched = jnp.concatenate([m_ref[f, here] for f in range(frames)], axis=0)
        tokens = jnp.concatenate(
            [matched, jnp.concatenate([query] * frames, axis=0)], axis=1
        ).astype(jnp.float32)
        power = jnp.mean(tokens * tokens, axis=1, keepdims=True)
        normed = (tokens * lax.rsqrt(power + 1e-06)).astype(jnp.bfloat16)
        section = tokens
        for part in range(mixes_ref.shape[0]):
            section = section + jnp.dot(
                mixes_ref[part], normed, preferred_element_type=jnp.float32
            )
        kept = section.astype(jnp.bfloat16)
        section = kept.astype(jnp.float32)
        power = jnp.mean(section * section, axis=1, keepdims=True)
        inner = (section * lax.rsqrt(power + 1e-06)).astype(jnp.bfloat16)
        acc = jnp.dot(kept, tq_ref[...], preferred_element_type=jnp.float32)
        for h in range(0, hidden, step):
            upper = jnp.dot(inner, up_ref[:, h : h + step], preferred_element_type=jnp.float32)
            upper = jax.nn.gelu(upper).astype(jnp.bfloat16)
            acc = acc + jnp.dot(
                upper, folded_ref[h : h + step], preferred_element_type=jnp.float32
            )
        delta = acc.astype(jnp.bfloat16).astype(jnp.float32)
        query = query.astype(jnp.float32)
        for f in range(frames):
            out_ref[f, here] = (query + delta[f * repeat : (f + 1) * repeat]).astype(jnp.bfloat16)


def mixer(matched, query, mixes, w_up, folded, w_query, step=256):
    return pl.pallas_call(
        functools.partial(mixer_kernel, step),
        out_shape=jax.ShapeDtypeStruct(matched.shape, jnp.bfloat16),
        in_specs=[IN_VMEM] * 6,
        out_specs=IN_VMEM,
        compiler_params=params(16),
        cost_estimate=cost(matched.shape[0] * matched.shape[1] * (w_up.size + folded.size), 2 * w_up.size),
        name="mixer",
    )(matched, query, mixes, w_up, folded, w_query)


def ring_pairs(chips, step):
    return [
        (chip * 2 + core, (chip + step) % chips * 2 + core)
        for chip in range(chips)
        for core in range(2)
    ]


def swap_pairs(chips):
    return [(chip * 2 + core, chip * 2 + 1 - core) for chip in range(chips) for core in range(2)]


def shards(feats, query_frame, query_pos, time_mix, w_up, w_down, w_query):
    tile = feats[0]
    points = query_frame.shape[0]
    width = tile.shape[1]
    groups = lax.axis_size("tm")
    share = points // groups
    chips = lax.axis_size("pts") // 2
    query_frame = query_frame.reshape(1, points)
    query_pos = query_pos.reshape(1, points)
    swap = swap_pairs(chips)
    tiles = []
    aways = []

    def add(piece, away):
        tiles.extend([piece, lax.ppermute(piece, "pts", swap)])
        aways.append(away)

    add(tile, 0)
    below = above = tile
    own = ()
    done = 0
    for step in range(1, chips // 2 + 1):
        below = lax.ppermute(below, "pts", ring_pairs(chips, 1))
        if step < chips // 2:
            above = lax.ppermute(above, "pts", ring_pairs(chips, -1))
            add(above, step)
        add(below, -step)
        if step != 1:
            own = (pick(query_frame, query_pos, aways[done:], tiles[2 * done :], own),)
            done = len(aways)
    parts = lax.all_to_all(own[0].reshape(groups, share, width), "tm", 0, 0, tiled=True)
    query_here, copies = join(parts)
    query = lax.all_to_all(copies, "tm", 0, 0, tiled=True).reshape(points, width)
    mixes, folded = prep(time_mix, w_down, w_query)
    matched = match(query, tiles).reshape(groups, share, width)
    matched = lax.all_to_all(matched, "tm", 0, 0, tiled=True)
    refined = mixer(matched, query_here, mixes, w_up, folded, w_query)
    refined = lax.all_to_all(refined, "tm", 0, 0, tiled=True).reshape(points, width)
    return rematch(refined, aways, tiles)


def solution(mesh):
    placed = (P("tm", "pts", None), P("pts"), P("pts"), P(), P(), P(), P())
    return jax.shard_map(
        shards,
        mesh=mesh,
        in_specs=placed,
        out_specs=(P("tm", "pts"), P("tm", "pts")),
        check_vma=False,
    )
```

profile of v0, /device:TPU:8, one launch (start us, length us, event | category | flops | bytes accessed | tf_op | source)
XLA Modules:
  0.0 117.7 jit_solution(2701661266425760896)
XLA Ops:
  0.6 2.0 %collective-permute-start = (bf16[256,256]{1,0:T(8,128)(2,1)}, bf16[256,256]{1,0:T(8,128)(2,1)S(1)}, u32[]{:S(2)}, u32[]{:S(2)}) collective-permute-start(bf16[256,256]{1,0:T(8,128)(2,1)} %bitcast.16), channel_id=1, source_target_pairs={{0,2},{1,3},{2,4},{3,5},{4,6},{5,7},{6,8},{7,9},{8,10},{9,11},{10,... | collective-permute-start | bytes 393224 | tf_op jit(solution)/shard_map/ppermute | solution.py:343
  2.6 4.0 %collective-permute-start.5 = (bf16[256,256]{1,0:T(8,128)(2,1)}, bf16[256,256]{1,0:T(8,128)(2,1)S(1)}, u32[]{:S(2)}, u32[]{:S(2)}) collective-permute-start(bf16[256,256]{1,0:T(8,128)(2,1)} %bitcast.17), channel_id=1, source_target_pairs={{0,14},{1,15},{2,0},{3,1},{4,2},{5,3},{6,4},{7,5},{8,6},{9,7},{10,... | collective-permute-start | bytes 393224 | tf_op jit(solution)/shard_map/ppermute | solution.py:345
  6.7 3.6 %collective-permute-done.refs_4_ = bf16[256,256]{1,0:T(8,128)(2,1)S(1)} collective-permute-done((bf16[256,256]{1,0:T(8,128)(2,1)}, bf16[256,256]{1,0:T(8,128)(2,1)S(1)}, u32[]{:S(2)}, u32[]{:S(2)}) %collective-permute-start) | collective-permute-done | bytes 131104 | tf_op jit(solution)/shard_map/ppermute | solution.py:343
  10.3 3.2 %collective-permute-start.6 = (bf16[256,256]{1,0:T(8,128)(2,1)S(1)}, bf16[256,256]{1,0:T(8,128)(2,1)S(1)}, u32[]{:S(2)}, u32[]{:S(2)}) collective-permute-start(bf16[256,256]{1,0:T(8,128)(2,1)S(1)} %collective-permute-done.5.refs_2_), channel_id=1, source_target_pairs={{0,14},{1,15},{2,0},{3,1},{4,2},{5,3},{6,4},{7,5},{8,6},{9,7},{10,... | collective-permute-start | bytes 393224 | tf_op jit(solution)/shard_map/ppermute | solution.py:345
  13.5 2.9 %collective-permute-done.1.refs_8_ = bf16[256,256]{1,0:T(8,128)(2,1)S(1)} collective-permute-done((bf16[256,256]{1,0:T(8,128)(2,1)S(1)}, bf16[256,256]{1,0:T(8,128)(2,1)S(1)}, u32[]{:S(2)}, u32[]{:S(2)}) %collective-permute-start.1) | collective-permute-done | bytes 131104 | tf_op jit(solution)/shard_map/ppermute | solution.py:343
  17.0 3.2 %collective-permute-start.7 = (bf16[256,256]{1,0:T(8,128)(2,1)S(1)}, bf16[256,256]{1,0:T(8,128)(2,1)S(1)}, u32[]{:S(2)}, u32[]{:S(2)}) collective-permute-start(bf16[256,256]{1,0:T(8,128)(2,1)S(1)} %collective-permute-done.6.refs_6_), channel_id=1, source_target_pairs={{0,14},{1,15},{2,0},{3,1},{4,2},{5,3},{6,4},{7,5},{8,6},{9,7},{10,... | collective-permute-start | bytes 393224 | tf_op jit(solution)/shard_map/ppermute | solution.py:345
  20.2 2.4 %collective-permute-done.2.refs_2_.refs_12_ = bf16[256,256]{1,0:T(8,128)(2,1)S(1)} collective-permute-done((bf16[256,256]{1,0:T(8,128)(2,1)S(1)}, bf16[256,256]{1,0:T(8,128)(2,1)S(1)}, u32[]{:S(2)}, u32[]{:S(2)}) %collective-permute-start.2) | collective-permute-done | bytes 131104 | tf_op jit(solution)/shard_map/ppermute | solution.py:343
  23.8 5.0 %collective-permute-done.3.refs_0_.refs_14_ = bf16[256,256]{1,0:T(8,128)(2,1)S(1)} collective-permute-done((bf16[256,256]{1,0:T(8,128)(2,1)S(1)}, bf16[256,256]{1,0:T(8,128)(2,1)S(1)}, u32[]{:S(2)}, u32[]{:S(2)}) %collective-permute-start.3) | collective-permute-done | bytes 131104 | tf_op jit(solution)/shard_map/ppermute | solution.py:343
  30.3 0.9 copy-done.8
  31.2 1.6 %pick.3.refs_4_ = bf16[1024,256]{1,0:T(8,128)(2,1)S(1)} custom-call(s32[1,1024]{1,0:T(1,128)S(1)} %bitcast.10, s32[1,1024]{1,0:T(1,128)S(1)} %bitcast.13, bf16[256,256]{1,0:T(8,128)(2,1)S(1)} %bitcast.19, bf16[256,256]{1,0:T(8,128)(2,1)S(1)} %collective-permute-done.10.refs_1_, bf16[256,256]{1,0:T(8,128)(2,1)S(1)} %collective-permute-done.5.refs_2_, ...), custom_call_target="tpu_custom_call" | custom-call | flops 1342177280 | bytes 1310720 | tf_op jit(solution)/shard_map/pick/pallas_call | solution.py:65
  32.8 0.8 pick.4.refs_2_
  34.1 18.0 %all_to_all.20.parts_ref = bf16[16,64,256]{2,1,0:T(8,128)(2,1)S(1)} all-to-all(bf16[16,64,256]{2,1,0:T(8,128)(2,1)S(1)} %bitcast.7), channel_id=1, replica_groups=mesh['tm'=16,'pts'=16] {'tm'}, dimensions={0} | all-to-all | bytes 1048576 | tf_op jit(solution)/shard_map/all_to_all | solution.py:351
  52.2 14.3 %all_to_all.21 = bf16[16,64,256]{2,1,0:T(8,128)(2,1)S(1)} all-to-all(bf16[16,64,256]{2,1,0:T(8,128)(2,1)S(1)} %get-tuple-element.6), channel_id=1, replica_groups=mesh['tm'=16,'pts'=16] {'tm'}, dimensions={0} | all-to-all | bytes 1048576 | tf_op jit(solution)/shard_map/all_to_all | solution.py:353
  66.7 7.9 %match.1 = bf16[1024,256]{1,0:T(8,128)(2,1)} custom-call(bf16[1024,256]{1,0:T(8,128)(2,1)S(1)} %bitcast.9, bf16[256,256]{1,0:T(8,128)(2,1)S(1)} %bitcast.20, bf16[256,256]{1,0:T(8,128)(2,1)S(1)} %collective-permute-done.10.refs_1_, bf16[256,256]{1,0:T(8,128)(2,1)S(1)} %collective-permute-done.5.refs_2_, ...), custom_call_target="tpu_custom_call" | custom-call | flops 4294967296 | bytes 2097152 | tf_op jit(solution)/shard_map/match/pallas_call | solution.py:139
  74.5 4.8 %all-to-all-start.2 = ((bf16[16,64,256]{2,1,0:T(8,128)(2,1)}), bf16[16,64,256]{2,1,0:T(8,128)(2,1)S(1)}, u32[]{:S(2)}, u32[]{:S(2)}) async-start(bf16[16,64,256]{2,1,0:T(8,128)(2,1)} %bitcast.5), calls=%async_computation.2 | async-start | bytes 1048576 | tf_op jit(solution)/shard_map/all_to_all | solution.py:356
  79.4 0.9 prep.1
  80.3 1.0 copy-done.6
  81.3 6.9 %all-to-all-done.2.m_ref = bf16[16,64,256]{2,1,0:T(8,128)(2,1)S(1)} async-done(((bf16[16,64,256]{2,1,0:T(8,128)(2,1)}), bf16[16,64,256]{2,1,0:T(8,128)(2,1)S(1)}, u32[]{:S(2)}, u32[]{:S(2)}) %all-to-all-start.2) | async-done | bytes 524320 | tf_op jit(solution)/shard_map/all_to_all | solution.py:356
  88.2 1.6 %copy-done.5 = bf16[512,2048]{1,0:T(8,128)(2,1)S(1)} copy-done((bf16[512,2048]{1,0:T(8,128)(2,1)S(1)}, bf16[512,2048]{1,0:T(8,128)(2,1)}, u32[]{:S(2)}) %copy-start.5) | copy-done | bytes 2097176
  89.8 1.2 %copy-done.7 = bf16[2048,256]{1,0:T(8,128)(2,1)S(1)} copy-done((bf16[2048,256]{1,0:T(8,128)(2,1)S(1)}, bf16[2048,256]{1,0:T(8,128)(2,1)}, u32[]{:S(2)}) %copy-start.7) | copy-done | bytes 1048600
  91.0 0.8 copy-done.37
  91.9 6.3 %mixer.1 = bf16[16,64,256]{2,1,0:T(8,128)(2,1)S(1)} custom-call(bf16[16,64,256]{2,1,0:T(8,128)(2,1)S(1)} %all-to-all-done.2.m_ref, bf16[64,256]{1,0:T(8,128)(2,1)S(1)} %copy-done.37, bf16[2,256,256]{2,1,0:T(8,128)(2,1)S(1)} %get-tuple-element.8.mixes_ref, bf16[512,2048]{1,0:T(8,128)(2,1)S(1)} %copy-done.5, bf16[2048,256]{1,0:T(8,128)(2,1)S(1)} %copy-done.7, ...), custom_call_target="tpu_custom_call" | custom-call | flops 3221225472 | bytes 2097152 | tf_op jit(solution)/shard_map/mixer/pallas_call | solution.py:298
  98.2 13.3 %all_to_all.22 = bf16[16,64,256]{2,1,0:T(8,128)(2,1)S(1)} all-to-all(bf16[16,64,256]{2,1,0:T(8,128)(2,1)S(1)} %mixer.1), channel_id=1, replica_groups=mesh['tm'=16,'pts'=16] {'tm'}, dimensions={0} | all-to-all | bytes 1048576 | tf_op jit(solution)/shard_map/all_to_all | solution.py:358
  111.6 6.1 %rematch.1 = (f32[1,1024]{1,0:T(1,128)}, f32[1,1024]{1,0:T(1,128)}) custom-call(bf16[1024,256]{1,0:T(8,128)(2,1)S(1)} %bitcast.8, bf16[256,256]{1,0:T(8,128)(2,1)S(1)} %bitcast.21, bf16[256,256]{1,0:T(8,128)(2,1)S(1)} %copy-done.21, bf16[256,256]{1,0:T(8,128)(2,1)S(1)} %copy-done.13, bf16[256,256]{1,0:T(8,128)(2,1)S(1)} %copy-done.23, ...), custom_call_target="tpu_custom_call" | custom-call | flops 2147483648 | bytes 2097152 | tf_op jit(solution)/shard_map/rematch/pallas_call | solution.py:211
  (95 shorter events, 3.8 us)
Async XLA Ops:
  0.6 9.6 %collective-permute-start = (bf16[256,256]{1,0:T(8,128)(2,1)}, bf16[256,256]{1,0:T(8,128)(2,1)S(1)}, u32[]{:S(2)}, u32[]{:S(2)}) collective-permute-start(bf16[256,256]{1,0:T(8,128)(2,1)} %bitcast.16), channel_id=1, source_target_pairs={{0,2},{1,3},{2,4},{3,5},{4,6},{5,7},{6,8},{7,9},{8,10},{9,11},{10,... | collective-permute-start | bytes 393224 | tf_op jit(solution)/shard_map/ppermute | solution.py:343
  2.6 7.7 %collective-permute-start.5 = (bf16[256,256]{1,0:T(8,128)(2,1)}, bf16[256,256]{1,0:T(8,128)(2,1)S(1)}, u32[]{:S(2)}, u32[]{:S(2)}) collective-permute-start(bf16[256,256]{1,0:T(8,128)(2,1)} %bitcast.17), channel_id=1, source_target_pairs={{0,14},{1,15},{2,0},{3,1},{4,2},{5,3},{6,4},{7,5},{8,6},{9,7},{10,... | collective-permute-start | bytes 393224 | tf_op jit(solution)/shard_map/ppermute | solution.py:345
  10.3 56.2 %copy-start.10 = (bf16[256,256]{1,0:T(8,128)(2,1)}, bf16[256,256]{1,0:T(8,128)(2,1)S(1)}, u32[]{:S(2)}) copy-start(bf16[256,256]{1,0:T(8,128)(2,1)S(1)} %collective-permute-done.refs_4_) | copy-start | bytes 393220
  10.3 6.2 %collective-permute-start.1 = (bf16[256,256]{1,0:T(8,128)(2,1)S(1)}, bf16[256,256]{1,0:T(8,128)(2,1)S(1)}, u32[]{:S(2)}, u32[]{:S(2)}) collective-permute-start(bf16[256,256]{1,0:T(8,128)(2,1)S(1)} %collective-permute-done.refs_4_), channel_id=1, source_target_pairs={{0,2},{1,3},{2,4},{3,5},{4,6},{5,7},{6,8},{7,9},{8,10},{9,11},{10,... | collective-permute-start | bytes 393224 | tf_op jit(solution)/shard_map/ppermute | solution.py:343
  10.3 56.2 %copy-start.12 = (bf16[256,256]{1,0:T(8,128)(2,1)}, bf16[256,256]{1,0:T(8,128)(2,1)S(1)}, u32[]{:S(2)}) copy-start(bf16[256,256]{1,0:T(8,128)(2,1)S(1)} %collective-permute-done.5.refs_2_) | copy-start | bytes 393220
  10.3 6.7 %collective-permute-start.6 = (bf16[256,256]{1,0:T(8,128)(2,1)S(1)}, bf16[256,256]{1,0:T(8,128)(2,1)S(1)}, u32[]{:S(2)}, u32[]{:S(2)}) collective-permute-start(bf16[256,256]{1,0:T(8,128)(2,1)S(1)} %collective-permute-done.5.refs_2_), channel_id=1, source_target_pairs={{0,14},{1,15},{2,0},{3,1},{4,2},{5,3},{6,4},{7,5},{8,6},{9,7},{10,... | collective-permute-start | bytes 393224 | tf_op jit(solution)/shard_map/ppermute | solution.py:345
  16.5 50.1 %copy-start.14 = (bf16[256,256]{1,0:T(8,128)(2,1)}, bf16[256,256]{1,0:T(8,128)(2,1)S(1)}, u32[]{:S(2)}) copy-start(bf16[256,256]{1,0:T(8,128)(2,1)S(1)} %collective-permute-done.1.refs_8_) | copy-start | bytes 393220
  16.5 6.2 %collective-permute-start.2 = (bf16[256,256]{1,0:T(8,128)(2,1)S(1)}, bf16[256,256]{1,0:T(8,128)(2,1)S(1)}, u32[]{:S(2)}, u32[]{:S(2)}) collective-permute-start(bf16[256,256]{1,0:T(8,128)(2,1)S(1)} %collective-permute-done.1.refs_8_), channel_id=1, source_target_pairs={{0,2},{1,3},{2,4},{3,5},{4,6},{5,7},{6,8},{7,9},{8,10},{9,11},{10,... | collective-permute-start | bytes 393224 | tf_op jit(solution)/shard_map/ppermute | solution.py:343
  16.5 6.2 %collective-permute-start.10 = (bf16[256,256]{1,0:T(8,128)(2,1)}, bf16[256,256]{1,0:T(8,128)(2,1)S(1)}, u32[]{:S(2)}, u32[]{:S(2)}) collective-permute-start(bf16[256,256]{1,0:T(8,128)(2,1)} %bitcast.18), channel_id=1, source_target_pairs={{0,1},{1,0},{2,3},{3,2},{4,5},{5,4},{6,7},{7,6},{8,9},{9,8},{10,11... | collective-permute-start | bytes 393224 | tf_op jit(solution)/shard_map/ppermute | solution.py:335
  16.5 6.3 %collective-permute-start.11 = (bf16[256,256]{1,0:T(8,128)(2,1)S(1)}, bf16[256,256]{1,0:T(8,128)(2,1)S(1)}, u32[]{:S(2)}, u32[]{:S(2)}) collective-permute-start(bf16[256,256]{1,0:T(8,128)(2,1)S(1)} %collective-permute-done.5.refs_2_), channel_id=1, source_target_pairs={{0,1},{1,0},{2,3},{3,2},{4,5},{5,4},{6,7},{7,6},{8,9},{9,8},{10,11... | collective-permute-start | bytes 393224 | tf_op jit(solution)/shard_map/ppermute | solution.py:335
  17.0 49.5 %copy-start.16 = (bf16[256,256]{1,0:T(8,128)(2,1)}, bf16[256,256]{1,0:T(8,128)(2,1)S(1)}, u32[]{:S(2)}) copy-start(bf16[256,256]{1,0:T(8,128)(2,1)S(1)} %collective-permute-done.6.refs_6_) | copy-start | bytes 393220
  17.0 6.3 %collective-permute-start.7 = (bf16[256,256]{1,0:T(8,128)(2,1)S(1)}, bf16[256,256]{1,0:T(8,128)(2,1)S(1)}, u32[]{:S(2)}, u32[]{:S(2)}) collective-permute-start(bf16[256,256]{1,0:T(8,128)(2,1)S(1)} %collective-permute-done.6.refs_6_), channel_id=1, source_target_pairs={{0,14},{1,15},{2,0},{3,1},{4,2},{5,3},{6,4},{7,5},{8,6},{9,7},{10,... | collective-permute-start | bytes 393224 | tf_op jit(solution)/shard_map/ppermute | solution.py:345
  20.2 3.2 %collective-permute-start.12 = (bf16[256,256]{1,0:T(8,128)(2,1)S(1)}, bf16[256,256]{1,0:T(8,128)(2,1)S(1)}, u32[]{:S(2)}, u32[]{:S(2)}) collective-permute-start(bf16[256,256]{1,0:T(8,128)(2,1)S(1)} %collective-permute-done.refs_4_), channel_id=1, source_target_pairs={{0,1},{1,0},{2,3},{3,2},{4,5},{5,4},{6,7},{7,6},{8,9},{9,8},{10,11... | collective-permute-start | bytes 393224 | tf_op jit(solution)/shard_map/ppermute | solution.py:335
  22.6 43.9 %copy-start.18 = (bf16[256,256]{1,0:T(8,128)(2,1)}, bf16[256,256]{1,0:T(8,128)(2,1)S(1)}, u32[]{:S(2)}) copy-start(bf16[256,256]{1,0:T(8,128)(2,1)S(1)} %collective-permute-done.2.refs_2_.refs_12_) | copy-start | bytes 393220
  22.6 6.2 %collective-permute-start.3 = (bf16[256,256]{1,0:T(8,128)(2,1)S(1)}, bf16[256,256]{1,0:T(8,128)(2,1)S(1)}, u32[]{:S(2)}, u32[]{:S(2)}) collective-permute-start(bf16[256,256]{1,0:T(8,128)(2,1)S(1)} %collective-permute-done.2.refs_2_.refs_12_), channel_id=1, source_target_pairs={{0,2},{1,3},{2,4},{3,5},{4,6},{5,7},{6,8},{7,9},{8,10},{9,11},{10,... | collective-permute-start | bytes 393224 | tf_op jit(solution)/shard_map/ppermute | solution.py:343
  22.6 43.9 %copy-start.20 = (bf16[256,256]{1,0:T(8,128)(2,1)}, bf16[256,256]{1,0:T(8,128)(2,1)S(1)}, u32[]{:S(2)}) copy-start(bf16[256,256]{1,0:T(8,128)(2,1)S(1)} %collective-permute-done.10.refs_1_) | copy-start | bytes 393220
  22.7 6.2 %collective-permute-start.13 = (bf16[256,256]{1,0:T(8,128)(2,1)S(1)}, bf16[256,256]{1,0:T(8,128)(2,1)S(1)}, u32[]{:S(2)}, u32[]{:S(2)}) collective-permute-start(bf16[256,256]{1,0:T(8,128)(2,1)S(1)} %collective-permute-done.6.refs_6_), channel_id=1, source_target_pairs={{0,1},{1,0},{2,3},{3,2},{4,5},{5,4},{6,7},{7,6},{8,9},{9,8},{10,11... | collective-permute-start | bytes 393224 | tf_op jit(solution)/shard_map/ppermute | solution.py:335
  22.8 43.8 %copy-start.22 = (bf16[256,256]{1,0:T(8,128)(2,1)}, bf16[256,256]{1,0:T(8,128)(2,1)S(1)}, u32[]{:S(2)}) copy-start(bf16[256,256]{1,0:T(8,128)(2,1)S(1)} %collective-permute-done.11.refs_3_) | copy-start | bytes 393220
  22.8 6.1 %collective-permute-start.14 = (bf16[256,256]{1,0:T(8,128)(2,1)S(1)}, bf16[256,256]{1,0:T(8,128)(2,1)S(1)}, u32[]{:S(2)}, u32[]{:S(2)}) collective-permute-start(bf16[256,256]{1,0:T(8,128)(2,1)S(1)} %collective-permute-done.1.refs_8_), channel_id=1, source_target_pairs={{0,1},{1,0},{2,3},{3,2},{4,5},{5,4},{6,7},{7,6},{8,9},{9,8},{10,11... | collective-permute-start | bytes 393224 | tf_op jit(solution)/shard_map/ppermute | solution.py:335
  23.3 43.3 %copy-start.24 = (bf16[256,256]{1,0:T(8,128)(2,1)}, bf16[256,256]{1,0:T(8,128)(2,1)S(1)}, u32[]{:S(2)}) copy-start(bf16[256,256]{1,0:T(8,128)(2,1)S(1)} %collective-permute-done.7.refs_0_.refs_10_) | copy-start | bytes 393220
  23.3 9.5 %collective-permute-start.8 = (bf16[256,256]{1,0:T(8,128)(2,1)S(1)}, bf16[256,256]{1,0:T(8,128)(2,1)S(1)}, u32[]{:S(2)}, u32[]{:S(2)}) collective-permute-start(bf16[256,256]{1,0:T(8,128)(2,1)S(1)} %collective-permute-done.7.refs_0_.refs_10_), channel_id=1, source_target_pairs={{0,1},{1,0},{2,3},{3,2},{4,5},{5,4},{6,7},{7,6},{8,9},{9,8},{10,11... | collective-permute-start | bytes 393224 | tf_op jit(solution)/shard_map/ppermute | solution.py:335
  23.4 9.4 %collective-permute-start.9 = (bf16[256,256]{1,0:T(8,128)(2,1)S(1)}, bf16[256,256]{1,0:T(8,128)(2,1)S(1)}, u32[]{:S(2)}, u32[]{:S(2)}) collective-permute-start(bf16[256,256]{1,0:T(8,128)(2,1)S(1)} %collective-permute-done.2.refs_2_.refs_12_), channel_id=1, source_target_pairs={{0,1},{1,0},{2,3},{3,2},{4,5},{5,4},{6,7},{7,6},{8,9},{9,8},{10,11... | collective-permute-start | bytes 393224 | tf_op jit(solution)/shard_map/ppermute | solution.py:335
  28.8 4.8 %collective-permute-start.4 = (bf16[256,256]{1,0:T(8,128)(2,1)S(1)}, bf16[256,256]{1,0:T(8,128)(2,1)S(1)}, u32[]{:S(2)}, u32[]{:S(2)}) collective-permute-start(bf16[256,256]{1,0:T(8,128)(2,1)S(1)} %collective-permute-done.3.refs_0_.refs_14_), channel_id=1, source_target_pairs={{0,1},{1,0},{2,3},{3,2},{4,5},{5,4},{6,7},{7,6},{8,9},{9,8},{10,11... | collective-permute-start | bytes 393224 | tf_op jit(solution)/shard_map/ppermute | solution.py:335
  74.5 13.6 %all-to-all-start.2 = ((bf16[16,64,256]{2,1,0:T(8,128)(2,1)}), bf16[16,64,256]{2,1,0:T(8,128)(2,1)S(1)}, u32[]{:S(2)}, u32[]{:S(2)}) async-start(bf16[16,64,256]{2,1,0:T(8,128)(2,1)} %bitcast.5), calls=%async_computation.2 | async-start | bytes 1048576 | tf_op jit(solution)/shard_map/all_to_all | solution.py:356
  (30 other events, 535.6 us)
where the time goes:
time: 118 us
  blocking collectives  45.6 us (39%)
  Pallas kernels  24.1 us (20%)
  waiting for transfers between devices  20.9 us (18%)
  starting transfers between devices  18.9 us (16%)
  local copies, waits for them, and re-layouts  7.02 us (6%)
    all_to_all x1, blocking collectives, shards(): lax.all_to_all(own[0].reshape(groups, share, width), 'tm', 0, 0, tiled=True)  18 us
    all_to_all x1, blocking collectives, shards(): lax.all_to_all(copies, 'tm', 0, 0, tiled=True).reshape(points, width)  14.3 us
    ppermute x4, waiting for transfers between devices, shards(): below = lax.ppermute(below, 'pts', ring_pairs(chips, 1))  14 us
    all_to_all x1, blocking collectives, shards(): lax.all_to_all(refined, 'tm', 0, 0, tiled=True).reshape(points, width)  13.3 us
    ppermute x3, starting transfers between devices, shards(): above = lax.ppermute(above, 'pts', ring_pairs(chips, -1))  10.5 us
    pallas_call x1, Pallas kernels, match(): pl.pallas_call(functools.partial(match_kernel, count, block, LOG2E * widt...  7.88 us
    unnamed x76, local copies, waits for them, and re-layouts  7.02 us
    all_to_all x1, waiting for transfers between devices, shards(): matched = lax.all_to_all(matched, 'tm', 0, 0, tiled=True)  6.89 us
  transfers between devices with their start and end apart: 16, of which 5 were waited for; matrix products, arithmetic and copies ran while one was open for 0% of the time, Pallas kernels for 3%

commit v1 on v0

--- a/solution.py
+++ b/solution.py
@@ -10,6 +10,7 @@
 GRID = 64
 LOG2E = 1.4426950408889634
 IN_VMEM = pl.BlockSpec(memory_space=pltpu.VMEM)
+IN_HBM = pl.BlockSpec(memory_space=pltpu.HBM)
 NT = (((1,), (1,)), ((), ()))
 
 
@@ -32,16 +33,45 @@
     return bases
 
 
-def pick_kernel(aways, frame_ref, pos_ref, *refs):
+def begin_kernel(tile_hbm, frame_hbm, pos_hbm, tile_out, want_ref, frame_ref, pos_ref, sems):
+    pairs = [(frame_hbm, frame_ref), (pos_hbm, pos_ref), (tile_hbm, tile_out)]
+    copies = [
+        pltpu.make_async_copy(source, target, sems.at[n]) for n, (source, target) in enumerate(pairs)
+    ]
+    for copy in copies:
+        copy.start()
+    copies[0].wait()
+    copies[1].wait()
+    want = jnp.where(frame_ref[...] == lax.axis_index("tm"), pos_ref[...], -1)
+    for first in range(0, want.shape[1], 128):
+        row = jnp.broadcast_to(want[:, first : first + 128], (128, 128))
+        want_ref[first : first + 128] = jnp.transpose(row)
+    copies[2].wait()
+
+
+def begin(tile, query_frame, query_pos):
+    points = query_pos.shape[1]
+    return pl.pallas_call(
+        begin_kernel,
+        out_shape=[
+            jax.ShapeDtypeStruct(tile.shape, tile.dtype),
+            jax.ShapeDtypeStruct((points, 128), jnp.int32),
+        ],
+        in_specs=[IN_HBM] * 3,
+        out_specs=[IN_VMEM] * 2,
+        scratch_shapes=[pltpu.VMEM((1, points), jnp.int32)] * 2 + [pltpu.SemaphoreType.DMA((3,))],
+        compiler_params=params(60),
+        cost_estimate=cost(points * 128, 4 * points * 128),
+        name="begin",
+    )(tile, query_frame, query_pos)
+
+
+def pick_kernel(aways, given, sent, want_ref, *refs):
     count = 2 * len(aways)
-    tiles, before, out = refs[:count], refs[count:-1], refs[-1]
-    points = pos_ref.shape[1]
-    want = jnp.where(frame_ref[...] == lax.axis_index("tm"), pos_ref[...], -1)
-    spread = []
-    for first in range(0, points, 128):
-        row = jnp.broadcast_to(want[:, first : first + 128], (128, 128))
-        spread.append(jnp.transpose(row))
-    want = jnp.concatenate(spread, axis=0)
+    tiles, refs = refs[:count], refs[count:]
+    before, refs = refs[:given], refs[given:]
+    sources, out, targets = refs[:sent], refs[-1 - sent], refs[len(refs) - sent :]
+    want = want_ref[...]
     lane = lax.broadcasted_iota(jnp.int32, (1, 128), 1)
     total = None
     for tile, base in zip(tiles, tile_bases(aways, tiles[0].shape[0])):
@@ -57,20 +87,29 @@
     for other in before:
         total = total + other[...].astype(jnp.float32)
     out[...] = total.astype(jnp.bfloat16)
-
-
-def pick(query_frame, query_pos, aways, tiles, before=()):
-    points, width = query_pos.shape[1], tiles[0].shape[1]
+    for source, target in zip(sources, targets):
+        target[...] = source[...]
+
+
+def pick(want, aways, tiles, before=(), sent=(), after=()):
+    points, width = want.shape[0], tiles[0].shape[1]
     count = len(tiles)
-    return pl.pallas_call(
-        functools.partial(pick_kernel, aways),
-        out_shape=jax.ShapeDtypeStruct((points, width), jnp.bfloat16),
-        in_specs=[IN_VMEM] * (2 + count + len(before)),
-        out_specs=IN_VMEM,
+
+    def kernel(*refs):
+        ahead = 1 + count + len(before) + len(sent)
+        pick_kernel(aways, len(before), len(sent), *refs[:ahead], *refs[ahead + len(after) :])
+
+    return pl.pallas_call(
+        kernel,
+        out_shape=[jax.ShapeDtypeStruct((points, width), jnp.bfloat16)]
+        + [jax.ShapeDtypeStruct(piece.shape, piece.dtype) for piece in sent],
+        in_specs=[IN_VMEM] * (1 + count + len(before) + len(sent))
+        + [pl.BlockSpec(memory_space=pl.ANY)] * len(after),
+        out_specs=[IN_VMEM] * (1 + len(sent)),
         compiler_params=params(12),
         cost_estimate=cost(points * count * tiles[0].size, 2 * count * tiles[0].size),
         name="pick",
-    )(query_frame, query_pos, *tiles, *before)
+    )(want, *tiles, *before, *sent, *after)
 
 
 def join_kernel(parts_ref, query_ref, copies_ref):
@@ -219,10 +258,21 @@
     )(refined, *tiles)
 
 
-def prep_kernel(mix_ref, down_ref, to_query_ref, mixes_ref, folded_ref):
+def prep_kernel(mix_hbm, down_hbm, tq_hbm, mixes_ref, folded_ref, token_ref, mix_ref, down_ref, tq_ref, sems):
     frames = mix_ref.shape[0]
     side = mixes_ref.shape[1]
     repeat = side // frames
+    rows = down_ref.shape[0] // 8
+    pieces = [pl.ds(at * rows, rows) for at in range(8)]
+    copies = [
+        pltpu.make_async_copy(mix_hbm, mix_ref, sems.at[0]),
+        pltpu.make_async_copy(tq_hbm, tq_ref, sems.at[1]),
+    ] + [
+        pltpu.make_async_copy(down_hbm.at[piece], down_ref.at[piece], sems.at[2 + n])
+        for n, piece in enumerate(pieces)
+    ]
+    for copy in copies:
+        copy.start()
 
     def iota(shape, axis):
         return lax.broadcasted_iota(jnp.int32, shape, axis)
@@ -230,16 +280,22 @@
     spread = iota((side, frames), 0) // repeat == iota((side, frames), 1)
     spread = spread.astype(jnp.float32).astype(jnp.bfloat16)
     same = iota((side, side), 0) % repeat == iota((side, side), 1) % repeat
+    copies[0].wait()
     rest = mix_ref[...]
     for part in range(mixes_ref.shape[0]):
         now = rest.astype(jnp.bfloat16)
         rest = rest - now.astype(jnp.float32)
-        rows = jnp.dot(spread, now, preferred_element_type=jnp.float32).astype(jnp.bfloat16)
-        full = lax.dot_general(rows, spread, NT, preferred_element_type=jnp.float32)
+        rows_of = jnp.dot(spread, now, preferred_element_type=jnp.float32).astype(jnp.bfloat16)
+        full = lax.dot_general(rows_of, spread, NT, preferred_element_type=jnp.float32)
         mixes_ref[part] = jnp.where(same, full, 0.0).astype(jnp.bfloat16)
-    folded_ref[...] = jnp.dot(
-        down_ref[...], to_query_ref[...], preferred_element_type=jnp.float32
-    ).astype(jnp.bfloat16)
+    token_ref[...] = jnp.zeros_like(token_ref)
+    copies[1].wait()
+    for n in range(8):
+        copies[2 + n].wait()
+        here = slice(n * rows, (n + 1) * rows)
+        folded_ref[here] = jnp.dot(
+            down_ref[here], tq_ref[...], preferred_element_type=jnp.float32
+        ).astype(jnp.bfloat16)
 
 
 def prep(time_mix, w_down, w_query, side=256, parts=2):
@@ -249,10 +305,17 @@
         out_shape=[
             jax.ShapeDtypeStruct((parts, side, side), jnp.bfloat16),
             jax.ShapeDtypeStruct((hidden, w_query.shape[1]), jnp.bfloat16),
+            jax.ShapeDtypeStruct((8, 128), jnp.float32),
         ],
-        in_specs=[IN_VMEM] * 3,
-        out_specs=[IN_VMEM] * 2,
-        compiler_params=params(10),
+        in_specs=[IN_HBM] * 3,
+        out_specs=[IN_VMEM] * 3,
+        scratch_shapes=[
+            pltpu.VMEM(time_mix.shape, time_mix.dtype),
+            pltpu.VMEM(w_down.shape, w_down.dtype),
+            pltpu.VMEM(w_query.shape, w_query.dtype),
+            pltpu.SemaphoreType.DMA((10,)),
+        ],
+        compiler_params=params(56),
         cost_estimate=cost(w_down.size * w_query.shape[1], 2 * w_down.size),
         name="prep",
     )(time_mix, w_down, w_query)
@@ -319,39 +382,41 @@
 
 
 def shards(feats, query_frame, query_pos, time_mix, w_up, w_down, w_query):
-    tile = feats[0]
     points = query_frame.shape[0]
-    width = tile.shape[1]
     groups = lax.axis_size("tm")
     share = points // groups
     chips = lax.axis_size("pts") // 2
-    query_frame = query_frame.reshape(1, points)
-    query_pos = query_pos.reshape(1, points)
+    width = feats.shape[2]
+    tile, want = begin(feats[0], query_frame.reshape(1, points), query_pos.reshape(1, points))
+    mixes, folded, token = prep(time_mix, w_down, w_query)
     swap = swap_pairs(chips)
-    tiles = []
-    aways = []
-
-    def add(piece, away):
-        tiles.extend([piece, lax.ppermute(piece, "pts", swap)])
-        aways.append(away)
-
-    add(tile, 0)
-    below = above = tile
-    own = ()
+    up, down = ring_pairs(chips, 1), ring_pairs(chips, -1)
+    half = chips // 2
+    tiles = [tile, lax.ppermute(tile, "pts", swap)]
+    aways = [0]
+    own = []
     done = 0
-    for step in range(1, chips // 2 + 1):
-        below = lax.ppermute(below, "pts", ring_pairs(chips, 1))
-        if step < chips // 2:
-            above = lax.ppermute(above, "pts", ring_pairs(chips, -1))
-            add(above, step)
-        add(below, -step)
-        if step != 1:
-            own = (pick(query_frame, query_pos, aways[done:], tiles[2 * done :], own),)
+    below, above = lax.ppermute(tile, "pts", up), lax.ppermute(tile, "pts", down)
+    for step in range(1, half + 1):
+        sent = [above, below] if step < half else [below]
+        if step < half:
+            below = lax.ppermute(below, "pts", up)
+            above = lax.ppermute(above, "pts", down) if step + 1 < half else None
+        if step > 1 and step < half:
+            after = (token,) if step == 2 else ()
+            picked, *sent = pick(want, aways[done:], tiles[2 * done :], own, sent, after)
+            own = [picked]
             done = len(aways)
+        elif step == half:
+            own = pick(want, aways[done:], tiles[2 * done :], own)
+            done = len(aways)
+        for piece in sent:
+            tiles += [piece, lax.ppermute(piece, "pts", swap)]
+        aways += [step, -step] if step < half else [-step]
+    own = pick(want, aways[done:], tiles[2 * done :], own)
     parts = lax.all_to_all(own[0].reshape(groups, share, width), "tm", 0, 0, tiled=True)
     query_here, copies = join(parts)
     query = lax.all_to_all(copies, "tm", 0, 0, tiled=True).reshape(points, width)
-    mixes, folded = prep(time_mix, w_down, w_query)
     matched = match(query, tiles).reshape(groups, share, width)
     matched = lax.all_to_all(matched, "tm", 0, 0, tiled=True)
     refined = mixer(matched, query_here, mixes, w_up, folded, w_query)

time: 118 us -> 113 us (0.958)
  blocking collectives: 45.6 us -> 58.2 us
  waiting for transfers between devices: 20.9 us -> 10.7 us
  local copies, waits for them, and re-layouts: 7.02 us -> 0.71 us
  starting transfers between devices: 18.9 us -> 14 us
  Pallas kernels: 24.1 us -> 28.5 us
    all_to_all x0 -> x1, blocking collectives: none -> 13.3 us  [shards(): matched = lax.all_to_all(matched, 'tm', 0, 0, tiled=True)]
    all_to_all x1 -> x0, waiting for transfers between devices: 6.89 us -> none  [shards(): matched = lax.all_to_all(matched, 'tm', 0, 0, tiled=True)]
    unnamed x76 -> x14, local copies, waits for them, and re-layouts: 7.02 us -> 0.71 us
    all_to_all x1 -> x0, starting transfers between devices: 4.82 us -> none  [shards(): matched = lax.all_to_all(matched, 'tm', 0, 0, tiled=True)]
    pallas_call x1, Pallas kernels: 0.9 us -> 4.43 us  [prep(): pl.pallas_call(prep_kernel, out_shape=[jax.ShapeDtypeStruct((parts, side,...]
    ppermute x15, waiting for transfers between devices: 14 us -> 10.7 us  [the longest x3 4.76 us: shards(): below = lax.ppermute(below, 'pts', up)]
    pallas_call x3 -> x5, Pallas kernels: 2.83 us -> 4.69 us  [the longest x4 2.84 us: pick(): pl.pallas_call(kernel, out_shape=[jax.ShapeDtypeStruct((points, width), j...]
  transfers between devices with their start and end apart: 16 -> 15, of which waited for: 5 -> 5; matrix products, arithmetic and copies ran while one was open for 0% -> 0% of each run, Pallas kernels for 3% -> 6%
where the time goes in v1:
time: 113 us
  blocking collectives  58.2 us (52%)
  Pallas kernels  28.5 us (25%)
  starting transfers between devices  14 us (12%)
  waiting for transfers between devices  10.7 us (9%)
    all_to_all x1, blocking collectives, shards(): lax.all_to_all(own[0].reshape(groups, share, width), 'tm', 0, 0, tiled=True)  17.6 us
    all_to_all x1, blocking collectives, shards(): lax.all_to_all(copies, 'tm', 0, 0, tiled=True).reshape(points, width)  13.9 us
    all_to_all x1, blocking collectives, shards(): lax.all_to_all(refined, 'tm', 0, 0, tiled=True).reshape(points, width)  13.3 us
    all_to_all x1, blocking collectives, shards(): matched = lax.all_to_all(matched, 'tm', 0, 0, tiled=True)  13.3 us
    pallas_call x1, Pallas kernels, match(): pl.pallas_call(functools.partial(match_kernel, count, block, LOG2E * widt...  7.05 us
    ppermute x2, starting transfers between devices, shards(): above = lax.ppermute(above, 'pts', down) if step + 1 < half else None  6.3 us
    pallas_call x1, Pallas kernels, mixer(): pl.pallas_call(functools.partial(mixer_kernel, step), out_shape=jax.Shape...  6.22 us
    pallas_call x1, Pallas kernels, rematch(): pl.pallas_call(functools.partial(rematch_kernel, aways, block, LOG2E * wi...  6.07 us
  transfers between devices with their start and end apart: 15, of which 5 were waited for; matrix products, arithmetic and copies ran while one was open for 0% of the time, Pallas kernels for 6%

profile of v1, /device:TPU:8, one launch (start us, length us, event | category | flops | bytes accessed | tf_op | source)
XLA Modules:
  0.0 112.9 jit_solution(14955288095222432405)
XLA Ops:
  0.6 1.8 %begin.1 = (bf16[256,256]{1,0:T(8,128)(2,1)}, s32[1024,128]{1,0:T(8,128)}) custom-call(bf16[256,256]{1,0:T(8,128)(2,1)} %bitcast.11, s32[1,1024]{1,0:T(1,128)} %bitcast.12, s32[1,1024]{1,0:T(1,128)} %bitcast.13), custom_call_target="tpu_custom_call" | custom-call | flops 262144 | bytes 524288 | tf_op jit(solution)/shard_map/begin/pallas_call | solution.py:54
  2.5 2.0 %collective-permute-start = (bf16[256,256]{1,0:T(8,128)(2,1)}, bf16[256,256]{1,0:T(8,128)(2,1)S(1)}, u32[]{:S(2)}, u32[]{:S(2)}) collective-permute-start(bf16[256,256]{1,0:T(8,128)(2,1)} %get-tuple-element.16.refs_1_.refs_0_), channel_id=1, source_target_pairs={{0,2},{1,3},{2,4},{3,5},{4,6},{5,7},{6,8},{7,9},{8,10},{9,11},{10,... | collective-permute-start | bytes 393224 | tf_op jit(solution)/shard_map/ppermute | solution.py:399
  4.5 4.0 %collective-permute-start.6 = (bf16[256,256]{1,0:T(8,128)(2,1)}, bf16[256,256]{1,0:T(8,128)(2,1)S(1)}, u32[]{:S(2)}, u32[]{:S(2)}) collective-permute-start(bf16[256,256]{1,0:T(8,128)(2,1)} %get-tuple-element.16.refs_1_.refs_0_), channel_id=1, source_target_pairs={{0,14},{1,15},{2,0},{3,1},{4,2},{5,3},{6,4},{7,5},{8,6},{9,7},{10,... | collective-permute-start | bytes 393224 | tf_op jit(solution)/shard_map/ppermute | solution.py:399
  8.5 3.6 %collective-permute-done.refs_5_.refs_4_ = bf16[256,256]{1,0:T(8,128)(2,1)S(1)} collective-permute-done((bf16[256,256]{1,0:T(8,128)(2,1)}, bf16[256,256]{1,0:T(8,128)(2,1)S(1)}, u32[]{:S(2)}, u32[]{:S(2)}) %collective-permute-start) | collective-permute-done | bytes 131104 | tf_op jit(solution)/shard_map/ppermute | solution.py:399
  12.2 3.2 %collective-permute-start.9 = (bf16[256,256]{1,0:T(8,128)(2,1)S(1)}, bf16[256,256]{1,0:T(8,128)(2,1)S(1)}, u32[]{:S(2)}, u32[]{:S(2)}) collective-permute-start(bf16[256,256]{1,0:T(8,128)(2,1)S(1)} %collective-permute-done.6.refs_3_.refs_2_), channel_id=1, source_target_pairs={{0,14},{1,15},{2,0},{3,1},{4,2},{5,3},{6,4},{7,5},{8,6},{9,7},{10,... | collective-permute-start | bytes 393224 | tf_op jit(solution)/shard_map/ppermute | solution.py:404
  15.9 4.4 %prep.1 = (bf16[2,256,256]{2,1,0:T(8,128)(2,1)}, bf16[2048,256]{1,0:T(8,128)(2,1)}, f32[8,128]{1,0:T(8,128)}) custom-call(f32[16,16]{1,0:T(8,128)} %mix_hbm.1, bf16[2048,512]{1,0:T(8,128)(2,1)} %down_hbm.1, bf16[512,256]{1,0:T(8,128)(2,1)} %tq_ref.1), custom_call_target="tpu_custom_call" | custom-call | flops 536870912 | bytes 2097152 | tf_op jit(solution)/shard_map/prep/pallas_call | solution.py:303
  20.5 0.7 copy-done.6
  21.2 1.0 pick.4
  22.5 3.1 %collective-permute-start.12 = (bf16[256,256]{1,0:T(8,128)(2,1)S(1)}, bf16[256,256]{1,0:T(8,128)(2,1)S(1)}, u32[]{:S(2)}, u32[]{:S(2)}) collective-permute-start(bf16[256,256]{1,0:T(8,128)(2,1)S(1)} %collective-permute-done.9.refs_7_), channel_id=1, source_target_pairs={{0,14},{1,15},{2,0},{3,1},{4,2},{5,3},{6,4},{7,5},{8,6},{9,7},{10,... | collective-permute-start | bytes 393224 | tf_op jit(solution)/shard_map/ppermute | solution.py:404
  25.7 1.6 %collective-permute-done.2.refs_7_ = bf16[256,256]{1,0:T(8,128)(2,1)S(1)} collective-permute-done((bf16[256,256]{1,0:T(8,128)(2,1)S(1)}, bf16[256,256]{1,0:T(8,128)(2,1)S(1)}, u32[]{:S(2)}, u32[]{:S(2)}) %collective-permute-start.2) | collective-permute-done | bytes 131104 | tf_op jit(solution)/shard_map/ppermute | solution.py:403
  27.3 1.6 %collective-permute-done.12.refs_6_ = bf16[256,256]{1,0:T(8,128)(2,1)S(1)} collective-permute-done((bf16[256,256]{1,0:T(8,128)(2,1)S(1)}, bf16[256,256]{1,0:T(8,128)(2,1)S(1)}, u32[]{:S(2)}, u32[]{:S(2)}) %collective-permute-start.12) | collective-permute-done | bytes 131104 | tf_op jit(solution)/shard_map/ppermute | solution.py:404
  28.9 0.7 pick.5
  29.7 0.5 collective-permute-start.14
  30.2 3.2 %collective-permute-done.3.refs_1_.refs_14_ = bf16[256,256]{1,0:T(8,128)(2,1)S(1)} collective-permute-done((bf16[256,256]{1,0:T(8,128)(2,1)S(1)}, bf16[256,256]{1,0:T(8,128)(2,1)S(1)}, u32[]{:S(2)}, u32[]{:S(2)}) %collective-permute-start.3) | collective-permute-done | bytes 131104 | tf_op jit(solution)/shard_map/ppermute | solution.py:403
  33.5 0.7 pick.6.refs_3_
  34.2 0.6 collective-permute-done.4.refs_2_.refs_15_
  34.8 0.4 pick.7
  35.2 17.6 %all_to_all.20.parts_ref = bf16[16,64,256]{2,1,0:T(8,128)(2,1)S(1)} all-to-all(bf16[16,64,256]{2,1,0:T(8,128)(2,1)S(1)} %bitcast.7), channel_id=1, replica_groups=mesh['tm'=16,'pts'=16] {'tm'}, dimensions={0} | all-to-all | bytes 1048576 | tf_op jit(solution)/shard_map/all_to_all | solution.py:417
  53.0 13.9 %all_to_all.21 = bf16[16,64,256]{2,1,0:T(8,128)(2,1)S(1)} all-to-all(bf16[16,64,256]{2,1,0:T(8,128)(2,1)S(1)} %get-tuple-element.24), channel_id=1, replica_groups=mesh['tm'=16,'pts'=16] {'tm'}, dimensions={0} | all-to-all | bytes 1048576 | tf_op jit(solution)/shard_map/all_to_all | solution.py:419
  66.9 7.0 %match.1 = bf16[1024,256]{1,0:T(8,128)(2,1)S(1)} custom-call(bf16[1024,256]{1,0:T(8,128)(2,1)S(1)} %bitcast.9, bf16[256,256]{1,0:T(8,128)(2,1)S(1)} %copy-done.5, bf16[256,256]{1,0:T(8,128)(2,1)S(1)} %collective-permute-done.5.refs_2_.refs_1_, bf16[256,256]{1,0:T(8,128)(2,1)S(1)} %collective-permute-done.6.refs_3_.refs_2_, ...), custom_call_target="tpu_custom_call" | custom-call | flops 4294967296 | bytes 2097152 | tf_op jit(solution)/shard_map/match/pallas_call | solution.py:178
  73.9 13.3 %all_to_all.22.m_ref = bf16[16,64,256]{2,1,0:T(8,128)(2,1)S(1)} all-to-all(bf16[16,64,256]{2,1,0:T(8,128)(2,1)S(1)} %bitcast.10), channel_id=1, replica_groups=mesh['tm'=16,'pts'=16] {'tm'}, dimensions={0} | all-to-all | bytes 1048576 | tf_op jit(solution)/shard_map/all_to_all | solution.py:421
  87.3 6.2 %mixer.1 = bf16[16,64,256]{2,1,0:T(8,128)(2,1)S(1)} custom-call(bf16[16,64,256]{2,1,0:T(8,128)(2,1)S(1)} %all_to_all.22.m_ref, bf16[64,256]{1,0:T(8,128)(2,1)S(1)} %get-tuple-element.25.q_ref, bf16[2,256,256]{2,1,0:T(8,128)(2,1)S(1)} %copy-done.4, bf16[512,2048]{1,0:T(8,128)(2,1)S(1)} %copy-done.2, bf16[2048,256]{1,0:T(8,128)(2,1)S(1)} %copy-done.3, ...), custom_call_target="tpu_custom_call" | custom-call | flops 3221225472 | bytes 2097152 | tf_op jit(solution)/shard_map/mixer/pallas_call | solution.py:361
  93.5 13.3 %all_to_all.23 = bf16[16,64,256]{2,1,0:T(8,128)(2,1)S(1)} all-to-all(bf16[16,64,256]{2,1,0:T(8,128)(2,1)S(1)} %mixer.1), channel_id=1, replica_groups=mesh['tm'=16,'pts'=16] {'tm'}, dimensions={0} | all-to-all | bytes 1048576 | tf_op jit(solution)/shard_map/all_to_all | solution.py:423
  106.9 6.1 %rematch.1 = (f32[1,1024]{1,0:T(1,128)}, f32[1,1024]{1,0:T(1,128)}) custom-call(bf16[1024,256]{1,0:T(8,128)(2,1)S(1)} %bitcast.8, bf16[256,256]{1,0:T(8,128)(2,1)S(1)} %copy-done.5, bf16[256,256]{1,0:T(8,128)(2,1)S(1)} %collective-permute-done.5.refs_2_.refs_1_, bf16[256,256]{1,0:T(8,128)(2,1)S(1)} %collective-permute-done.6.refs_3_.refs_2_, ...), custom_call_target="tpu_custom_call" | custom-call | flops 2147483648 | bytes 2097152 | tf_op jit(solution)/shard_map/rematch/pallas_call | solution.py:250
  (34 shorter events, 1.3 us)
Async XLA Ops:
  2.5 18.0 %copy-start = (s32[1024,128]{1,0:T(8,128)S(1)}, s32[1024,128]{1,0:T(8,128)}, u32[]{:S(2)}) copy-start(s32[1024,128]{1,0:T(8,128)} %get-tuple-element.15.refs_0_) | copy-start | bytes 1572868
  2.5 18.0 %copy-start.5 = (bf16[256,256]{1,0:T(8,128)(2,1)S(1)}, bf16[256,256]{1,0:T(8,128)(2,1)}, u32[]{:S(2)}) copy-start(bf16[256,256]{1,0:T(8,128)(2,1)} %get-tuple-element.16.refs_1_.refs_0_) | copy-start | bytes 393220
  2.5 9.6 %collective-permute-start = (bf16[256,256]{1,0:T(8,128)(2,1)}, bf16[256,256]{1,0:T(8,128)(2,1)S(1)}, u32[]{:S(2)}, u32[]{:S(2)}) collective-permute-start(bf16[256,256]{1,0:T(8,128)(2,1)} %get-tuple-element.16.refs_1_.refs_0_), channel_id=1, source_target_pairs={{0,2},{1,3},{2,4},{3,5},{4,6},{5,7},{6,8},{7,9},{8,10},{9,11},{10,... | collective-permute-start | bytes 393224 | tf_op jit(solution)/shard_map/ppermute | solution.py:399
  4.5 7.7 %collective-permute-start.6 = (bf16[256,256]{1,0:T(8,128)(2,1)}, bf16[256,256]{1,0:T(8,128)(2,1)S(1)}, u32[]{:S(2)}, u32[]{:S(2)}) collective-permute-start(bf16[256,256]{1,0:T(8,128)(2,1)} %get-tuple-element.16.refs_1_.refs_0_), channel_id=1, source_target_pairs={{0,14},{1,15},{2,0},{3,1},{4,2},{5,3},{6,4},{7,5},{8,6},{9,7},{10,... | collective-permute-start | bytes 393224 | tf_op jit(solution)/shard_map/ppermute | solution.py:399
  12.1 8.2 %collective-permute-start.1 = (bf16[256,256]{1,0:T(8,128)(2,1)S(1)}, bf16[256,256]{1,0:T(8,128)(2,1)S(1)}, u32[]{:S(2)}, u32[]{:S(2)}) collective-permute-start(bf16[256,256]{1,0:T(8,128)(2,1)S(1)} %collective-permute-done.refs_5_.refs_4_), channel_id=1, source_target_pairs={{0,2},{1,3},{2,4},{3,5},{4,6},{5,7},{6,8},{7,9},{8,10},{9,11},{10,... | collective-permute-start | bytes 393224 | tf_op jit(solution)/shard_map/ppermute | solution.py:403
  12.2 8.3 %collective-permute-start.5 = (bf16[256,256]{1,0:T(8,128)(2,1)}, bf16[256,256]{1,0:T(8,128)(2,1)S(1)}, u32[]{:S(2)}, u32[]{:S(2)}) collective-permute-start(bf16[256,256]{1,0:T(8,128)(2,1)} %get-tuple-element.16.refs_1_.refs_0_), channel_id=1, source_target_pairs={{0,1},{1,0},{2,3},{3,2},{4,5},{5,4},{6,7},{7,6},{8,9},{9,8},{10,11... | collective-permute-start | bytes 393224 | tf_op jit(solution)/shard_map/ppermute | solution.py:395
  12.2 8.3 %collective-permute-start.9 = (bf16[256,256]{1,0:T(8,128)(2,1)S(1)}, bf16[256,256]{1,0:T(8,128)(2,1)S(1)}, u32[]{:S(2)}, u32[]{:S(2)}) collective-permute-start(bf16[256,256]{1,0:T(8,128)(2,1)S(1)} %collective-permute-done.6.refs_3_.refs_2_), channel_id=1, source_target_pairs={{0,14},{1,15},{2,0},{3,1},{4,2},{5,3},{6,4},{7,5},{8,6},{9,7},{10,... | collective-permute-start | bytes 393224 | tf_op jit(solution)/shard_map/ppermute | solution.py:404
  15.4 5.1 %collective-permute-start.7 = (bf16[256,256]{1,0:T(8,128)(2,1)S(1)}, bf16[256,256]{1,0:T(8,128)(2,1)S(1)}, u32[]{:S(2)}, u32[]{:S(2)}) collective-permute-start(bf16[256,256]{1,0:T(8,128)(2,1)S(1)} %collective-permute-done.6.refs_3_.refs_2_), channel_id=1, source_target_pairs={{0,1},{1,0},{2,3},{3,2},{4,5},{5,4},{6,7},{7,6},{8,9},{9,8},{10,11... | collective-permute-start | bytes 393224 | tf_op jit(solution)/shard_map/ppermute | solution.py:414
  15.6 4.9 %collective-permute-start.8 = (bf16[256,256]{1,0:T(8,128)(2,1)S(1)}, bf16[256,256]{1,0:T(8,128)(2,1)S(1)}, u32[]{:S(2)}, u32[]{:S(2)}) collective-permute-start(bf16[256,256]{1,0:T(8,128)(2,1)S(1)} %collective-permute-done.refs_5_.refs_4_), channel_id=1, source_target_pairs={{0,1},{1,0},{2,3},{3,2},{4,5},{5,4},{6,7},{7,6},{8,9},{9,8},{10,11... | collective-permute-start | bytes 393224 | tf_op jit(solution)/shard_map/ppermute | solution.py:414
  20.4 6.9 %collective-permute-start.2 = (bf16[256,256]{1,0:T(8,128)(2,1)S(1)}, bf16[256,256]{1,0:T(8,128)(2,1)S(1)}, u32[]{:S(2)}, u32[]{:S(2)}) collective-permute-start(bf16[256,256]{1,0:T(8,128)(2,1)S(1)} %collective-permute-done.1.refs_8_), channel_id=1, source_target_pairs={{0,2},{1,3},{2,4},{3,5},{4,6},{5,7},{6,8},{7,9},{8,10},{9,11},{10,... | collective-permute-start | bytes 393224 | tf_op jit(solution)/shard_map/ppermute | solution.py:403
  20.5 0.7 copy-start.6
  22.2 6.7 %collective-permute-start.10 = (bf16[256,256]{1,0:T(8,128)(2,1)S(1)}, bf16[256,256]{1,0:T(8,128)(2,1)S(1)}, u32[]{:S(2)}, u32[]{:S(2)}) collective-permute-start(bf16[256,256]{1,0:T(8,128)(2,1)S(1)} %get-tuple-element.18.refs_1_.refs_6_), channel_id=1, source_target_pairs={{0,1},{1,0},{2,3},{3,2},{4,5},{5,4},{6,7},{7,6},{8,9},{9,8},{10,11... | collective-permute-start | bytes 393224 | tf_op jit(solution)/shard_map/ppermute | solution.py:414
  22.5 6.4 %collective-permute-start.12 = (bf16[256,256]{1,0:T(8,128)(2,1)S(1)}, bf16[256,256]{1,0:T(8,128)(2,1)S(1)}, u32[]{:S(2)}, u32[]{:S(2)}) collective-permute-start(bf16[256,256]{1,0:T(8,128)(2,1)S(1)} %collective-permute-done.9.refs_7_), channel_id=1, source_target_pairs={{0,14},{1,15},{2,0},{3,1},{4,2},{5,3},{6,4},{7,5},{8,6},{9,7},{10,... | collective-permute-start | bytes 393224 | tf_op jit(solution)/shard_map/ppermute | solution.py:404
  25.6 3.4 %collective-permute-start.11 = (bf16[256,256]{1,0:T(8,128)(2,1)S(1)}, bf16[256,256]{1,0:T(8,128)(2,1)S(1)}, u32[]{:S(2)}, u32[]{:S(2)}) collective-permute-start(bf16[256,256]{1,0:T(8,128)(2,1)S(1)} %get-tuple-element.19.refs_3_.refs_8_), channel_id=1, source_target_pairs={{0,1},{1,0},{2,3},{3,2},{4,5},{5,4},{6,7},{7,6},{8,9},{9,8},{10,11... | collective-permute-start | bytes 393224 | tf_op jit(solution)/shard_map/ppermute | solution.py:414
  27.3 6.2 %collective-permute-start.3 = (bf16[256,256]{1,0:T(8,128)(2,1)S(1)}, bf16[256,256]{1,0:T(8,128)(2,1)S(1)}, u32[]{:S(2)}, u32[]{:S(2)}) collective-permute-start(bf16[256,256]{1,0:T(8,128)(2,1)S(1)} %collective-permute-done.2.refs_7_), channel_id=1, source_target_pairs={{0,2},{1,3},{2,4},{3,5},{4,6},{5,7},{6,8},{7,9},{8,10},{9,11},{10,... | collective-permute-start | bytes 393224 | tf_op jit(solution)/shard_map/ppermute | solution.py:403
  29.6 3.8 %collective-permute-start.13 = (bf16[256,256]{1,0:T(8,128)(2,1)S(1)}, bf16[256,256]{1,0:T(8,128)(2,1)S(1)}, u32[]{:S(2)}, u32[]{:S(2)}) collective-permute-start(bf16[256,256]{1,0:T(8,128)(2,1)S(1)} %get-tuple-element.21.refs_1_.refs_10_), channel_id=1, source_target_pairs={{0,1},{1,0},{2,3},{3,2},{4,5},{5,4},{6,7},{7,6},{8,9},{9,8},{10,11... | collective-permute-start | bytes 393224 | tf_op jit(solution)/shard_map/ppermute | solution.py:414
  29.7 3.7 %collective-permute-start.14 = (bf16[256,256]{1,0:T(8,128)(2,1)S(1)}, bf16[256,256]{1,0:T(8,128)(2,1)S(1)}, u32[]{:S(2)}, u32[]{:S(2)}) collective-permute-start(bf16[256,256]{1,0:T(8,128)(2,1)S(1)} %get-tuple-element.22.refs_3_.refs_12_), channel_id=1, source_target_pairs={{0,1},{1,0},{2,3},{3,2},{4,5},{5,4},{6,7},{7,6},{8,9},{9,8},{10,11... | collective-permute-start | bytes 393224 | tf_op jit(solution)/shard_map/ppermute | solution.py:414
  33.5 1.3 %collective-permute-start.4 = (bf16[256,256]{1,0:T(8,128)(2,1)S(1)}, bf16[256,256]{1,0:T(8,128)(2,1)S(1)}, u32[]{:S(2)}, u32[]{:S(2)}) collective-permute-start(bf16[256,256]{1,0:T(8,128)(2,1)S(1)} %collective-permute-done.3.refs_1_.refs_14_), channel_id=1, source_target_pairs={{0,1},{1,0},{2,3},{3,2},{4,5},{5,4},{6,7},{7,6},{8,9},{9,8},{10,11... | collective-permute-start | bytes 393224 | tf_op jit(solution)/shard_map/ppermute | solution.py:414
  66.9 20.4 %copy-start.1 = (bf16[512,256]{1,0:T(8,128)(2,1)S(1)}, bf16[512,256]{1,0:T(8,128)(2,1)}, u32[]{:S(2)}) copy-start(bf16[512,256]{1,0:T(8,128)(2,1)} %tq_ref.1) | copy-start | bytes 786436
  66.9 20.4 %copy-start.2 = (bf16[512,2048]{1,0:T(8,128)(2,1)S(1)}, bf16[512,2048]{1,0:T(8,128)(2,1)}, u32[]{:S(2)}) copy-start(bf16[512,2048]{1,0:T(8,128)(2,1)} %up_ref.1) | copy-start | bytes 6291460
  66.9 20.4 %copy-start.3 = (bf16[2048,256]{1,0:T(8,128)(2,1)S(1)}, bf16[2048,256]{1,0:T(8,128)(2,1)}, u32[]{:S(2)}) copy-start(bf16[2048,256]{1,0:T(8,128)(2,1)} %get-tuple-element.27.folded_ref) | copy-start | bytes 3145732
  66.9 20.4 %copy-start.4 = (bf16[2,256,256]{2,1,0:T(8,128)(2,1)S(1)}, bf16[2,256,256]{2,1,0:T(8,128)(2,1)}, u32[]{:S(2)}) copy-start(bf16[2,256,256]{2,1,0:T(8,128)(2,1)} %get-tuple-element.26.mixes_ref) | copy-start | bytes 786436

commit v2 on v1

--- a/solution.py
+++ b/solution.py
@@ -10,6 +10,7 @@
 GRID = 64
 LOG2E = 1.4426950408889634
 IN_VMEM = pl.BlockSpec(memory_space=pltpu.VMEM)
+IN_SMEM = pl.BlockSpec(memory_space=pltpu.SMEM)
 IN_HBM = pl.BlockSpec(memory_space=pltpu.HBM)
 NT = (((1,), (1,)), ((), ()))
 
@@ -104,7 +105,7 @@
         out_shape=[jax.ShapeDtypeStruct((points, width), jnp.bfloat16)]
         + [jax.ShapeDtypeStruct(piece.shape, piece.dtype) for piece in sent],
         in_specs=[IN_VMEM] * (1 + count + len(before) + len(sent))
-        + [pl.BlockSpec(memory_space=pl.ANY)] * len(after),
+        + [IN_SMEM] * len(after),
         out_specs=[IN_VMEM] * (1 + len(sent)),
         compiler_params=params(12),
         cost_estimate=cost(points * count * tiles[0].size, 2 * count * tiles[0].size),
@@ -258,20 +259,26 @@
     )(refined, *tiles)
 
 
-def prep_kernel(mix_hbm, down_hbm, tq_hbm, mixes_ref, folded_ref, token_ref, mix_ref, down_ref, tq_ref, sems):
+def prep_kernel(mix_hbm, down_hbm, tq_hbm, mixes_hbm, folded_hbm, token_ref, *scratch):
+    mixes_ref, folded_ref, mix_ref, down_ref, tq_ref, sems_in, sems_out = scratch
     frames = mix_ref.shape[0]
     side = mixes_ref.shape[1]
     repeat = side // frames
-    rows = down_ref.shape[0] // 8
-    pieces = [pl.ds(at * rows, rows) for at in range(8)]
-    copies = [
-        pltpu.make_async_copy(mix_hbm, mix_ref, sems.at[0]),
-        pltpu.make_async_copy(tq_hbm, tq_ref, sems.at[1]),
+    count = sems_in.shape[0] - 2
+    rows = down_ref.shape[0] // count
+    pieces = [pl.ds(at * rows, rows) for at in range(count)]
+    loads = [
+        pltpu.make_async_copy(mix_hbm, mix_ref, sems_in.at[0]),
+        pltpu.make_async_copy(tq_hbm, tq_ref, sems_in.at[1]),
     ] + [
-        pltpu.make_async_copy(down_hbm.at[piece], down_ref.at[piece], sems.at[2 + n])
+        pltpu.make_async_copy(down_hbm.at[piece], down_ref.at[piece], sems_in.at[2 + n])
         for n, piece in enumerate(pieces)
     ]
-    for copy in copies:
+    saves = [
+        pltpu.make_async_copy(folded_ref.at[piece], folded_hbm.at[piece], sems_out.at[n])
+        for n, piece in enumerate(pieces)
+    ] + [pltpu.make_async_copy(mixes_ref, mixes_hbm, sems_out.at[count])]
+    for copy in loads:
         copy.start()
 
     def iota(shape, axis):
@@ -280,7 +287,7 @@
     spread = iota((side, frames), 0) // repeat == iota((side, frames), 1)
     spread = spread.astype(jnp.float32).astype(jnp.bfloat16)
     same = iota((side, side), 0) % repeat == iota((side, side), 1) % repeat
-    copies[0].wait()
+    loads[0].wait()
     rest = mix_ref[...]
     for part in range(mixes_ref.shape[0]):
         now = rest.astype(jnp.bfloat16)
@@ -288,33 +295,31 @@
         rows_of = jnp.dot(spread, now, preferred_element_type=jnp.float32).astype(jnp.bfloat16)
         full = lax.dot_general(rows_of, spread, NT, preferred_element_type=jnp.float32)
         mixes_ref[part] = jnp.where(same, full, 0.0).astype(jnp.bfloat16)
-    token_ref[...] = jnp.zeros_like(token_ref)
-    copies[1].wait()
-    for n in range(8):
-        copies[2 + n].wait()
+    saves[count].start()
+    loads[1].wait()
+    for n in range(count):
+        loads[2 + n].wait()
         here = slice(n * rows, (n + 1) * rows)
         folded_ref[here] = jnp.dot(
             down_ref[here], tq_ref[...], preferred_element_type=jnp.float32
         ).astype(jnp.bfloat16)
-
-
-def prep(time_mix, w_down, w_query, side=256, parts=2):
-    hidden, width = w_down.shape
+        saves[n].start()
+    token_ref[0, 0] = 0
+    for copy in saves:
+        copy.wait()
+
+
+def prep(time_mix, w_down, w_query, side=256, parts=2, count=8):
+    mixes = jax.ShapeDtypeStruct((parts, side, side), jnp.bfloat16)
+    folded = jax.ShapeDtypeStruct((w_down.shape[0], w_query.shape[1]), jnp.bfloat16)
+    held = (mixes, folded, time_mix, w_down, w_query)
     return pl.pallas_call(
         prep_kernel,
-        out_shape=[
-            jax.ShapeDtypeStruct((parts, side, side), jnp.bfloat16),
-            jax.ShapeDtypeStruct((hidden, w_query.shape[1]), jnp.bfloat16),
-            jax.ShapeDtypeStruct((8, 128), jnp.float32),
-        ],
+        out_shape=[mixes, folded, jax.ShapeDtypeStruct((1, 1), jnp.int32)],
         in_specs=[IN_HBM] * 3,
-        out_specs=[IN_VMEM] * 3,
-        scratch_shapes=[
-            pltpu.VMEM(time_mix.shape, time_mix.dtype),
-            pltpu.VMEM(w_down.shape, w_down.dtype),
-            pltpu.VMEM(w_query.shape, w_query.dtype),
-            pltpu.SemaphoreType.DMA((10,)),
-        ],
+        out_specs=[IN_HBM] * 2 + [IN_SMEM],
+        scratch_shapes=[pltpu.VMEM(array.shape, array.dtype) for array in held]
+        + [pltpu.SemaphoreType.DMA((count + 2,)), pltpu.SemaphoreType.DMA((count + 1,))],
         compiler_params=params(56),
         cost_estimate=cost(w_down.size * w_query.shape[1], 2 * w_down.size),
         name="prep",
@@ -396,7 +401,7 @@
     aways = [0]
     own = []
     done = 0
-    below, above = lax.ppermute(tile, "pts", up), lax.ppermute(tile, "pts", down)
+    below, above = lax.ppermute(feats[0], "pts", up), lax.ppermute(feats[0], "pts", down)
     for step in range(1, half + 1):
         sent = [above, below] if step < half else [below]
         if step < half:

time: 113 us -> 112 us (level)
  waiting for transfers between devices: 10.7 us -> 8.85 us
    ppermute x2, waiting for transfers between devices: 3.62 us -> 1.76 us  [the longest x1 1.76 us: shards(): lax.ppermute(feats[0], 'pts', up)]
  transfers between devices with their start and end apart: 15 -> 15, of which waited for: 5 -> 5; matrix products, arithmetic and copies ran while one was open for 0% -> 0% of each run, Pallas kernels for 6% -> 9%
where the time goes in v2:
time: 112 us; the launch traced here: 111 us
  blocking collectives  58.2 us (52%)
  Pallas kernels  29.4 us (26%)
  starting transfers between devices  14 us (12%)
  waiting for transfers between devices  8.85 us (8%)
    all_to_all x1, blocking collectives, shards(): lax.all_to_all(own[0].reshape(groups, share, width), 'tm', 0, 0, tiled=True)  17.6 us
    all_to_all x1, blocking collectives, shards(): lax.all_to_all(copies, 'tm', 0, 0, tiled=True).reshape(points, width)  13.9 us
    all_to_all x1, blocking collectives, shards(): lax.all_to_all(refined, 'tm', 0, 0, tiled=True).reshape(points, width)  13.3 us
    all_to_all x1, blocking collectives, shards(): matched = lax.all_to_all(matched, 'tm', 0, 0, tiled=True)  13.3 us
    pallas_call x1, Pallas kernels, match(): pl.pallas_call(functools.partial(match_kernel, count, block, LOG2E * widt...  7.04 us
    ppermute x2, starting transfers between devices, shards(): above = lax.ppermute(above, 'pts', down) if step + 1 < half else None  6.29 us
    pallas_call x1, Pallas kernels, mixer(): pl.pallas_call(functools.partial(mixer_kernel, step), out_shape=jax.Shape...  6.22 us
    pallas_call x1, Pallas kernels, rematch(): pl.pallas_call(functools.partial(rematch_kernel, aways, block, LOG2E * wi...  6.08 us
  transfers between devices with their start and end apart: 15, of which 5 were waited for; matrix products, arithmetic and copies ran while one was open for 0% of the time, Pallas kernels for 9%

profile of v2, /device:TPU:8, one launch (start us, length us, event | category | flops | bytes accessed | tf_op | source)
XLA Modules:
  0.0 111.3 jit_solution(4516996905800911358)
XLA Ops:
  0.6 2.0 %collective-permute-start = (bf16[256,256]{1,0:T(8,128)(2,1)}, bf16[256,256]{1,0:T(8,128)(2,1)S(1)}, u32[]{:S(2)}, u32[]{:S(2)}) collective-permute-start(bf16[256,256]{1,0:T(8,128)(2,1)} %bitcast.11), channel_id=1, source_target_pairs={{0,2},{1,3},{2,4},{3,5},{4,6},{5,7},{6,8},{7,9},{8,10},{9,11},{10,... | collective-permute-start | bytes 393224 | tf_op jit(solution)/shard_map/ppermute | solution.py:404
  2.6 4.0 %collective-permute-start.6 = (bf16[256,256]{1,0:T(8,128)(2,1)}, bf16[256,256]{1,0:T(8,128)(2,1)S(1)}, u32[]{:S(2)}, u32[]{:S(2)}) collective-permute-start(bf16[256,256]{1,0:T(8,128)(2,1)} %bitcast.12), channel_id=1, source_target_pairs={{0,14},{1,15},{2,0},{3,1},{4,2},{5,3},{6,4},{7,5},{8,6},{9,7},{10,... | collective-permute-start | bytes 393224 | tf_op jit(solution)/shard_map/ppermute | solution.py:404
  6.7 1.8 %begin.1 = (bf16[256,256]{1,0:T(8,128)(2,1)}, s32[1024,128]{1,0:T(8,128)}) custom-call(bf16[256,256]{1,0:T(8,128)(2,1)} %bitcast.13, s32[1,1024]{1,0:T(1,128)} %bitcast.14, s32[1,1024]{1,0:T(1,128)} %bitcast.15), custom_call_target="tpu_custom_call" | custom-call | flops 262144 | bytes 524288 | tf_op jit(solution)/shard_map/begin/pallas_call | solution.py:55
  8.5 1.8 %collective-permute-done.refs_5_.refs_4_ = bf16[256,256]{1,0:T(8,128)(2,1)S(1)} collective-permute-done((bf16[256,256]{1,0:T(8,128)(2,1)}, bf16[256,256]{1,0:T(8,128)(2,1)S(1)}, u32[]{:S(2)}, u32[]{:S(2)}) %collective-permute-start) | collective-permute-done | bytes 131104 | tf_op jit(solution)/shard_map/ppermute | solution.py:404
  10.3 3.2 %collective-permute-start.9 = (bf16[256,256]{1,0:T(8,128)(2,1)S(1)}, bf16[256,256]{1,0:T(8,128)(2,1)S(1)}, u32[]{:S(2)}, u32[]{:S(2)}) collective-permute-start(bf16[256,256]{1,0:T(8,128)(2,1)S(1)} %collective-permute-done.6.refs_3_.refs_2_), channel_id=1, source_target_pairs={{0,14},{1,15},{2,0},{3,1},{4,2},{5,3},{6,4},{7,5},{8,6},{9,7},{10,... | collective-permute-start | bytes 393224 | tf_op jit(solution)/shard_map/ppermute | solution.py:409
  14.0 4.7 %prep.1 = (bf16[2,256,256]{2,1,0:T(8,128)(2,1)}, bf16[2048,256]{1,0:T(8,128)(2,1)}, s32[1,1]{1,0:T(1,128)}) custom-call(f32[16,16]{1,0:T(8,128)} %mix_hbm.1, bf16[2048,512]{1,0:T(8,128)(2,1)} %down_hbm.1, bf16[512,256]{1,0:T(8,128)(2,1)} %tq_ref.1), custom_call_target="tpu_custom_call" | custom-call | flops 536870912 | bytes 2097152 | tf_op jit(solution)/shard_map/prep/pallas_call | solution.py:316
  18.9 1.6 %pick.4 = (bf16[1024,256]{1,0:T(8,128)(2,1)S(1)}, bf16[256,256]{1,0:T(8,128)(2,1)S(1)}, bf16[256,256]{1,0:T(8,128)(2,1)S(1)}) custom-call(s32[1024,128]{1,0:T(8,128)S(1)} %copy-done, bf16[256,256]{1,0:T(8,128)(2,1)S(1)} %copy-done.5, bf16[256,256]{1,0:T(8,128)(2,1)S(1)} %collective-permute-done.5.refs_2_.refs_1_, ...), custom_call_target="tpu_custom_call" | custom-call | flops 805306368 | bytes 786432 | tf_op jit(solution)/shard_map/pick/pallas_call | solution.py:103
  20.5 0.3 collective-permute-start.10
  20.8 3.1 %collective-permute-start.12 = (bf16[256,256]{1,0:T(8,128)(2,1)S(1)}, bf16[256,256]{1,0:T(8,128)(2,1)S(1)}, u32[]{:S(2)}, u32[]{:S(2)}) collective-permute-start(bf16[256,256]{1,0:T(8,128)(2,1)S(1)} %collective-permute-done.9.refs_7_), channel_id=1, source_target_pairs={{0,14},{1,15},{2,0},{3,1},{4,2},{5,3},{6,4},{7,5},{8,6},{9,7},{10,... | collective-permute-start | bytes 393224 | tf_op jit(solution)/shard_map/ppermute | solution.py:409
  24.0 1.6 %collective-permute-done.2.refs_7_ = bf16[256,256]{1,0:T(8,128)(2,1)S(1)} collective-permute-done((bf16[256,256]{1,0:T(8,128)(2,1)S(1)}, bf16[256,256]{1,0:T(8,128)(2,1)S(1)}, u32[]{:S(2)}, u32[]{:S(2)}) %collective-permute-start.2) | collective-permute-done | bytes 131104 | tf_op jit(solution)/shard_map/ppermute | solution.py:408
  25.6 1.6 %collective-permute-done.12.refs_6_ = bf16[256,256]{1,0:T(8,128)(2,1)S(1)} collective-permute-done((bf16[256,256]{1,0:T(8,128)(2,1)S(1)}, bf16[256,256]{1,0:T(8,128)(2,1)S(1)}, u32[]{:S(2)}, u32[]{:S(2)}) %collective-permute-start.12) | collective-permute-done | bytes 131104 | tf_op jit(solution)/shard_map/ppermute | solution.py:409
  27.2 0.7 pick.5
  28.1 0.5 collective-permute-start.14
  28.6 3.3 %collective-permute-done.3.refs_1_.refs_14_ = bf16[256,256]{1,0:T(8,128)(2,1)S(1)} collective-permute-done((bf16[256,256]{1,0:T(8,128)(2,1)S(1)}, bf16[256,256]{1,0:T(8,128)(2,1)S(1)}, u32[]{:S(2)}, u32[]{:S(2)}) %collective-permute-start.3) | collective-permute-done | bytes 131104 | tf_op jit(solution)/shard_map/ppermute | solution.py:408
  31.8 0.7 pick.6.refs_3_
  32.5 0.6 collective-permute-done.4.refs_2_.refs_15_
  33.2 0.4 pick.7
  33.6 17.6 %all_to_all.20.parts_ref = bf16[16,64,256]{2,1,0:T(8,128)(2,1)S(1)} all-to-all(bf16[16,64,256]{2,1,0:T(8,128)(2,1)S(1)} %bitcast.7), channel_id=1, replica_groups=mesh['tm'=16,'pts'=16] {'tm'}, dimensions={0} | all-to-all | bytes 1048576 | tf_op jit(solution)/shard_map/all_to_all | solution.py:422
  51.3 13.9 %all_to_all.21 = bf16[16,64,256]{2,1,0:T(8,128)(2,1)S(1)} all-to-all(bf16[16,64,256]{2,1,0:T(8,128)(2,1)S(1)} %get-tuple-element.24), channel_id=1, replica_groups=mesh['tm'=16,'pts'=16] {'tm'}, dimensions={0} | all-to-all | bytes 1048576 | tf_op jit(solution)/shard_map/all_to_all | solution.py:424
  65.2 7.0 %match.1 = bf16[1024,256]{1,0:T(8,128)(2,1)S(1)} custom-call(bf16[1024,256]{1,0:T(8,128)(2,1)S(1)} %bitcast.9, bf16[256,256]{1,0:T(8,128)(2,1)S(1)} %copy-done.5, bf16[256,256]{1,0:T(8,128)(2,1)S(1)} %collective-permute-done.5.refs_2_.refs_1_, bf16[256,256]{1,0:T(8,128)(2,1)S(1)} %collective-permute-done.6.refs_3_.refs_2_, ...), custom_call_target="tpu_custom_call" | custom-call | flops 4294967296 | bytes 2097152 | tf_op jit(solution)/shard_map/match/pallas_call | solution.py:179
  72.3 13.3 %all_to_all.22.m_ref = bf16[16,64,256]{2,1,0:T(8,128)(2,1)S(1)} all-to-all(bf16[16,64,256]{2,1,0:T(8,128)(2,1)S(1)} %bitcast.10), channel_id=1, replica_groups=mesh['tm'=16,'pts'=16] {'tm'}, dimensions={0} | all-to-all | bytes 1048576 | tf_op jit(solution)/shard_map/all_to_all | solution.py:426
  85.7 6.2 %mixer.1 = bf16[16,64,256]{2,1,0:T(8,128)(2,1)S(1)} custom-call(bf16[16,64,256]{2,1,0:T(8,128)(2,1)S(1)} %all_to_all.22.m_ref, bf16[64,256]{1,0:T(8,128)(2,1)S(1)} %get-tuple-element.25.q_ref, bf16[2,256,256]{2,1,0:T(8,128)(2,1)S(1)} %copy-done.4, bf16[512,2048]{1,0:T(8,128)(2,1)S(1)} %copy-done.2, bf16[2048,256]{1,0:T(8,128)(2,1)S(1)} %copy-done.3, ...), custom_call_target="tpu_custom_call" | custom-call | flops 3221225472 | bytes 2097152 | tf_op jit(solution)/shard_map/mixer/pallas_call | solution.py:366
  91.9 13.3 %all_to_all.23 = bf16[16,64,256]{2,1,0:T(8,128)(2,1)S(1)} all-to-all(bf16[16,64,256]{2,1,0:T(8,128)(2,1)S(1)} %mixer.1), channel_id=1, replica_groups=mesh['tm'=16,'pts'=16] {'tm'}, dimensions={0} | all-to-all | bytes 1048576 | tf_op jit(solution)/shard_map/all_to_all | solution.py:428
  105.2 6.1 %rematch.1 = (f32[1,1024]{1,0:T(1,128)}, f32[1,1024]{1,0:T(1,128)}) custom-call(bf16[1024,256]{1,0:T(8,128)(2,1)S(1)} %bitcast.8, bf16[256,256]{1,0:T(8,128)(2,1)S(1)} %copy-done.5, bf16[256,256]{1,0:T(8,128)(2,1)S(1)} %collective-permute-done.5.refs_2_.refs_1_, bf16[256,256]{1,0:T(8,128)(2,1)S(1)} %collective-permute-done.6.refs_3_.refs_2_, ...), custom_call_target="tpu_custom_call" | custom-call | flops 2147483648 | bytes 2097152 | tf_op jit(solution)/shard_map/rematch/pallas_call | solution.py:251
  (32 shorter events, 1.0 us)
Async XLA Ops:
  0.6 9.6 %collective-permute-start = (bf16[256,256]{1,0:T(8,128)(2,1)}, bf16[256,256]{1,0:T(8,128)(2,1)S(1)}, u32[]{:S(2)}, u32[]{:S(2)}) collective-permute-start(bf16[256,256]{1,0:T(8,128)(2,1)} %bitcast.11), channel_id=1, source_target_pairs={{0,2},{1,3},{2,4},{3,5},{4,6},{5,7},{6,8},{7,9},{8,10},{9,11},{10,... | collective-permute-start | bytes 393224 | tf_op jit(solution)/shard_map/ppermute | solution.py:404
  2.6 7.7 %collective-permute-start.6 = (bf16[256,256]{1,0:T(8,128)(2,1)}, bf16[256,256]{1,0:T(8,128)(2,1)S(1)}, u32[]{:S(2)}, u32[]{:S(2)}) collective-permute-start(bf16[256,256]{1,0:T(8,128)(2,1)} %bitcast.12), channel_id=1, source_target_pairs={{0,14},{1,15},{2,0},{3,1},{4,2},{5,3},{6,4},{7,5},{8,6},{9,7},{10,... | collective-permute-start | bytes 393224 | tf_op jit(solution)/shard_map/ppermute | solution.py:404
  8.5 10.4 %copy-start = (s32[1024,128]{1,0:T(8,128)S(1)}, s32[1024,128]{1,0:T(8,128)}, u32[]{:S(2)}) copy-start(s32[1024,128]{1,0:T(8,128)} %get-tuple-element.15.refs_0_) | copy-start | bytes 1572868
  8.5 10.4 %copy-start.5 = (bf16[256,256]{1,0:T(8,128)(2,1)S(1)}, bf16[256,256]{1,0:T(8,128)(2,1)}, u32[]{:S(2)}) copy-start(bf16[256,256]{1,0:T(8,128)(2,1)} %get-tuple-element.16.refs_1_.refs_0_) | copy-start | bytes 393220
  10.3 8.4 %collective-permute-start.1 = (bf16[256,256]{1,0:T(8,128)(2,1)S(1)}, bf16[256,256]{1,0:T(8,128)(2,1)S(1)}, u32[]{:S(2)}, u32[]{:S(2)}) collective-permute-start(bf16[256,256]{1,0:T(8,128)(2,1)S(1)} %collective-permute-done.refs_5_.refs_4_), channel_id=1, source_target_pairs={{0,2},{1,3},{2,4},{3,5},{4,6},{5,7},{6,8},{7,9},{8,10},{9,11},{10,... | collective-permute-start | bytes 393224 | tf_op jit(solution)/shard_map/ppermute | solution.py:408
  10.3 8.5 %collective-permute-start.5 = (bf16[256,256]{1,0:T(8,128)(2,1)}, bf16[256,256]{1,0:T(8,128)(2,1)S(1)}, u32[]{:S(2)}, u32[]{:S(2)}) collective-permute-start(bf16[256,256]{1,0:T(8,128)(2,1)} %get-tuple-element.16.refs_1_.refs_0_), channel_id=1, source_target_pairs={{0,1},{1,0},{2,3},{3,2},{4,5},{5,4},{6,7},{7,6},{8,9},{9,8},{10,11... | collective-permute-start | bytes 393224 | tf_op jit(solution)/shard_map/ppermute | solution.py:400
  10.3 8.5 %collective-permute-start.9 = (bf16[256,256]{1,0:T(8,128)(2,1)S(1)}, bf16[256,256]{1,0:T(8,128)(2,1)S(1)}, u32[]{:S(2)}, u32[]{:S(2)}) collective-permute-start(bf16[256,256]{1,0:T(8,128)(2,1)S(1)} %collective-permute-done.6.refs_3_.refs_2_), channel_id=1, source_target_pairs={{0,14},{1,15},{2,0},{3,1},{4,2},{5,3},{6,4},{7,5},{8,6},{9,7},{10,... | collective-permute-start | bytes 393224 | tf_op jit(solution)/shard_map/ppermute | solution.py:409
  13.5 5.3 %collective-permute-start.7 = (bf16[256,256]{1,0:T(8,128)(2,1)S(1)}, bf16[256,256]{1,0:T(8,128)(2,1)S(1)}, u32[]{:S(2)}, u32[]{:S(2)}) collective-permute-start(bf16[256,256]{1,0:T(8,128)(2,1)S(1)} %collective-permute-done.6.refs_3_.refs_2_), channel_id=1, source_target_pairs={{0,1},{1,0},{2,3},{3,2},{4,5},{5,4},{6,7},{7,6},{8,9},{9,8},{10,11... | collective-permute-start | bytes 393224 | tf_op jit(solution)/shard_map/ppermute | solution.py:419
  13.7 5.1 %collective-permute-start.8 = (bf16[256,256]{1,0:T(8,128)(2,1)S(1)}, bf16[256,256]{1,0:T(8,128)(2,1)S(1)}, u32[]{:S(2)}, u32[]{:S(2)}) collective-permute-start(bf16[256,256]{1,0:T(8,128)(2,1)S(1)} %collective-permute-done.refs_5_.refs_4_), channel_id=1, source_target_pairs={{0,1},{1,0},{2,3},{3,2},{4,5},{5,4},{6,7},{7,6},{8,9},{9,8},{10,11... | collective-permute-start | bytes 393224 | tf_op jit(solution)/shard_map/ppermute | solution.py:419
  18.7 6.9 %collective-permute-start.2 = (bf16[256,256]{1,0:T(8,128)(2,1)S(1)}, bf16[256,256]{1,0:T(8,128)(2,1)S(1)}, u32[]{:S(2)}, u32[]{:S(2)}) collective-permute-start(bf16[256,256]{1,0:T(8,128)(2,1)S(1)} %collective-permute-done.1.refs_8_), channel_id=1, source_target_pairs={{0,2},{1,3},{2,4},{3,5},{4,6},{5,7},{6,8},{7,9},{8,10},{9,11},{10,... | collective-permute-start | bytes 393224 | tf_op jit(solution)/shard_map/ppermute | solution.py:408
  20.5 6.7 %collective-permute-start.10 = (bf16[256,256]{1,0:T(8,128)(2,1)S(1)}, bf16[256,256]{1,0:T(8,128)(2,1)S(1)}, u32[]{:S(2)}, u32[]{:S(2)}) collective-permute-start(bf16[256,256]{1,0:T(8,128)(2,1)S(1)} %get-tuple-element.18.refs_1_.refs_6_), channel_id=1, source_target_pairs={{0,1},{1,0},{2,3},{3,2},{4,5},{5,4},{6,7},{7,6},{8,9},{9,8},{10,11... | collective-permute-start | bytes 393224 | tf_op jit(solution)/shard_map/ppermute | solution.py:419
  20.8 6.4 %collective-permute-start.12 = (bf16[256,256]{1,0:T(8,128)(2,1)S(1)}, bf16[256,256]{1,0:T(8,128)(2,1)S(1)}, u32[]{:S(2)}, u32[]{:S(2)}) collective-permute-start(bf16[256,256]{1,0:T(8,128)(2,1)S(1)} %collective-permute-done.9.refs_7_), channel_id=1, source_target_pairs={{0,14},{1,15},{2,0},{3,1},{4,2},{5,3},{6,4},{7,5},{8,6},{9,7},{10,... | collective-permute-start | bytes 393224 | tf_op jit(solution)/shard_map/ppermute | solution.py:409
  23.9 3.4 %collective-permute-start.11 = (bf16[256,256]{1,0:T(8,128)(2,1)S(1)}, bf16[256,256]{1,0:T(8,128)(2,1)S(1)}, u32[]{:S(2)}, u32[]{:S(2)}) collective-permute-start(bf16[256,256]{1,0:T(8,128)(2,1)S(1)} %get-tuple-element.19.refs_3_.refs_8_), channel_id=1, source_target_pairs={{0,1},{1,0},{2,3},{3,2},{4,5},{5,4},{6,7},{7,6},{8,9},{9,8},{10,11... | collective-permute-start | bytes 393224 | tf_op jit(solution)/shard_map/ppermute | solution.py:419
  25.6 6.2 %collective-permute-start.3 = (bf16[256,256]{1,0:T(8,128)(2,1)S(1)}, bf16[256,256]{1,0:T(8,128)(2,1)S(1)}, u32[]{:S(2)}, u32[]{:S(2)}) collective-permute-start(bf16[256,256]{1,0:T(8,128)(2,1)S(1)} %collective-permute-done.2.refs_7_), channel_id=1, source_target_pairs={{0,2},{1,3},{2,4},{3,5},{4,6},{5,7},{6,8},{7,9},{8,10},{9,11},{10,... | collective-permute-start | bytes 393224 | tf_op jit(solution)/shard_map/ppermute | solution.py:408
  28.0 3.9 %collective-permute-start.13 = (bf16[256,256]{1,0:T(8,128)(2,1)S(1)}, bf16[256,256]{1,0:T(8,128)(2,1)S(1)}, u32[]{:S(2)}, u32[]{:S(2)}) collective-permute-start(bf16[256,256]{1,0:T(8,128)(2,1)S(1)} %get-tuple-element.21.refs_1_.refs_10_), channel_id=1, source_target_pairs={{0,1},{1,0},{2,3},{3,2},{4,5},{5,4},{6,7},{7,6},{8,9},{9,8},{10,11... | collective-permute-start | bytes 393224 | tf_op jit(solution)/shard_map/ppermute | solution.py:419
  28.1 3.8 %collective-permute-start.14 = (bf16[256,256]{1,0:T(8,128)(2,1)S(1)}, bf16[256,256]{1,0:T(8,128)(2,1)S(1)}, u32[]{:S(2)}, u32[]{:S(2)}) collective-permute-start(bf16[256,256]{1,0:T(8,128)(2,1)S(1)} %get-tuple-element.22.refs_3_.refs_12_), channel_id=1, source_target_pairs={{0,1},{1,0},{2,3},{3,2},{4,5},{5,4},{6,7},{7,6},{8,9},{9,8},{10,11... | collective-permute-start | bytes 393224 | tf_op jit(solution)/shard_map/ppermute | solution.py:419
  31.8 1.3 %collective-permute-start.4 = (bf16[256,256]{1,0:T(8,128)(2,1)S(1)}, bf16[256,256]{1,0:T(8,128)(2,1)S(1)}, u32[]{:S(2)}, u32[]{:S(2)}) collective-permute-start(bf16[256,256]{1,0:T(8,128)(2,1)S(1)} %collective-permute-done.3.refs_1_.refs_14_), channel_id=1, source_target_pairs={{0,1},{1,0},{2,3},{3,2},{4,5},{5,4},{6,7},{7,6},{8,9},{9,8},{10,11... | collective-permute-start | bytes 393224 | tf_op jit(solution)/shard_map/ppermute | solution.py:419
  65.2 20.4 %copy-start.1 = (bf16[512,256]{1,0:T(8,128)(2,1)S(1)}, bf16[512,256]{1,0:T(8,128)(2,1)}, u32[]{:S(2)}) copy-start(bf16[512,256]{1,0:T(8,128)(2,1)} %tq_ref.1) | copy-start | bytes 786436
  65.2 20.4 %copy-start.2 = (bf16[512,2048]{1,0:T(8,128)(2,1)S(1)}, bf16[512,2048]{1,0:T(8,128)(2,1)}, u32[]{:S(2)}) copy-start(bf16[512,2048]{1,0:T(8,128)(2,1)} %up_ref.1) | copy-start | bytes 6291460
  65.2 20.4 %copy-start.3 = (bf16[2048,256]{1,0:T(8,128)(2,1)S(1)}, bf16[2048,256]{1,0:T(8,128)(2,1)}, u32[]{:S(2)}) copy-start(bf16[2048,256]{1,0:T(8,128)(2,1)} %get-tuple-element.27.folded_ref) | copy-start | bytes 3145732
  65.2 20.4 %copy-start.4 = (bf16[2,256,256]{2,1,0:T(8,128)(2,1)S(1)}, bf16[2,256,256]{2,1,0:T(8,128)(2,1)}, u32[]{:S(2)}) copy-start(bf16[2,256,256]{2,1,0:T(8,128)(2,1)} %get-tuple-element.26.mixes_ref) | copy-start | bytes 786436

commit v3 on v1

--- a/solution.py
+++ b/solution.py
@@ -60,7 +60,7 @@
         in_specs=[IN_HBM] * 3,
         out_specs=[IN_VMEM] * 2,
         scratch_shapes=[pltpu.VMEM((1, points), jnp.int32)] * 2 + [pltpu.SemaphoreType.DMA((3,))],
-        compiler_params=params(60),
+        compiler_params=params(6),
         cost_estimate=cost(points * 128, 4 * points * 128),
         name="begin",
     )(tile, query_frame, query_pos)
@@ -91,25 +91,19 @@
         target[...] = source[...]
 
 
-def pick(want, aways, tiles, before=(), sent=(), after=()):
+def pick(want, aways, tiles, before=(), sent=()):
     points, width = want.shape[0], tiles[0].shape[1]
     count = len(tiles)
-
-    def kernel(*refs):
-        ahead = 1 + count + len(before) + len(sent)
-        pick_kernel(aways, len(before), len(sent), *refs[:ahead], *refs[ahead + len(after) :])
-
-    return pl.pallas_call(
-        kernel,
+    return pl.pallas_call(
+        functools.partial(pick_kernel, aways, len(before), len(sent)),
         out_shape=[jax.ShapeDtypeStruct((points, width), jnp.bfloat16)]
         + [jax.ShapeDtypeStruct(piece.shape, piece.dtype) for piece in sent],
-        in_specs=[IN_VMEM] * (1 + count + len(before) + len(sent))
-        + [pl.BlockSpec(memory_space=pl.ANY)] * len(after),
+        in_specs=[IN_VMEM] * (1 + count + len(before) + len(sent)),
         out_specs=[IN_VMEM] * (1 + len(sent)),
         compiler_params=params(12),
         cost_estimate=cost(points * count * tiles[0].size, 2 * count * tiles[0].size),
         name="pick",
-    )(want, *tiles, *before, *sent, *after)
+    )(want, *tiles, *before, *sent)
 
 
 def join_kernel(parts_ref, query_ref, copies_ref):
@@ -258,21 +252,10 @@
     )(refined, *tiles)
 
 
-def prep_kernel(mix_hbm, down_hbm, tq_hbm, mixes_ref, folded_ref, token_ref, mix_ref, down_ref, tq_ref, sems):
+def prep_kernel(mix_ref, down_ref, to_query_ref, mixes_ref, folded_ref):
     frames = mix_ref.shape[0]
     side = mixes_ref.shape[1]
     repeat = side // frames
-    rows = down_ref.shape[0] // 8
-    pieces = [pl.ds(at * rows, rows) for at in range(8)]
-    copies = [
-        pltpu.make_async_copy(mix_hbm, mix_ref, sems.at[0]),
-        pltpu.make_async_copy(tq_hbm, tq_ref, sems.at[1]),
-    ] + [
-        pltpu.make_async_copy(down_hbm.at[piece], down_ref.at[piece], sems.at[2 + n])
-        for n, piece in enumerate(pieces)
-    ]
-    for copy in copies:
-        copy.start()
 
     def iota(shape, axis):
         return lax.broadcasted_iota(jnp.int32, shape, axis)
@@ -280,22 +263,16 @@
     spread = iota((side, frames), 0) // repeat == iota((side, frames), 1)
     spread = spread.astype(jnp.float32).astype(jnp.bfloat16)
     same = iota((side, side), 0) % repeat == iota((side, side), 1) % repeat
-    copies[0].wait()
     rest = mix_ref[...]
     for part in range(mixes_ref.shape[0]):
         now = rest.astype(jnp.bfloat16)
         rest = rest - now.astype(jnp.float32)
-        rows_of = jnp.dot(spread, now, preferred_element_type=jnp.float32).astype(jnp.bfloat16)
-        full = lax.dot_general(rows_of, spread, NT, preferred_element_type=jnp.float32)
+        rows = jnp.dot(spread, now, preferred_element_type=jnp.float32).astype(jnp.bfloat16)
+        full = lax.dot_general(rows, spread, NT, preferred_element_type=jnp.float32)
         mixes_ref[part] = jnp.where(same, full, 0.0).astype(jnp.bfloat16)
-    token_ref[...] = jnp.zeros_like(token_ref)
-    copies[1].wait()
-    for n in range(8):
-        copies[2 + n].wait()
-        here = slice(n * rows, (n + 1) * rows)
-        folded_ref[here] = jnp.dot(
-            down_ref[here], tq_ref[...], preferred_element_type=jnp.float32
-        ).astype(jnp.bfloat16)
+    folded_ref[...] = jnp.dot(
+        down_ref[...], to_query_ref[...], preferred_element_type=jnp.float32
+    ).astype(jnp.bfloat16)
 
 
 def prep(time_mix, w_down, w_query, side=256, parts=2):
@@ -305,27 +282,31 @@
         out_shape=[
             jax.ShapeDtypeStruct((parts, side, side), jnp.bfloat16),
             jax.ShapeDtypeStruct((hidden, w_query.shape[1]), jnp.bfloat16),
-            jax.ShapeDtypeStruct((8, 128), jnp.float32),
         ],
-        in_specs=[IN_HBM] * 3,
-        out_specs=[IN_VMEM] * 3,
-        scratch_shapes=[
-            pltpu.VMEM(time_mix.shape, time_mix.dtype),
-            pltpu.VMEM(w_down.shape, w_down.dtype),
-            pltpu.VMEM(w_query.shape, w_query.dtype),
-            pltpu.SemaphoreType.DMA((10,)),
-        ],
-        compiler_params=params(56),
+        in_specs=[IN_VMEM] * 3,
+        out_specs=[IN_VMEM] * 2,
+        compiler_params=params(10),
         cost_estimate=cost(w_down.size * w_query.shape[1], 2 * w_down.size),
         name="prep",
     )(time_mix, w_down, w_query)
 
 
-def mixer_kernel(step, m_ref, q_ref, mixes_ref, up_ref, folded_ref, tq_ref, out_ref):
+def mixer_kernel(step, m_ref, q_ref, mixes_hbm, up_hbm, folded_hbm, tq_hbm, out_ref, *scratch):
+    mixes_ref, up_ref, folded_ref, tq_ref, sems = scratch
     frames, points, width = m_ref.shape
     side = mixes_ref.shape[1]
     repeat = side // frames
     hidden = up_ref.shape[1]
+    pairs = [(mixes_hbm, mixes_ref), (tq_hbm, tq_ref)]
+    for h in range(0, hidden, step):
+        part = pl.ds(h, step)
+        pairs.append((up_hbm.at[:, part], up_ref.at[:, part]))
+        pairs.append((folded_hbm.at[part], folded_ref.at[part]))
+    copies = [
+        pltpu.make_async_copy(source, target, sems.at[n]) for n, (source, target) in enumerate(pairs)
+    ]
+    for copy in copies:
+        copy.start()
     for j in range(points // repeat):
         here = slice(j * repeat, (j + 1) * repeat)
         query = q_ref[here]
@@ -335,6 +316,8 @@
         ).astype(jnp.float32)
         power = jnp.mean(tokens * tokens, axis=1, keepdims=True)
         normed = (tokens * lax.rsqrt(power + 1e-06)).astype(jnp.bfloat16)
+        if j == 0:
+            copies[0].wait()
         section = tokens
         for part in range(mixes_ref.shape[0]):
             section = section + jnp.dot(
@@ -344,8 +327,13 @@
         section = kept.astype(jnp.float32)
         power = jnp.mean(section * section, axis=1, keepdims=True)
         inner = (section * lax.rsqrt(power + 1e-06)).astype(jnp.bfloat16)
+        if j == 0:
+            copies[1].wait()
         acc = jnp.dot(kept, tq_ref[...], preferred_element_type=jnp.float32)
-        for h in range(0, hidden, step):
+        for n, h in enumerate(range(0, hidden, step)):
+            if j == 0:
+                copies[2 + 2 * n].wait()
+                copies[3 + 2 * n].wait()
             upper = jnp.dot(inner, up_ref[:, h : h + step], preferred_element_type=jnp.float32)
             upper = jax.nn.gelu(upper).astype(jnp.bfloat16)
             acc = acc + jnp.dot(
@@ -358,12 +346,15 @@
 
 
 def mixer(matched, query, mixes, w_up, folded, w_query, step=256):
+    held = (mixes, w_up, folded, w_query)
     return pl.pallas_call(
         functools.partial(mixer_kernel, step),
         out_shape=jax.ShapeDtypeStruct(matched.shape, jnp.bfloat16),
-        in_specs=[IN_VMEM] * 6,
+        in_specs=[IN_VMEM] * 2 + [IN_HBM] * 4,
         out_specs=IN_VMEM,
-        compiler_params=params(16),
+        scratch_shapes=[pltpu.VMEM(array.shape, array.dtype) for array in held]
+        + [pltpu.SemaphoreType.DMA((2 + 2 * (w_up.shape[1] // step),))],
+        compiler_params=params(54),
         cost_estimate=cost(matched.shape[0] * matched.shape[1] * (w_up.size + folded.size), 2 * w_up.size),
         name="mixer",
     )(matched, query, mixes, w_up, folded, w_query)
@@ -388,7 +379,6 @@
     chips = lax.axis_size("pts") // 2
     width = feats.shape[2]
     tile, want = begin(feats[0], query_frame.reshape(1, points), query_pos.reshape(1, points))
-    mixes, folded, token = prep(time_mix, w_down, w_query)
     swap = swap_pairs(chips)
     up, down = ring_pairs(chips, 1), ring_pairs(chips, -1)
     half = chips // 2
@@ -396,15 +386,14 @@
     aways = [0]
     own = []
     done = 0
-    below, above = lax.ppermute(tile, "pts", up), lax.ppermute(tile, "pts", down)
+    below, above = lax.ppermute(feats[0], "pts", up), lax.ppermute(feats[0], "pts", down)
     for step in range(1, half + 1):
         sent = [above, below] if step < half else [below]
         if step < half:
             below = lax.ppermute(below, "pts", up)
             above = lax.ppermute(above, "pts", down) if step + 1 < half else None
-        if step > 1 and step < half:
-            after = (token,) if step == 2 else ()
-            picked, *sent = pick(want, aways[done:], tiles[2 * done :], own, sent, after)
+        if step == half - 1:
+            picked, *sent = pick(want, aways[done:], tiles[2 * done :], own, sent)
             own = [picked]
             done = len(aways)
         elif step == half:
@@ -417,6 +406,7 @@
     parts = lax.all_to_all(own[0].reshape(groups, share, width), "tm", 0, 0, tiled=True)
     query_here, copies = join(parts)
     query = lax.all_to_all(copies, "tm", 0, 0, tiled=True).reshape(points, width)
+    mixes, folded = prep(time_mix, w_down, w_query)
     matched = match(query, tiles).reshape(groups, share, width)
     matched = lax.all_to_all(matched, "tm", 0, 0, tiled=True)
     refined = mixer(matched, query_here, mixes, w_up, folded, w_query)

time: 113 us -> 116 us (1.027)
  blocking collectives: 58.2 us -> 45.2 us
  waiting for transfers between devices: 10.7 us -> 16.7 us
  starting transfers between devices: 14 us -> 19.5 us
  local copies, waits for them, and re-layouts: 0.71 us -> 4.08 us
    all_to_all x1 -> x0, blocking collectives: 13.3 us -> none  [shards(): matched = lax.all_to_all(matched, 'tm', 0, 0, tiled=True)]
    all_to_all x0 -> x1, waiting for transfers between devices: none -> 6.3 us  [shards(): matched = lax.all_to_all(matched, 'tm', 0, 0, tiled=True)]
    all_to_all x0 -> x1, starting transfers between devices: none -> 5.42 us  [shards(): matched = lax.all_to_all(matched, 'tm', 0, 0, tiled=True)]
    pallas_call x1, Pallas kernels: 6.22 us -> 10.8 us  [mixer(): pl.pallas_call(functools.partial(mixer_kernel, step), out_shape=jax.Shape...]
    ppermute x3, waiting for transfers between devices: 4.76 us -> 8.82 us  [shards(): below = lax.ppermute(below, 'pts', up)]
    pallas_call x1, Pallas kernels: 4.43 us -> 0.9 us  [prep(): pl.pallas_call(prep_kernel, out_shape=[jax.ShapeDtypeStruct((parts, side,...]
    unnamed x14 -> x46, local copies, waits for them, and re-layouts: 0.71 us -> 4.08 us
    ppermute x2, waiting for transfers between devices: 3.62 us -> 0.91 us  [the longest x1 0.9 us: shards(): lax.ppermute(feats[0], 'pts', up)]
  transfers between devices with their start and end apart: 15 -> 16, of which waited for: 5 -> 6; matrix products, arithmetic and copies ran while one was open for 0% -> 0% of each run, Pallas kernels for 6% -> 3%
where the time goes in v3:
time: 116 us; the launch traced here: 115 us
  blocking collectives  45.2 us (39%)
  Pallas kernels  28.9 us (25%)
  starting transfers between devices  19.5 us (17%)
  waiting for transfers between devices  16.7 us (14%)
  local copies, waits for them, and re-layouts  4.08 us (4%)
    all_to_all x1, blocking collectives, shards(): lax.all_to_all(own[0].reshape(groups, share, width), 'tm', 0, 0, tiled=True)  17.6 us
    all_to_all x1, blocking collectives, shards(): lax.all_to_all(copies, 'tm', 0, 0, tiled=True).reshape(points, width)  13.9 us
    all_to_all x1, blocking collectives, shards(): lax.all_to_all(refined, 'tm', 0, 0, tiled=True).reshape(points, width)  13.6 us
    pallas_call x1, Pallas kernels, mixer(): pl.pallas_call(functools.partial(mixer_kernel, step), out_shape=jax.Shape...  10.8 us
    ppermute x3, waiting for transfers between devices, shards(): below = lax.ppermute(below, 'pts', up)  8.82 us
    pallas_call x1, Pallas kernels, match(): pl.pallas_call(functools.partial(match_kernel, count, block, LOG2E * widt...  7.93 us
    ppermute x2, starting transfers between devices, shards(): above = lax.ppermute(above, 'pts', down) if step + 1 < half else None  6.46 us
    all_to_all x1, waiting for transfers between devices, shards(): matched = lax.all_to_all(matched, 'tm', 0, 0, tiled=True)  6.3 us
  transfers between devices with their start and end apart: 16, of which 6 were waited for; matrix products, arithmetic and copies ran while one was open for 0% of the time, Pallas kernels for 3%

profile of v3, /device:TPU:8, one launch (start us, length us, event | category | flops | bytes accessed | tf_op | source)
XLA Modules:
  0.0 115.3 jit_solution(10637638910233984937)
XLA Ops:
  0.6 2.0 %collective-permute-start = (bf16[256,256]{1,0:T(8,128)(2,1)}, bf16[256,256]{1,0:T(8,128)(2,1)S(1)}, u32[]{:S(2)}, u32[]{:S(2)}) collective-permute-start(bf16[256,256]{1,0:T(8,128)(2,1)} %bitcast.10), channel_id=1, source_target_pairs={{0,2},{1,3},{2,4},{3,5},{4,6},{5,7},{6,8},{7,9},{8,10},{9,11},{10,... | collective-permute-start | bytes 393224 | tf_op jit(solution)/shard_map/ppermute | solution.py:389
  2.6 4.0 %collective-permute-start.6 = (bf16[256,256]{1,0:T(8,128)(2,1)}, bf16[256,256]{1,0:T(8,128)(2,1)S(1)}, u32[]{:S(2)}, u32[]{:S(2)}) collective-permute-start(bf16[256,256]{1,0:T(8,128)(2,1)} %bitcast.11), channel_id=1, source_target_pairs={{0,14},{1,15},{2,0},{3,1},{4,2},{5,3},{6,4},{7,5},{8,6},{9,7},{10,... | collective-permute-start | bytes 393224 | tf_op jit(solution)/shard_map/ppermute | solution.py:389
  6.7 0.9 copy-done.2
  7.6 0.7 copy-done.4
  8.3 0.7 copy-done.5
  9.4 0.9 collective-permute-done.refs_4_
  10.3 3.2 %collective-permute-start.9 = (bf16[256,256]{1,0:T(8,128)(2,1)S(1)}, bf16[256,256]{1,0:T(8,128)(2,1)S(1)}, u32[]{:S(2)}, u32[]{:S(2)}) collective-permute-start(bf16[256,256]{1,0:T(8,128)(2,1)S(1)} %collective-permute-done.6.refs_2_), channel_id=1, source_target_pairs={{0,14},{1,15},{2,0},{3,1},{4,2},{5,3},{6,4},{7,5},{8,6},{9,7},{10,... | collective-permute-start | bytes 393224 | tf_op jit(solution)/shard_map/ppermute | solution.py:394
  14.0 2.4 %collective-permute-done.1.refs_8_ = bf16[256,256]{1,0:T(8,128)(2,1)S(1)} collective-permute-done((bf16[256,256]{1,0:T(8,128)(2,1)S(1)}, bf16[256,256]{1,0:T(8,128)(2,1)S(1)}, u32[]{:S(2)}, u32[]{:S(2)}) %collective-permute-start.1) | collective-permute-done | bytes 131104 | tf_op jit(solution)/shard_map/ppermute | solution.py:393
  16.5 3.2 %collective-permute-start.12 = (bf16[256,256]{1,0:T(8,128)(2,1)S(1)}, bf16[256,256]{1,0:T(8,128)(2,1)S(1)}, u32[]{:S(2)}, u32[]{:S(2)}) collective-permute-start(bf16[256,256]{1,0:T(8,128)(2,1)S(1)} %collective-permute-done.9.refs_6_), channel_id=1, source_target_pairs={{0,14},{1,15},{2,0},{3,1},{4,2},{5,3},{6,4},{7,5},{8,6},{9,7},{10,... | collective-permute-start | bytes 393224 | tf_op jit(solution)/shard_map/ppermute | solution.py:394
  20.2 2.4 %collective-permute-done.2.refs_11_ = bf16[256,256]{1,0:T(8,128)(2,1)S(1)} collective-permute-done((bf16[256,256]{1,0:T(8,128)(2,1)S(1)}, bf16[256,256]{1,0:T(8,128)(2,1)S(1)}, u32[]{:S(2)}, u32[]{:S(2)}) %collective-permute-start.2) | collective-permute-done | bytes 131104 | tf_op jit(solution)/shard_map/ppermute | solution.py:393
  22.7 1.5 %pick.3 = (bf16[1024,256]{1,0:T(8,128)(2,1)S(1)}, bf16[256,256]{1,0:T(8,128)(2,1)S(1)}, bf16[256,256]{1,0:T(8,128)(2,1)S(1)}) custom-call(s32[1024,128]{1,0:T(8,128)S(1)} %get-tuple-element.11.want_ref, bf16[256,256]{1,0:T(8,128)(2,1)S(1)} %get-tuple-element.12.refs_0_, bf16[256,256]{1,0:T(8,128)(2,1)S(1)} %collective-permute-done.5.refs_1_, ...), custom_call_target="tpu_custom_call" | custom-call | flops 1342177280 | bytes 1310720 | tf_op jit(solution)/shard_map/pick/pallas_call | solution.py:97
  24.8 4.0 %collective-permute-done.3.refs_0_.refs_14_ = bf16[256,256]{1,0:T(8,128)(2,1)S(1)} collective-permute-done((bf16[256,256]{1,0:T(8,128)(2,1)S(1)}, bf16[256,256]{1,0:T(8,128)(2,1)S(1)}, u32[]{:S(2)}, u32[]{:S(2)}) %collective-permute-start.3) | collective-permute-done | bytes 131104 | tf_op jit(solution)/shard_map/ppermute | solution.py:393
  28.8 0.7 pick.4.refs_2_
  30.6 17.6 %all_to_all.20.parts_ref = bf16[16,64,256]{2,1,0:T(8,128)(2,1)S(1)} all-to-all(bf16[16,64,256]{2,1,0:T(8,128)(2,1)S(1)} %bitcast.7), channel_id=1, replica_groups=mesh['tm'=16,'pts'=16] {'tm'}, dimensions={0} | all-to-all | bytes 1048576 | tf_op jit(solution)/shard_map/all_to_all | solution.py:406
  48.3 13.9 %all_to_all.21 = bf16[16,64,256]{2,1,0:T(8,128)(2,1)S(1)} all-to-all(bf16[16,64,256]{2,1,0:T(8,128)(2,1)S(1)} %get-tuple-element.16), channel_id=1, replica_groups=mesh['tm'=16,'pts'=16] {'tm'}, dimensions={0} | all-to-all | bytes 1048576 | tf_op jit(solution)/shard_map/all_to_all | solution.py:408
  62.3 7.9 %match.1 = bf16[1024,256]{1,0:T(8,128)(2,1)} custom-call(bf16[1024,256]{1,0:T(8,128)(2,1)S(1)} %bitcast.9, bf16[256,256]{1,0:T(8,128)(2,1)S(1)} %get-tuple-element.12.refs_0_, bf16[256,256]{1,0:T(8,128)(2,1)S(1)} %collective-permute-done.5.refs_1_, bf16[256,256]{1,0:T(8,128)(2,1)S(1)} %collective-permute-done.6.refs_2_, ...), custom_call_target="tpu_custom_call" | custom-call | flops 4294967296 | bytes 2097152 | tf_op jit(solution)/shard_map/match/pallas_call | solution.py:172
  70.3 5.4 %all-to-all-start.2 = ((bf16[16,64,256]{2,1,0:T(8,128)(2,1)}), bf16[16,64,256]{2,1,0:T(8,128)(2,1)}, u32[]{:S(2)}, u32[]{:S(2)}) async-start(bf16[16,64,256]{2,1,0:T(8,128)(2,1)} %bitcast.5), calls=%async_computation.2 | async-start | bytes 1048576 | tf_op jit(solution)/shard_map/all_to_all | solution.py:411
  75.7 0.9 prep.1
  76.6 1.0 copy-done.6
  77.6 0.7 copy-done.7
  78.3 6.3 %all-to-all-done.2.m_ref = bf16[16,64,256]{2,1,0:T(8,128)(2,1)} async-done(((bf16[16,64,256]{2,1,0:T(8,128)(2,1)}), bf16[16,64,256]{2,1,0:T(8,128)(2,1)}, u32[]{:S(2)}, u32[]{:S(2)}) %all-to-all-start.2) | async-done | bytes 524320 | tf_op jit(solution)/shard_map/all_to_all | solution.py:411
  84.7 10.8 %mixer.1 = bf16[16,64,256]{2,1,0:T(8,128)(2,1)} custom-call(bf16[16,64,256]{2,1,0:T(8,128)(2,1)} %all-to-all-done.2.m_ref, bf16[64,256]{1,0:T(8,128)(2,1)} %copy-done.22, bf16[2,256,256]{2,1,0:T(8,128)(2,1)} %copy-done.7, bf16[512,2048]{1,0:T(8,128)(2,1)} %up_hbm.1, bf16[2048,256]{1,0:T(8,128)(2,1)} %copy-done.6, bf16[512,256]{1,0:T(8,128)(2,1)} %tq_hbm.1), custom_call_target="tpu_custom_call" | custom-call | flops 3221225472 | bytes 2097152 | tf_op jit(solution)/shard_map/mixer/pallas_call | solution.py:350
  95.4 13.6 %all_to_all.22 = bf16[16,64,256]{2,1,0:T(8,128)(2,1)S(1)} all-to-all(bf16[16,64,256]{2,1,0:T(8,128)(2,1)} %mixer.1), channel_id=1, replica_groups=mesh['tm'=16,'pts'=16] {'tm'}, dimensions={0} | all-to-all | bytes 1048576 | tf_op jit(solution)/shard_map/all_to_all | solution.py:413
  109.1 6.1 %rematch.1 = (f32[1,1024]{1,0:T(1,128)}, f32[1,1024]{1,0:T(1,128)}) custom-call(bf16[1024,256]{1,0:T(8,128)(2,1)S(1)} %bitcast.8, bf16[256,256]{1,0:T(8,128)(2,1)S(1)} %get-tuple-element.12.refs_0_, bf16[256,256]{1,0:T(8,128)(2,1)S(1)} %copy-done.13, bf16[256,256]{1,0:T(8,128)(2,1)S(1)} %collective-permute-done.6.refs_2_, bf16[256,256]{1,0:T(8,128)(2,1)S(1)} %copy-done.15, ...), custom_call_target="tpu_custom_call" | custom-call | flops 2147483648 | bytes 2097152 | tf_op jit(solution)/shard_map/rematch/pallas_call | solution.py:244
  (66 shorter events, 3.3 us)
Async XLA Ops:
  0.6 9.6 %collective-permute-start = (bf16[256,256]{1,0:T(8,128)(2,1)}, bf16[256,256]{1,0:T(8,128)(2,1)S(1)}, u32[]{:S(2)}, u32[]{:S(2)}) collective-permute-start(bf16[256,256]{1,0:T(8,128)(2,1)} %bitcast.10), channel_id=1, source_target_pairs={{0,2},{1,3},{2,4},{3,5},{4,6},{5,7},{6,8},{7,9},{8,10},{9,11},{10,... | collective-permute-start | bytes 393224 | tf_op jit(solution)/shard_map/ppermute | solution.py:389
  2.6 7.7 %collective-permute-start.6 = (bf16[256,256]{1,0:T(8,128)(2,1)}, bf16[256,256]{1,0:T(8,128)(2,1)S(1)}, u32[]{:S(2)}, u32[]{:S(2)}) collective-permute-start(bf16[256,256]{1,0:T(8,128)(2,1)} %bitcast.11), channel_id=1, source_target_pairs={{0,14},{1,15},{2,0},{3,1},{4,2},{5,3},{6,4},{7,5},{8,6},{9,7},{10,... | collective-permute-start | bytes 393224 | tf_op jit(solution)/shard_map/ppermute | solution.py:389
  10.3 6.2 %collective-permute-start.1 = (bf16[256,256]{1,0:T(8,128)(2,1)S(1)}, bf16[256,256]{1,0:T(8,128)(2,1)S(1)}, u32[]{:S(2)}, u32[]{:S(2)}) collective-permute-start(bf16[256,256]{1,0:T(8,128)(2,1)S(1)} %collective-permute-done.refs_4_), channel_id=1, source_target_pairs={{0,2},{1,3},{2,4},{3,5},{4,6},{5,7},{6,8},{7,9},{8,10},{9,11},{10,... | collective-permute-start | bytes 393224 | tf_op jit(solution)/shard_map/ppermute | solution.py:393
  10.3 6.2 %collective-permute-start.9 = (bf16[256,256]{1,0:T(8,128)(2,1)S(1)}, bf16[256,256]{1,0:T(8,128)(2,1)S(1)}, u32[]{:S(2)}, u32[]{:S(2)}) collective-permute-start(bf16[256,256]{1,0:T(8,128)(2,1)S(1)} %collective-permute-done.6.refs_2_), channel_id=1, source_target_pairs={{0,14},{1,15},{2,0},{3,1},{4,2},{5,3},{6,4},{7,5},{8,6},{9,7},{10,... | collective-permute-start | bytes 393224 | tf_op jit(solution)/shard_map/ppermute | solution.py:394
  13.5 6.2 %collective-permute-start.5 = (bf16[256,256]{1,0:T(8,128)(2,1)S(1)}, bf16[256,256]{1,0:T(8,128)(2,1)S(1)}, u32[]{:S(2)}, u32[]{:S(2)}) collective-permute-start(bf16[256,256]{1,0:T(8,128)(2,1)S(1)} %get-tuple-element.12.refs_0_), channel_id=1, source_target_pairs={{0,1},{1,0},{2,3},{3,2},{4,5},{5,4},{6,7},{7,6},{8,9},{9,8},{10,11... | collective-permute-start | bytes 393224 | tf_op jit(solution)/shard_map/ppermute | solution.py:385
  13.5 6.2 %collective-permute-start.7 = (bf16[256,256]{1,0:T(8,128)(2,1)S(1)}, bf16[256,256]{1,0:T(8,128)(2,1)S(1)}, u32[]{:S(2)}, u32[]{:S(2)}) collective-permute-start(bf16[256,256]{1,0:T(8,128)(2,1)S(1)} %collective-permute-done.6.refs_2_), channel_id=1, source_target_pairs={{0,1},{1,0},{2,3},{3,2},{4,5},{5,4},{6,7},{7,6},{8,9},{9,8},{10,11... | collective-permute-start | bytes 393224 | tf_op jit(solution)/shard_map/ppermute | solution.py:403
  14.0 8.6 %collective-permute-start.8 = (bf16[256,256]{1,0:T(8,128)(2,1)S(1)}, bf16[256,256]{1,0:T(8,128)(2,1)S(1)}, u32[]{:S(2)}, u32[]{:S(2)}) collective-permute-start(bf16[256,256]{1,0:T(8,128)(2,1)S(1)} %collective-permute-done.refs_4_), channel_id=1, source_target_pairs={{0,1},{1,0},{2,3},{3,2},{4,5},{5,4},{6,7},{7,6},{8,9},{9,8},{10,11... | collective-permute-start | bytes 393224 | tf_op jit(solution)/shard_map/ppermute | solution.py:403
  16.4 45.8 %copy-start.8 = (bf16[256,256]{1,0:T(8,128)(2,1)}, bf16[256,256]{1,0:T(8,128)(2,1)S(1)}, u32[]{:S(2)}) copy-start(bf16[256,256]{1,0:T(8,128)(2,1)S(1)} %collective-permute-done.1.refs_8_) | copy-start | bytes 393220
  16.4 6.2 %collective-permute-start.2 = (bf16[256,256]{1,0:T(8,128)(2,1)S(1)}, bf16[256,256]{1,0:T(8,128)(2,1)S(1)}, u32[]{:S(2)}, u32[]{:S(2)}) collective-permute-start(bf16[256,256]{1,0:T(8,128)(2,1)S(1)} %collective-permute-done.1.refs_8_), channel_id=1, source_target_pairs={{0,2},{1,3},{2,4},{3,5},{4,6},{5,7},{6,8},{7,9},{8,10},{9,11},{10,... | collective-permute-start | bytes 393224 | tf_op jit(solution)/shard_map/ppermute | solution.py:393
  16.5 45.8 %copy-start.10 = (bf16[256,256]{1,0:T(8,128)(2,1)}, bf16[256,256]{1,0:T(8,128)(2,1)S(1)}, u32[]{:S(2)}) copy-start(bf16[256,256]{1,0:T(8,128)(2,1)S(1)} %collective-permute-done.9.refs_6_) | copy-start | bytes 393220
  16.5 6.2 %collective-permute-start.12 = (bf16[256,256]{1,0:T(8,128)(2,1)S(1)}, bf16[256,256]{1,0:T(8,128)(2,1)S(1)}, u32[]{:S(2)}, u32[]{:S(2)}) collective-permute-start(bf16[256,256]{1,0:T(8,128)(2,1)S(1)} %collective-permute-done.9.refs_6_), channel_id=1, source_target_pairs={{0,14},{1,15},{2,0},{3,1},{4,2},{5,3},{6,4},{7,5},{8,6},{9,7},{10,... | collective-permute-start | bytes 393224 | tf_op jit(solution)/shard_map/ppermute | solution.py:394
  19.7 42.6 %copy-start.12 = (bf16[256,256]{1,0:T(8,128)(2,1)}, bf16[256,256]{1,0:T(8,128)(2,1)S(1)}, u32[]{:S(2)}) copy-start(bf16[256,256]{1,0:T(8,128)(2,1)S(1)} %collective-permute-done.5.refs_1_) | copy-start | bytes 393220
  19.7 3.0 %collective-permute-start.10 = (bf16[256,256]{1,0:T(8,128)(2,1)S(1)}, bf16[256,256]{1,0:T(8,128)(2,1)S(1)}, u32[]{:S(2)}, u32[]{:S(2)}) collective-permute-start(bf16[256,256]{1,0:T(8,128)(2,1)S(1)} %collective-permute-done.9.refs_6_), channel_id=1, source_target_pairs={{0,1},{1,0},{2,3},{3,2},{4,5},{5,4},{6,7},{7,6},{8,9},{9,8},{10,11... | collective-permute-start | bytes 393224 | tf_op jit(solution)/shard_map/ppermute | solution.py:403
  19.7 42.5 %copy-start.14 = (bf16[256,256]{1,0:T(8,128)(2,1)}, bf16[256,256]{1,0:T(8,128)(2,1)S(1)}, u32[]{:S(2)}) copy-start(bf16[256,256]{1,0:T(8,128)(2,1)S(1)} %collective-permute-done.7.refs_3_) | copy-start | bytes 393220
  19.7 2.9 %collective-permute-start.11 = (bf16[256,256]{1,0:T(8,128)(2,1)S(1)}, bf16[256,256]{1,0:T(8,128)(2,1)S(1)}, u32[]{:S(2)}, u32[]{:S(2)}) collective-permute-start(bf16[256,256]{1,0:T(8,128)(2,1)S(1)} %collective-permute-done.1.refs_8_), channel_id=1, source_target_pairs={{0,1},{1,0},{2,3},{3,2},{4,5},{5,4},{6,7},{7,6},{8,9},{9,8},{10,11... | collective-permute-start | bytes 393224 | tf_op jit(solution)/shard_map/ppermute | solution.py:403
  22.6 6.2 %collective-permute-start.3 = (bf16[256,256]{1,0:T(8,128)(2,1)S(1)}, bf16[256,256]{1,0:T(8,128)(2,1)S(1)}, u32[]{:S(2)}, u32[]{:S(2)}) collective-permute-start(bf16[256,256]{1,0:T(8,128)(2,1)S(1)} %collective-permute-done.2.refs_11_), channel_id=1, source_target_pairs={{0,2},{1,3},{2,4},{3,5},{4,6},{5,7},{6,8},{7,9},{8,10},{9,11},{10,... | collective-permute-start | bytes 393224 | tf_op jit(solution)/shard_map/ppermute | solution.py:393
  22.6 39.6 %copy-start.16 = (bf16[256,256]{1,0:T(8,128)(2,1)}, bf16[256,256]{1,0:T(8,128)(2,1)S(1)}, u32[]{:S(2)}) copy-start(bf16[256,256]{1,0:T(8,128)(2,1)S(1)} %collective-permute-done.8.refs_5_) | copy-start | bytes 393220
  22.7 39.6 %copy-start.18 = (bf16[256,256]{1,0:T(8,128)(2,1)}, bf16[256,256]{1,0:T(8,128)(2,1)S(1)}, u32[]{:S(2)}) copy-start(bf16[256,256]{1,0:T(8,128)(2,1)S(1)} %collective-permute-done.10.refs_7_) | copy-start | bytes 393220
  22.7 39.6 %copy-start.20 = (bf16[256,256]{1,0:T(8,128)(2,1)}, bf16[256,256]{1,0:T(8,128)(2,1)S(1)}, u32[]{:S(2)}) copy-start(bf16[256,256]{1,0:T(8,128)(2,1)S(1)} %collective-permute-done.11.refs_9_) | copy-start | bytes 393220
  24.2 4.6 %collective-permute-start.13 = (bf16[256,256]{1,0:T(8,128)(2,1)S(1)}, bf16[256,256]{1,0:T(8,128)(2,1)S(1)}, u32[]{:S(2)}, u32[]{:S(2)}) collective-permute-start(bf16[256,256]{1,0:T(8,128)(2,1)S(1)} %get-tuple-element.13.refs_0_.refs_10_), channel_id=1, source_target_pairs={{0,1},{1,0},{2,3},{3,2},{4,5},{5,4},{6,7},{7,6},{8,9},{9,8},{10,11... | collective-permute-start | bytes 393224 | tf_op jit(solution)/shard_map/ppermute | solution.py:403
  24.3 4.5 %collective-permute-start.14 = (bf16[256,256]{1,0:T(8,128)(2,1)S(1)}, bf16[256,256]{1,0:T(8,128)(2,1)S(1)}, u32[]{:S(2)}, u32[]{:S(2)}) collective-permute-start(bf16[256,256]{1,0:T(8,128)(2,1)S(1)} %get-tuple-element.14.refs_2_.refs_12_), channel_id=1, source_target_pairs={{0,1},{1,0},{2,3},{3,2},{4,5},{5,4},{6,7},{7,6},{8,9},{9,8},{10,11... | collective-permute-start | bytes 393224 | tf_op jit(solution)/shard_map/ppermute | solution.py:403
  28.8 1.3 %collective-permute-start.4 = (bf16[256,256]{1,0:T(8,128)(2,1)S(1)}, bf16[256,256]{1,0:T(8,128)(2,1)S(1)}, u32[]{:S(2)}, u32[]{:S(2)}) collective-permute-start(bf16[256,256]{1,0:T(8,128)(2,1)S(1)} %collective-permute-done.3.refs_0_.refs_14_), channel_id=1, source_target_pairs={{0,1},{1,0},{2,3},{3,2},{4,5},{5,4},{6,7},{7,6},{8,9},{9,8},{10,11... | collective-permute-start | bytes 393224 | tf_op jit(solution)/shard_map/ppermute | solution.py:403
  70.3 14.4 %all-to-all-start.2 = ((bf16[16,64,256]{2,1,0:T(8,128)(2,1)}), bf16[16,64,256]{2,1,0:T(8,128)(2,1)}, u32[]{:S(2)}, u32[]{:S(2)}) async-start(bf16[16,64,256]{2,1,0:T(8,128)(2,1)} %bitcast.5), calls=%async_computation.2 | async-start | bytes 1048576 | tf_op jit(solution)/shard_map/all_to_all | solution.py:411
  84.6 24.5 %copy-start.17 = (bf16[256,256]{1,0:T(8,128)(2,1)S(1)}, bf16[256,256]{1,0:T(8,128)(2,1)}, u32[]{:S(2)}) copy-start(bf16[256,256]{1,0:T(8,128)(2,1)} %copy-done.16) | copy-start | bytes 393220
  (15 other events, 204.8 us)

commit v4 on v3

--- a/solution.py
+++ b/solution.py
@@ -10,6 +10,7 @@
 GRID = 64
 LOG2E = 1.4426950408889634
 IN_VMEM = pl.BlockSpec(memory_space=pltpu.VMEM)
+IN_SMEM = pl.BlockSpec(memory_space=pltpu.SMEM)
 IN_HBM = pl.BlockSpec(memory_space=pltpu.HBM)
 NT = (((1,), (1,)), ((), ()))
 
@@ -91,19 +92,25 @@
         target[...] = source[...]
 
 
-def pick(want, aways, tiles, before=(), sent=()):
+def pick(want, aways, tiles, before=(), sent=(), after=()):
     points, width = want.shape[0], tiles[0].shape[1]
     count = len(tiles)
-    return pl.pallas_call(
-        functools.partial(pick_kernel, aways, len(before), len(sent)),
+
+    def kernel(*refs):
+        ahead = 1 + count + len(before) + len(sent)
+        pick_kernel(aways, len(before), len(sent), *refs[:ahead], *refs[ahead + len(after) :])
+
+    return pl.pallas_call(
+        kernel,
         out_shape=[jax.ShapeDtypeStruct((points, width), jnp.bfloat16)]
         + [jax.ShapeDtypeStruct(piece.shape, piece.dtype) for piece in sent],
-        in_specs=[IN_VMEM] * (1 + count + len(before) + len(sent)),
+        in_specs=[IN_VMEM] * (1 + count + len(before) + len(sent))
+        + [IN_SMEM] * len(after),
         out_specs=[IN_VMEM] * (1 + len(sent)),
         compiler_params=params(12),
         cost_estimate=cost(points * count * tiles[0].size, 2 * count * tiles[0].size),
         name="pick",
-    )(want, *tiles, *before, *sent)
+    )(want, *tiles, *before, *sent, *after)
 
 
 def join_kernel(parts_ref, query_ref, copies_ref):
@@ -252,7 +259,7 @@
     )(refined, *tiles)
 
 
-def prep_kernel(mix_ref, down_ref, to_query_ref, mixes_ref, folded_ref):
+def spread_kernel(mix_ref, mixes_ref, token_ref):
     frames = mix_ref.shape[0]
     side = mixes_ref.shape[1]
     repeat = side // frames
@@ -270,94 +277,86 @@
         rows = jnp.dot(spread, now, preferred_element_type=jnp.float32).astype(jnp.bfloat16)
         full = lax.dot_general(rows, spread, NT, preferred_element_type=jnp.float32)
         mixes_ref[part] = jnp.where(same, full, 0.0).astype(jnp.bfloat16)
-    folded_ref[...] = jnp.dot(
-        down_ref[...], to_query_ref[...], preferred_element_type=jnp.float32
-    ).astype(jnp.bfloat16)
-
-
-def prep(time_mix, w_down, w_query, side=256, parts=2):
-    hidden, width = w_down.shape
-    return pl.pallas_call(
-        prep_kernel,
+    token_ref[0, 0] = 0
+
+
+def spread_mix(time_mix, side=256, parts=2):
+    return pl.pallas_call(
+        spread_kernel,
         out_shape=[
             jax.ShapeDtypeStruct((parts, side, side), jnp.bfloat16),
-            jax.ShapeDtypeStruct((hidden, w_query.shape[1]), jnp.bfloat16),
+            jax.ShapeDtypeStruct((1, 1), jnp.int32),
         ],
-        in_specs=[IN_VMEM] * 3,
-        out_specs=[IN_VMEM] * 2,
-        compiler_params=params(10),
-        cost_estimate=cost(w_down.size * w_query.shape[1], 2 * w_down.size),
-        name="prep",
-    )(time_mix, w_down, w_query)
-
-
-def mixer_kernel(step, m_ref, q_ref, mixes_hbm, up_hbm, folded_hbm, tq_hbm, out_ref, *scratch):
-    mixes_ref, up_ref, folded_ref, tq_ref, sems = scratch
+        in_specs=[IN_VMEM],
+        out_specs=[IN_VMEM, IN_SMEM],
+        compiler_params=params(6),
+        cost_estimate=cost(2 * parts * side * side * 16, parts * side * side * 2),
+        name="spread_mix",
+    )(time_mix)
+
+
+def mixer_kernel(step, m_ref, q_ref, mixes_ref, up_ref, down_ref, tq_ref, out_ref, lift_ref):
     frames, points, width = m_ref.shape
     side = mixes_ref.shape[1]
     repeat = side // frames
     hidden = up_ref.shape[1]
-    pairs = [(mixes_hbm, mixes_ref), (tq_hbm, tq_ref)]
-    for h in range(0, hidden, step):
-        part = pl.ds(h, step)
-        pairs.append((up_hbm.at[:, part], up_ref.at[:, part]))
-        pairs.append((folded_hbm.at[part], folded_ref.at[part]))
-    copies = [
-        pltpu.make_async_copy(source, target, sems.at[n]) for n, (source, target) in enumerate(pairs)
-    ]
-    for copy in copies:
-        copy.start()
+    lift_ref[...] = jnp.dot(q_ref[...], up_ref[width:], preferred_element_type=jnp.float32)
     for j in range(points // repeat):
         here = slice(j * repeat, (j + 1) * repeat)
-        query = q_ref[here]
+        query = q_ref[here].astype(jnp.float32)
+        repeated = jnp.concatenate([query] * frames, axis=0)
+        square = jnp.sum(repeated * repeated, axis=1, keepdims=True)
         matched = jnp.concatenate([m_ref[f, here] for f in range(frames)], axis=0)
-        tokens = jnp.concatenate(
-            [matched, jnp.concatenate([query] * frames, axis=0)], axis=1
-        ).astype(jnp.float32)
-        power = jnp.mean(tokens * tokens, axis=1, keepdims=True)
-        normed = (tokens * lax.rsqrt(power + 1e-06)).astype(jnp.bfloat16)
-        if j == 0:
-            copies[0].wait()
-        section = tokens
-        for part in range(mixes_ref.shape[0]):
-            section = section + jnp.dot(
-                mixes_ref[part], normed, preferred_element_type=jnp.float32
+        matched = matched.astype(jnp.float32)
+        power = (jnp.sum(matched * matched, axis=1, keepdims=True) + square) * (0.5 / width)
+        scale = lax.rsqrt(power + 1e-06)
+        wide = jnp.broadcast_to(scale, (side, 128))
+        high = wide.astype(jnp.bfloat16)
+        low = (wide - high.astype(jnp.float32)).astype(jnp.bfloat16)
+        normed = jnp.concatenate([(matched * scale).astype(jnp.bfloat16), high, low], axis=1)
+        blend = jnp.dot(mixes_ref[0], normed, preferred_element_type=jnp.float32)
+        for part in range(1, mixes_ref.shape[0]):
+            blend = blend + jnp.dot(mixes_ref[part], normed, preferred_element_type=jnp.float32)
+        section = (matched + blend[:, :width]).astype(jnp.bfloat16).astype(jnp.float32)
+        times = 1.0 + blend[:, width : width + 128] + blend[:, width + 128 :]
+        power = (
+            jnp.sum(section * section, axis=1, keepdims=True) + times * times * square
+        ) * (0.5 / width)
+        scale = lax.rsqrt(power + 1e-06)
+        inner = (section * jnp.concatenate([scale] * (width // 128), axis=1)).astype(jnp.bfloat16)
+        lifted = jnp.concatenate([scale * times] * (step // 128), axis=1)
+        lifted = lifted.reshape(frames, repeat, step)
+        acc = None
+        for h in range(0, hidden, step):
+            upper = jnp.dot(
+                inner, up_ref[:width, h : h + step], preferred_element_type=jnp.float32
             )
-        kept = section.astype(jnp.bfloat16)
-        section = kept.astype(jnp.float32)
-        power = jnp.mean(section * section, axis=1, keepdims=True)
-        inner = (section * lax.rsqrt(power + 1e-06)).astype(jnp.bfloat16)
-        if j == 0:
-            copies[1].wait()
-        acc = jnp.dot(kept, tq_ref[...], preferred_element_type=jnp.float32)
-        for n, h in enumerate(range(0, hidden, step)):
-            if j == 0:
-                copies[2 + 2 * n].wait()
-                copies[3 + 2 * n].wait()
-            upper = jnp.dot(inner, up_ref[:, h : h + step], preferred_element_type=jnp.float32)
-            upper = jax.nn.gelu(upper).astype(jnp.bfloat16)
-            acc = acc + jnp.dot(
-                upper, folded_ref[h : h + step], preferred_element_type=jnp.float32
-            )
-        delta = acc.astype(jnp.bfloat16).astype(jnp.float32)
-        query = query.astype(jnp.float32)
+            upper = upper.reshape(frames, repeat, step) + lifted * lift_ref[here, h : h + step][None]
+            upper = jax.nn.gelu(upper.reshape(side, step)).astype(jnp.bfloat16)
+            part = jnp.dot(upper, down_ref[h : h + step], preferred_element_type=jnp.float32)
+            acc = part if acc is None else acc + part
+        kept = jnp.concatenate(
+            [section, repeated * jnp.concatenate([times] * (width // 128), axis=1)], axis=1
+        )
+        mixed = (kept + acc).astype(jnp.bfloat16)
+        delta = jnp.dot(mixed, tq_ref[...], preferred_element_type=jnp.float32)
+        delta = delta.astype(jnp.bfloat16).astype(jnp.float32)
         for f in range(frames):
             out_ref[f, here] = (query + delta[f * repeat : (f + 1) * repeat]).astype(jnp.bfloat16)
 
 
-def mixer(matched, query, mixes, w_up, folded, w_query, step=256):
-    held = (mixes, w_up, folded, w_query)
+def mixer(matched, query, mixes, w_up, w_down, w_query, step=1024):
+    tokens = matched.shape[0] * matched.shape[1]
     return pl.pallas_call(
         functools.partial(mixer_kernel, step),
         out_shape=jax.ShapeDtypeStruct(matched.shape, jnp.bfloat16),
-        in_specs=[IN_VMEM] * 2 + [IN_HBM] * 4,
+        in_specs=[IN_VMEM] * 6,
         out_specs=IN_VMEM,
-        scratch_shapes=[pltpu.VMEM(array.shape, array.dtype) for array in held]
-        + [pltpu.SemaphoreType.DMA((2 + 2 * (w_up.shape[1] // step),))],
-        compiler_params=params(54),
-        cost_estimate=cost(matched.shape[0] * matched.shape[1] * (w_up.size + folded.size), 2 * w_up.size),
+        scratch_shapes=[pltpu.VMEM((query.shape[0], w_up.shape[1]), jnp.float32)],
+        compiler_params=params(18),
+        cost_estimate=cost(tokens * (w_up.size + w_down.size), 2 * (w_up.size + w_down.size)),
         name="mixer",
-    )(matched, query, mixes, w_up, folded, w_query)
+    )(matched, query, mixes, w_up, w_down, w_query)
 
 
 def ring_pairs(chips, step):
@@ -379,6 +378,7 @@
     chips = lax.axis_size("pts") // 2
     width = feats.shape[2]
     tile, want = begin(feats[0], query_frame.reshape(1, points), query_pos.reshape(1, points))
+    mixes, token = spread_mix(time_mix)
     swap = swap_pairs(chips)
     up, down = ring_pairs(chips, 1), ring_pairs(chips, -1)
     half = chips // 2
@@ -393,7 +393,7 @@
             below = lax.ppermute(below, "pts", up)
             above = lax.ppermute(above, "pts", down) if step + 1 < half else None
         if step == half - 1:
-            picked, *sent = pick(want, aways[done:], tiles[2 * done :], own, sent)
+            picked, *sent = pick(want, aways[done:], tiles[2 * done :], own, sent, (token,))
             own = [picked]
             done = len(aways)
         elif step == half:
@@ -406,10 +406,9 @@
     parts = lax.all_to_all(own[0].reshape(groups, share, width), "tm", 0, 0, tiled=True)
     query_here, copies = join(parts)
     query = lax.all_to_all(copies, "tm", 0, 0, tiled=True).reshape(points, width)
-    mixes, folded = prep(time_mix, w_down, w_query)
     matched = match(query, tiles).reshape(groups, share, width)
     matched = lax.all_to_all(matched, "tm", 0, 0, tiled=True)
-    refined = mixer(matched, query_here, mixes, w_up, folded, w_query)
+    refined = mixer(matched, query_here, mixes, w_up, w_down, w_query)
     refined = lax.all_to_all(refined, "tm", 0, 0, tiled=True).reshape(points, width)
     return rematch(refined, aways, tiles)
 

time: 116 us -> 109 us (0.940)
  blocking collectives: 45.2 us -> 58.2 us
  waiting for transfers between devices: 16.7 us -> 8.53 us
  starting transfers between devices: 19.5 us -> 14.1 us
  Pallas kernels: 28.9 us -> 23.9 us
    all_to_all x0 -> x1, blocking collectives: none -> 13.3 us  [shards(): matched = lax.all_to_all(matched, 'tm', 0, 0, tiled=True)]
    all_to_all x1 -> x0, waiting for transfers between devices: 6.3 us -> none  [shards(): matched = lax.all_to_all(matched, 'tm', 0, 0, tiled=True)]
    all_to_all x1 -> x0, starting transfers between devices: 5.42 us -> none  [shards(): matched = lax.all_to_all(matched, 'tm', 0, 0, tiled=True)]
    pallas_call x1, Pallas kernels: 10.8 us -> 6.46 us  [mixer(): pl.pallas_call(functools.partial(mixer_kernel, step), out_shape=jax.Shape...]
    ppermute x3, waiting for transfers between devices: 8.82 us -> 6.99 us  [shards(): below = lax.ppermute(below, 'pts', up)]
    unnamed x46 -> x14, local copies, waits for them, and re-layouts: 4.08 us -> 3.02 us
  transfers between devices with their start and end apart: 16 -> 15, of which waited for: 6 -> 5; matrix products, arithmetic and copies ran while one was open for 0% -> 0% of each run, Pallas kernels for 3% -> 4%
where the time goes in v4:
time: 109 us
  blocking collectives  58.2 us (53%)
  Pallas kernels  23.9 us (22%)
  starting transfers between devices  14.1 us (13%)
  waiting for transfers between devices  8.53 us (8%)
  local copies, waits for them, and re-layouts  3.02 us (3%)
    all_to_all x1, blocking collectives, shards(): lax.all_to_all(own[0].reshape(groups, share, width), 'tm', 0, 0, tiled=True)  17.6 us
    all_to_all x1, blocking collectives, shards(): lax.all_to_all(copies, 'tm', 0, 0, tiled=True).reshape(points, width)  13.9 us
    all_to_all x1, blocking collectives, shards(): matched = lax.all_to_all(matched, 'tm', 0, 0, tiled=True)  13.3 us
    all_to_all x1, blocking collectives, shards(): lax.all_to_all(refined, 'tm', 0, 0, tiled=True).reshape(points, width)  13.3 us
    pallas_call x1, Pallas kernels, match(): pl.pallas_call(functools.partial(match_kernel, count, block, LOG2E * widt...  7.04 us
    ppermute x3, waiting for transfers between devices, shards(): below = lax.ppermute(below, 'pts', up)  6.99 us
    ppermute x2, starting transfers between devices, shards(): above = lax.ppermute(above, 'pts', down) if step + 1 < half else None  6.47 us
    pallas_call x1, Pallas kernels, mixer(): pl.pallas_call(functools.partial(mixer_kernel, step), out_shape=jax.Shape...  6.46 us
  transfers between devices with their start and end apart: 15, of which 5 were waited for; matrix products, arithmetic and copies ran while one was open for 0% of the time, Pallas kernels for 4%

profile of v4, /device:TPU:8, one launch (start us, length us, event | category | flops | bytes accessed | tf_op | source)
XLA Modules:
  0.0 108.5 jit_solution(864077929069661983)
XLA Ops:
  0.6 2.0 %collective-permute-start = (bf16[256,256]{1,0:T(8,128)(2,1)}, bf16[256,256]{1,0:T(8,128)(2,1)S(1)}, u32[]{:S(2)}, u32[]{:S(2)}) collective-permute-start(bf16[256,256]{1,0:T(8,128)(2,1)} %bitcast.11), channel_id=1, source_target_pairs={{0,2},{1,3},{2,4},{3,5},{4,6},{5,7},{6,8},{7,9},{8,10},{9,11},{10,... | collective-permute-start | bytes 393224 | tf_op jit(solution)/shard_map/ppermute | solution.py:389
  2.6 4.0 %collective-permute-start.6 = (bf16[256,256]{1,0:T(8,128)(2,1)}, bf16[256,256]{1,0:T(8,128)(2,1)S(1)}, u32[]{:S(2)}, u32[]{:S(2)}) collective-permute-start(bf16[256,256]{1,0:T(8,128)(2,1)} %bitcast.12), channel_id=1, source_target_pairs={{0,14},{1,15},{2,0},{3,1},{4,2},{5,3},{6,4},{7,5},{8,6},{9,7},{10,... | collective-permute-start | bytes 393224 | tf_op jit(solution)/shard_map/ppermute | solution.py:389
  6.7 0.9 copy-done
  7.6 0.7 copy-done.1
  8.3 0.7 copy-done.2
  9.4 0.9 collective-permute-done.refs_5_.refs_4_
  10.3 3.2 %collective-permute-start.9 = (bf16[256,256]{1,0:T(8,128)(2,1)S(1)}, bf16[256,256]{1,0:T(8,128)(2,1)S(1)}, u32[]{:S(2)}, u32[]{:S(2)}) collective-permute-start(bf16[256,256]{1,0:T(8,128)(2,1)S(1)} %collective-permute-done.6.refs_3_.refs_2_), channel_id=1, source_target_pairs={{0,14},{1,15},{2,0},{3,1},{4,2},{5,3},{6,4},{7,5},{8,6},{9,7},{10,... | collective-permute-start | bytes 393224 | tf_op jit(solution)/shard_map/ppermute | solution.py:394
  13.5 0.5 collective-permute-start.7
  14.0 2.4 %collective-permute-done.1.refs_9_.refs_8_ = bf16[256,256]{1,0:T(8,128)(2,1)S(1)} collective-permute-done((bf16[256,256]{1,0:T(8,128)(2,1)S(1)}, bf16[256,256]{1,0:T(8,128)(2,1)S(1)}, u32[]{:S(2)}, u32[]{:S(2)}) %collective-permute-start.1) | collective-permute-done | bytes 131104 | tf_op jit(solution)/shard_map/ppermute | solution.py:393
  16.5 3.2 %collective-permute-start.12 = (bf16[256,256]{1,0:T(8,128)(2,1)S(1)}, bf16[256,256]{1,0:T(8,128)(2,1)S(1)}, u32[]{:S(2)}, u32[]{:S(2)}) collective-permute-start(bf16[256,256]{1,0:T(8,128)(2,1)S(1)} %collective-permute-done.9.refs_7_.refs_6_), channel_id=1, source_target_pairs={{0,14},{1,15},{2,0},{3,1},{4,2},{5,3},{6,4},{7,5},{8,6},{9,7},{10,... | collective-permute-start | bytes 393224 | tf_op jit(solution)/shard_map/ppermute | solution.py:394
  20.2 0.7 copy-done.6
  20.9 0.5 spread_mix.1
  21.4 1.2 %collective-permute-done.2.refs_12_ = bf16[256,256]{1,0:T(8,128)(2,1)S(1)} collective-permute-done((bf16[256,256]{1,0:T(8,128)(2,1)S(1)}, bf16[256,256]{1,0:T(8,128)(2,1)S(1)}, u32[]{:S(2)}, u32[]{:S(2)}) %collective-permute-start.2) | collective-permute-done | bytes 131104 | tf_op jit(solution)/shard_map/ppermute | solution.py:393
  22.7 2.2 %pick.3 = (bf16[1024,256]{1,0:T(8,128)(2,1)S(1)}, bf16[256,256]{1,0:T(8,128)(2,1)S(1)}, bf16[256,256]{1,0:T(8,128)(2,1)S(1)}) custom-call(s32[1024,128]{1,0:T(8,128)S(1)} %get-tuple-element.11.refs_0_, bf16[256,256]{1,0:T(8,128)(2,1)S(1)} %get-tuple-element.12.refs_1_.refs_0_, bf16[256,256]{1,0:T(8,128)(2,1)S(1)} %collective-permute-done.5.refs_2_.refs_1_, ...), custom_call_target="tpu_custom_call" | custom-call | flops 1342177280 | bytes 1310720 | tf_op jit(solution)/shard_map/pick/pallas_call | solution.py:103
  25.4 3.4 %collective-permute-done.3.refs_1_.refs_14_ = bf16[256,256]{1,0:T(8,128)(2,1)S(1)} collective-permute-done((bf16[256,256]{1,0:T(8,128)(2,1)S(1)}, bf16[256,256]{1,0:T(8,128)(2,1)S(1)}, u32[]{:S(2)}, u32[]{:S(2)}) %collective-permute-start.3) | collective-permute-done | bytes 131104 | tf_op jit(solution)/shard_map/ppermute | solution.py:393
  28.8 0.7 pick.4.refs_3_
  29.5 0.6 collective-permute-done.4.refs_2_.refs_15_
  30.6 17.6 %all_to_all.20.parts_ref = bf16[16,64,256]{2,1,0:T(8,128)(2,1)S(1)} all-to-all(bf16[16,64,256]{2,1,0:T(8,128)(2,1)S(1)} %bitcast.7), channel_id=1, replica_groups=mesh['tm'=16,'pts'=16] {'tm'}, dimensions={0} | all-to-all | bytes 1048576 | tf_op jit(solution)/shard_map/all_to_all | solution.py:406
  48.3 13.9 %all_to_all.21 = bf16[16,64,256]{2,1,0:T(8,128)(2,1)S(1)} all-to-all(bf16[16,64,256]{2,1,0:T(8,128)(2,1)S(1)} %get-tuple-element.17), channel_id=1, replica_groups=mesh['tm'=16,'pts'=16] {'tm'}, dimensions={0} | all-to-all | bytes 1048576 | tf_op jit(solution)/shard_map/all_to_all | solution.py:408
  62.2 7.0 %match.1 = bf16[1024,256]{1,0:T(8,128)(2,1)S(1)} custom-call(bf16[1024,256]{1,0:T(8,128)(2,1)S(1)} %bitcast.9, bf16[256,256]{1,0:T(8,128)(2,1)S(1)} %get-tuple-element.12.refs_1_.refs_0_, bf16[256,256]{1,0:T(8,128)(2,1)S(1)} %collective-permute-done.5.refs_2_.refs_1_, bf16[256,256]{1,0:T(8,128)(2,1)S(1)} %collective-permute-done.6.refs_3_.refs_2_, ...), custom_call_target="tpu_custom_call" | custom-call | flops 4294967296 | bytes 2097152 | tf_op jit(solution)/shard_map/match/pallas_call | solution.py:179
  69.3 13.3 %all_to_all.22.m_ref = bf16[16,64,256]{2,1,0:T(8,128)(2,1)S(1)} all-to-all(bf16[16,64,256]{2,1,0:T(8,128)(2,1)S(1)} %bitcast.10), channel_id=1, replica_groups=mesh['tm'=16,'pts'=16] {'tm'}, dimensions={0} | all-to-all | bytes 1048576 | tf_op jit(solution)/shard_map/all_to_all | solution.py:410
  82.6 6.5 %mixer.1 = bf16[16,64,256]{2,1,0:T(8,128)(2,1)S(1)} custom-call(bf16[16,64,256]{2,1,0:T(8,128)(2,1)S(1)} %all_to_all.22.m_ref, bf16[64,256]{1,0:T(8,128)(2,1)S(1)} %get-tuple-element.18.q_ref, bf16[2,256,256]{2,1,0:T(8,128)(2,1)S(1)} %get-tuple-element.19.mixes_ref, bf16[512,2048]{1,0:T(8,128)(2,1)S(1)} %copy-done.3, bf16[2048,512]{1,0:T(8,128)(2,1)S(1)} %copy-done.4, ...), custom_call_target="tpu_custom_call" | custom-call | flops 4294967296 | bytes 4194304 | tf_op jit(solution)/shard_map/mixer/pallas_call | solution.py:350
  89.1 13.3 %all_to_all.23 = bf16[16,64,256]{2,1,0:T(8,128)(2,1)S(1)} all-to-all(bf16[16,64,256]{2,1,0:T(8,128)(2,1)S(1)} %mixer.1), channel_id=1, replica_groups=mesh['tm'=16,'pts'=16] {'tm'}, dimensions={0} | all-to-all | bytes 1048576 | tf_op jit(solution)/shard_map/all_to_all | solution.py:412
  102.4 6.1 %rematch.1 = (f32[1,1024]{1,0:T(1,128)}, f32[1,1024]{1,0:T(1,128)}) custom-call(bf16[1024,256]{1,0:T(8,128)(2,1)S(1)} %bitcast.8, bf16[256,256]{1,0:T(8,128)(2,1)S(1)} %get-tuple-element.12.refs_1_.refs_0_, bf16[256,256]{1,0:T(8,128)(2,1)S(1)} %collective-permute-done.5.refs_2_.refs_1_, bf16[256,256]{1,0:T(8,128)(2,1)S(1)} %collective-permute-done.6.refs_3_.refs_2_, ...), custom_call_target="tpu_custom_call" | custom-call | flops 2147483648 | bytes 2097152 | tf_op jit(solution)/shard_map/rematch/pallas_call | solution.py:251
  (33 shorter events, 2.1 us)
Async XLA Ops:
  0.6 9.6 %collective-permute-start = (bf16[256,256]{1,0:T(8,128)(2,1)}, bf16[256,256]{1,0:T(8,128)(2,1)S(1)}, u32[]{:S(2)}, u32[]{:S(2)}) collective-permute-start(bf16[256,256]{1,0:T(8,128)(2,1)} %bitcast.11), channel_id=1, source_target_pairs={{0,2},{1,3},{2,4},{3,5},{4,6},{5,7},{6,8},{7,9},{8,10},{9,11},{10,... | collective-permute-start | bytes 393224 | tf_op jit(solution)/shard_map/ppermute | solution.py:389
  2.6 7.7 %collective-permute-start.6 = (bf16[256,256]{1,0:T(8,128)(2,1)}, bf16[256,256]{1,0:T(8,128)(2,1)S(1)}, u32[]{:S(2)}, u32[]{:S(2)}) collective-permute-start(bf16[256,256]{1,0:T(8,128)(2,1)} %bitcast.12), channel_id=1, source_target_pairs={{0,14},{1,15},{2,0},{3,1},{4,2},{5,3},{6,4},{7,5},{8,6},{9,7},{10,... | collective-permute-start | bytes 393224 | tf_op jit(solution)/shard_map/ppermute | solution.py:389
  6.7 0.9 copy-start
  7.6 0.7 copy-start.1
  8.3 0.7 copy-start.2
  10.3 6.2 %collective-permute-start.1 = (bf16[256,256]{1,0:T(8,128)(2,1)S(1)}, bf16[256,256]{1,0:T(8,128)(2,1)S(1)}, u32[]{:S(2)}, u32[]{:S(2)}) collective-permute-start(bf16[256,256]{1,0:T(8,128)(2,1)S(1)} %collective-permute-done.refs_5_.refs_4_), channel_id=1, source_target_pairs={{0,2},{1,3},{2,4},{3,5},{4,6},{5,7},{6,8},{7,9},{8,10},{9,11},{10,... | collective-permute-start | bytes 393224 | tf_op jit(solution)/shard_map/ppermute | solution.py:393
  10.3 6.2 %collective-permute-start.9 = (bf16[256,256]{1,0:T(8,128)(2,1)S(1)}, bf16[256,256]{1,0:T(8,128)(2,1)S(1)}, u32[]{:S(2)}, u32[]{:S(2)}) collective-permute-start(bf16[256,256]{1,0:T(8,128)(2,1)S(1)} %collective-permute-done.6.refs_3_.refs_2_), channel_id=1, source_target_pairs={{0,14},{1,15},{2,0},{3,1},{4,2},{5,3},{6,4},{7,5},{8,6},{9,7},{10,... | collective-permute-start | bytes 393224 | tf_op jit(solution)/shard_map/ppermute | solution.py:394
  13.5 6.2 %collective-permute-start.5 = (bf16[256,256]{1,0:T(8,128)(2,1)S(1)}, bf16[256,256]{1,0:T(8,128)(2,1)S(1)}, u32[]{:S(2)}, u32[]{:S(2)}) collective-permute-start(bf16[256,256]{1,0:T(8,128)(2,1)S(1)} %get-tuple-element.12.refs_1_.refs_0_), channel_id=1, source_target_pairs={{0,1},{1,0},{2,3},{3,2},{4,5},{5,4},{6,7},{7,6},{8,9},{9,8},{10,11... | collective-permute-start | bytes 393224 | tf_op jit(solution)/shard_map/ppermute | solution.py:385
  13.5 6.2 %collective-permute-start.7 = (bf16[256,256]{1,0:T(8,128)(2,1)S(1)}, bf16[256,256]{1,0:T(8,128)(2,1)S(1)}, u32[]{:S(2)}, u32[]{:S(2)}) collective-permute-start(bf16[256,256]{1,0:T(8,128)(2,1)S(1)} %collective-permute-done.6.refs_3_.refs_2_), channel_id=1, source_target_pairs={{0,1},{1,0},{2,3},{3,2},{4,5},{5,4},{6,7},{7,6},{8,9},{9,8},{10,11... | collective-permute-start | bytes 393224 | tf_op jit(solution)/shard_map/ppermute | solution.py:403
  14.0 8.6 %collective-permute-start.8 = (bf16[256,256]{1,0:T(8,128)(2,1)S(1)}, bf16[256,256]{1,0:T(8,128)(2,1)S(1)}, u32[]{:S(2)}, u32[]{:S(2)}) collective-permute-start(bf16[256,256]{1,0:T(8,128)(2,1)S(1)} %collective-permute-done.refs_5_.refs_4_), channel_id=1, source_target_pairs={{0,1},{1,0},{2,3},{3,2},{4,5},{5,4},{6,7},{7,6},{8,9},{9,8},{10,11... | collective-permute-start | bytes 393224 | tf_op jit(solution)/shard_map/ppermute | solution.py:403
  16.4 6.2 %collective-permute-start.2 = (bf16[256,256]{1,0:T(8,128)(2,1)S(1)}, bf16[256,256]{1,0:T(8,128)(2,1)S(1)}, u32[]{:S(2)}, u32[]{:S(2)}) collective-permute-start(bf16[256,256]{1,0:T(8,128)(2,1)S(1)} %collective-permute-done.1.refs_9_.refs_8_), channel_id=1, source_target_pairs={{0,2},{1,3},{2,4},{3,5},{4,6},{5,7},{6,8},{7,9},{8,10},{9,11},{10,... | collective-permute-start | bytes 393224 | tf_op jit(solution)/shard_map/ppermute | solution.py:393
  16.5 6.2 %collective-permute-start.12 = (bf16[256,256]{1,0:T(8,128)(2,1)S(1)}, bf16[256,256]{1,0:T(8,128)(2,1)S(1)}, u32[]{:S(2)}, u32[]{:S(2)}) collective-permute-start(bf16[256,256]{1,0:T(8,128)(2,1)S(1)} %collective-permute-done.9.refs_7_.refs_6_), channel_id=1, source_target_pairs={{0,14},{1,15},{2,0},{3,1},{4,2},{5,3},{6,4},{7,5},{8,6},{9,7},{10,... | collective-permute-start | bytes 393224 | tf_op jit(solution)/shard_map/ppermute | solution.py:394
  19.7 3.0 %collective-permute-start.10 = (bf16[256,256]{1,0:T(8,128)(2,1)S(1)}, bf16[256,256]{1,0:T(8,128)(2,1)S(1)}, u32[]{:S(2)}, u32[]{:S(2)}) collective-permute-start(bf16[256,256]{1,0:T(8,128)(2,1)S(1)} %collective-permute-done.9.refs_7_.refs_6_), channel_id=1, source_target_pairs={{0,1},{1,0},{2,3},{3,2},{4,5},{5,4},{6,7},{7,6},{8,9},{9,8},{10,11... | collective-permute-start | bytes 393224 | tf_op jit(solution)/shard_map/ppermute | solution.py:403
  19.7 3.0 %collective-permute-start.11 = (bf16[256,256]{1,0:T(8,128)(2,1)S(1)}, bf16[256,256]{1,0:T(8,128)(2,1)S(1)}, u32[]{:S(2)}, u32[]{:S(2)}) collective-permute-start(bf16[256,256]{1,0:T(8,128)(2,1)S(1)} %collective-permute-done.1.refs_9_.refs_8_), channel_id=1, source_target_pairs={{0,1},{1,0},{2,3},{3,2},{4,5},{5,4},{6,7},{7,6},{8,9},{9,8},{10,11... | collective-permute-start | bytes 393224 | tf_op jit(solution)/shard_map/ppermute | solution.py:403
  20.2 0.7 copy-start.6
  22.6 6.2 %collective-permute-start.3 = (bf16[256,256]{1,0:T(8,128)(2,1)S(1)}, bf16[256,256]{1,0:T(8,128)(2,1)S(1)}, u32[]{:S(2)}, u32[]{:S(2)}) collective-permute-start(bf16[256,256]{1,0:T(8,128)(2,1)S(1)} %collective-permute-done.2.refs_12_), channel_id=1, source_target_pairs={{0,2},{1,3},{2,4},{3,5},{4,6},{5,7},{6,8},{7,9},{8,10},{9,11},{10,... | collective-permute-start | bytes 393224 | tf_op jit(solution)/shard_map/ppermute | solution.py:393
  24.8 4.0 %collective-permute-start.13 = (bf16[256,256]{1,0:T(8,128)(2,1)S(1)}, bf16[256,256]{1,0:T(8,128)(2,1)S(1)}, u32[]{:S(2)}, u32[]{:S(2)}) collective-permute-start(bf16[256,256]{1,0:T(8,128)(2,1)S(1)} %get-tuple-element.14.refs_1_.refs_10_), channel_id=1, source_target_pairs={{0,1},{1,0},{2,3},{3,2},{4,5},{5,4},{6,7},{7,6},{8,9},{9,8},{10,11... | collective-permute-start | bytes 393224 | tf_op jit(solution)/shard_map/ppermute | solution.py:403
  24.9 3.9 %collective-permute-start.14 = (bf16[256,256]{1,0:T(8,128)(2,1)S(1)}, bf16[256,256]{1,0:T(8,128)(2,1)S(1)}, u32[]{:S(2)}, u32[]{:S(2)}) collective-permute-start(bf16[256,256]{1,0:T(8,128)(2,1)S(1)} %get-tuple-element.15.refs_3_.refs_12_), channel_id=1, source_target_pairs={{0,1},{1,0},{2,3},{3,2},{4,5},{5,4},{6,7},{7,6},{8,9},{9,8},{10,11... | collective-permute-start | bytes 393224 | tf_op jit(solution)/shard_map/ppermute | solution.py:403
  28.8 1.3 %collective-permute-start.4 = (bf16[256,256]{1,0:T(8,128)(2,1)S(1)}, bf16[256,256]{1,0:T(8,128)(2,1)S(1)}, u32[]{:S(2)}, u32[]{:S(2)}) collective-permute-start(bf16[256,256]{1,0:T(8,128)(2,1)S(1)} %collective-permute-done.3.refs_1_.refs_14_), channel_id=1, source_target_pairs={{0,1},{1,0},{2,3},{3,2},{4,5},{5,4},{6,7},{7,6},{8,9},{9,8},{10,11... | collective-permute-start | bytes 393224 | tf_op jit(solution)/shard_map/ppermute | solution.py:403
  62.2 20.4 %copy-start.3 = (bf16[512,2048]{1,0:T(8,128)(2,1)S(1)}, bf16[512,2048]{1,0:T(8,128)(2,1)}, u32[]{:S(2)}) copy-start(bf16[512,2048]{1,0:T(8,128)(2,1)} %up_ref.1) | copy-start | bytes 6291460
  62.2 20.4 %copy-start.4 = (bf16[2048,512]{1,0:T(8,128)(2,1)S(1)}, bf16[2048,512]{1,0:T(8,128)(2,1)}, u32[]{:S(2)}) copy-start(bf16[2048,512]{1,0:T(8,128)(2,1)} %down_ref.1) | copy-start | bytes 6291460
  62.2 20.4 %copy-start.5 = (bf16[512,256]{1,0:T(8,128)(2,1)S(1)}, bf16[512,256]{1,0:T(8,128)(2,1)}, u32[]{:S(2)}) copy-start(bf16[512,256]{1,0:T(8,128)(2,1)} %tq_ref.1) | copy-start | bytes 786436

commit v5 on v4

--- a/solution.py
+++ b/solution.py
@@ -23,14 +23,14 @@
     return pl.CostEstimate(flops=2 * macs, bytes_accessed=nbytes, transcendentals=0)
 
 
-def tile_bases(aways, rows):
+def tile_bases(marks, rows):
     chips = lax.axis_size("pts") // 2
     place = lax.axis_index("pts")
     core = lax.rem(place, 2)
     bases = []
-    for away in aways:
+    for away, other in marks:
         chip = lax.rem(place // 2 + (away + chips) % chips, chips)
-        bases += [(chip * 2 + core) * rows, (chip * 2 + 1 - core) * rows]
+        bases.append((chip * 2 + (1 - core if other else core)) * rows)
     return bases
 
 
@@ -67,15 +67,15 @@
     )(tile, query_frame, query_pos)
 
 
-def pick_kernel(aways, given, sent, want_ref, *refs):
-    count = 2 * len(aways)
+def pick_kernel(marks, given, sent, want_ref, *refs):
+    count = len(marks)
     tiles, refs = refs[:count], refs[count:]
     before, refs = refs[:given], refs[given:]
     sources, out, targets = refs[:sent], refs[-1 - sent], refs[len(refs) - sent :]
     want = want_ref[...]
     lane = lax.broadcasted_iota(jnp.int32, (1, 128), 1)
     total = None
-    for tile, base in zip(tiles, tile_bases(aways, tiles[0].shape[0])):
+    for tile, base in zip(tiles, tile_bases(marks, tiles[0].shape[0])):
         hot = jnp.concatenate(
             [
                 (want == lane + (base + first)).astype(jnp.float32).astype(jnp.bfloat16)
@@ -92,13 +92,13 @@
         target[...] = source[...]
 
 
-def pick(want, aways, tiles, before=(), sent=(), after=()):
+def pick(want, marks, tiles, before=(), sent=(), after=()):
     points, width = want.shape[0], tiles[0].shape[1]
     count = len(tiles)
 
     def kernel(*refs):
         ahead = 1 + count + len(before) + len(sent)
-        pick_kernel(aways, len(before), len(sent), *refs[:ahead], *refs[ahead + len(after) :])
+        pick_kernel(marks, len(before), len(sent), *refs[:ahead], *refs[ahead + len(after) :])
 
     return pl.pallas_call(
         kernel,
@@ -188,22 +188,25 @@
     )(query, *tiles)
 
 
-def rematch_kernel(aways, block, factor, q_ref, *refs):
+def rematch_kernel(marks, block, factor, q_ref, *refs):
     tiles, out_x, out_y = refs[:-2], refs[-2], refs[-1]
     count = len(tiles)
     rows = tiles[0].shape[0]
-    bases = tile_bases(aways, rows)
+    bases = tile_bases(marks, rows)
     sub = lax.broadcasted_iota(jnp.int32, (8, 1), 0)
     columns = [(2 * (sub + at) + 1).astype(jnp.float32) / GRID - 1.0 for at in range(0, GRID, 8)]
-    work = [(i, t) for i in range(q_ref.shape[0] // block) for t in range(count)]
+    work = [(i, t) for i in range(q_ref.shape[0] // block) for t in range(0, count, 2)]
 
     def score(i, t):
-        return lax.dot_general(
-            tiles[t][...],
-            q_ref[i * block : (i + 1) * block],
-            NT,
-            preferred_element_type=jnp.float32,
-        ).reshape(rows // 8, 8, block)
+        return [
+            lax.dot_general(
+                tile[...],
+                q_ref[i * block : (i + 1) * block],
+                NT,
+                preferred_element_type=jnp.float32,
+            ).reshape(rows // 8, 8, block)
+            for tile in tiles[t : t + 2]
+        ]
 
     ahead = score(*work[0])
     for n, (i, t) in enumerate(work):
@@ -214,7 +217,7 @@
             top = None
             sums = [None] * len(columns)
             sum_y = jnp.zeros((8, block), jnp.float32)
-        high = jnp.max(s, axis=0)
+        high = jnp.maximum(jnp.max(s[0], axis=0), jnp.max(s[1], axis=0))
         if top is not None:
             high = jnp.maximum(high, top)
             shrink = jnp.exp2((top - high) * factor)
@@ -222,16 +225,16 @@
             sums = [value * shrink for value in sums]
         top = high
         high = high * factor
-        first = bases[t] // GRID
-        for line in range(rows // GRID):
-            y = (2 * (first + line) + 1).astype(jnp.float32) / GRID - 1.0
-            here = None
-            for c in range(len(columns)):
-                expo = jnp.exp2(s[line * len(columns) + c] * factor - high)
-                sums[c] = expo if sums[c] is None else sums[c] + expo
-                here = expo if here is None else here + expo
-            sum_y = sum_y + here * y
-        if t == count - 1:
+        for piece, base in zip(s, bases[t : t + 2]):
+            for line in range(rows // GRID):
+                y = (2 * (base // GRID + line) + 1).astype(jnp.float32) / GRID - 1.0
+                here = None
+                for c in range(len(columns)):
+                    expo = jnp.exp2(piece[line * len(columns) + c] * factor - high)
+                    sums[c] = expo if sums[c] is None else sums[c] + expo
+                    here = expo if here is None else here + expo
+                sum_y = sum_y + here * y
+        if t == count - 2:
             total = sums[0]
             sum_x = sums[0] * columns[0]
             for value, x in zip(sums[1:], columns[1:]):
@@ -244,12 +247,12 @@
             out_y[:, here] = jnp.sum(sum_y * weight, axis=0, keepdims=True) / total
 
 
-def rematch(refined, aways, tiles, block=256):
+def rematch(refined, marks, tiles, block=256):
     points, width = refined.shape
     count = len(tiles)
     places = count * tiles[0].shape[0]
     return pl.pallas_call(
-        functools.partial(rematch_kernel, aways, block, LOG2E * width**-0.5),
+        functools.partial(rematch_kernel, marks, block, LOG2E * width**-0.5),
         out_shape=[jax.ShapeDtypeStruct((1, points), jnp.float32)] * 2,
         in_specs=[IN_VMEM] * (1 + count),
         out_specs=[IN_VMEM] * 2,
@@ -382,27 +385,40 @@
     swap = swap_pairs(chips)
     up, down = ring_pairs(chips, 1), ring_pairs(chips, -1)
     half = chips // 2
-    tiles = [tile, lax.ppermute(tile, "pts", swap)]
-    aways = [0]
+    tiles = []
+    marks = []
     own = []
     done = 0
+
+    def hold(piece, away, other):
+        tiles.append(piece)
+        marks.append((away, other))
+
+    def swapped(piece):
+        return lax.ppermute(piece, "pts", swap)
+
+    hold(tile, 0, False)
+    hold(swapped(tile), 0, True)
     below, above = lax.ppermute(feats[0], "pts", up), lax.ppermute(feats[0], "pts", down)
-    for step in range(1, half + 1):
-        sent = [above, below] if step < half else [below]
-        if step < half:
-            below = lax.ppermute(below, "pts", up)
-            above = lax.ppermute(above, "pts", down) if step + 1 < half else None
+    for step in range(1, half):
+        arrived = [(above, step), (below, -step)]
+        below = lax.ppermute(below, "pts", up)
+        if step + 1 < half:
+            above = lax.ppermute(above, "pts", down)
+        for piece, away in arrived:
+            hold(piece, away, False)
+        sent = [piece for piece, _ in arrived]
         if step == half - 1:
-            picked, *sent = pick(want, aways[done:], tiles[2 * done :], own, sent, (token,))
+            picked, *sent = pick(want, marks, tiles, own, sent, (token,))
             own = [picked]
-            done = len(aways)
-        elif step == half:
-            own = pick(want, aways[done:], tiles[2 * done :], own)
-            done = len(aways)
-        for piece in sent:
-            tiles += [piece, lax.ppermute(piece, "pts", swap)]
-        aways += [step, -step] if step < half else [-step]
-    own = pick(want, aways[done:], tiles[2 * done :], own)
+            done = len(tiles)
+        for piece, (_, away) in zip(sent, arrived):
+            hold(swapped(piece), away, True)
+    hold(below, -half, False)
+    last = swapped(below)
+    own = pick(want, marks[done:], tiles[done:], own)
+    hold(last, -half, True)
+    own = pick(want, marks[-1:], tiles[-1:], own)
     parts = lax.all_to_all(own[0].reshape(groups, share, width), "tm", 0, 0, tiled=True)
     query_here, copies = join(parts)
     query = lax.all_to_all(copies, "tm", 0, 0, tiled=True).reshape(points, width)
@@ -410,7 +426,7 @@
     matched = lax.all_to_all(matched, "tm", 0, 0, tiled=True)
     refined = mixer(matched, query_here, mixes, w_up, w_down, w_query)
     refined = lax.all_to_all(refined, "tm", 0, 0, tiled=True).reshape(points, width)
-    return rematch(refined, aways, tiles)
+    return rematch(refined, marks, tiles)
 
 
 def solution(mesh):

time: 109 us -> 109 us (level)
  no operation moved by 1% of the time
where the time goes in v5:
time: 109 us
  blocking collectives  58.2 us (53%)
  Pallas kernels  24 us (22%)
  starting transfers between devices  14.1 us (13%)
  waiting for transfers between devices  8.39 us (8%)
  local copies, waits for them, and re-layouts  3.02 us (3%)
    all_to_all x1, blocking collectives, shards(): lax.all_to_all(own[0].reshape(groups, share, width), 'tm', 0, 0, tiled=True)  17.6 us
    all_to_all x1, blocking collectives, shards(): lax.all_to_all(copies, 'tm', 0, 0, tiled=True).reshape(points, width)  13.9 us
    all_to_all x1, blocking collectives, shards(): matched = lax.all_to_all(matched, 'tm', 0, 0, tiled=True)  13.3 us
    all_to_all x1, blocking collectives, shards(): lax.all_to_all(refined, 'tm', 0, 0, tiled=True).reshape(points, width)  13.3 us
    pallas_call x1, Pallas kernels, match(): pl.pallas_call(functools.partial(match_kernel, count, block, LOG2E * widt...  7.04 us
    ppermute x3, waiting for transfers between devices, shards(): below = lax.ppermute(below, 'pts', up)  6.71 us
    ppermute x2, starting transfers between devices, shards(): above = lax.ppermute(above, 'pts', down)  6.47 us
    pallas_call x1, Pallas kernels, mixer(): pl.pallas_call(functools.partial(mixer_kernel, step), out_shape=jax.Shape...  6.46 us
  transfers between devices with their start and end apart: 15, of which 5 were waited for; matrix products, arithmetic and copies ran while one was open for 0% of the time, Pallas kernels for 4%

profile of v5, /device:TPU:8, one launch (start us, length us, event | category | flops | bytes accessed | tf_op | source)
XLA Modules:
  0.0 108.5 jit_solution(1132979654951353859)
XLA Ops:
  0.6 2.0 %collective-permute-start = (bf16[256,256]{1,0:T(8,128)(2,1)}, bf16[256,256]{1,0:T(8,128)(2,1)S(1)}, u32[]{:S(2)}, u32[]{:S(2)}) collective-permute-start(bf16[256,256]{1,0:T(8,128)(2,1)} %bitcast.11), channel_id=1, source_target_pairs={{0,2},{1,3},{2,4},{3,5},{4,6},{5,7},{6,8},{7,9},{8,10},{9,11},{10,... | collective-permute-start | bytes 393224 | tf_op jit(solution)/shard_map/ppermute | solution.py:402
  2.6 4.0 %collective-permute-start.6 = (bf16[256,256]{1,0:T(8,128)(2,1)}, bf16[256,256]{1,0:T(8,128)(2,1)S(1)}, u32[]{:S(2)}, u32[]{:S(2)}) collective-permute-start(bf16[256,256]{1,0:T(8,128)(2,1)} %bitcast.12), channel_id=1, source_target_pairs={{0,14},{1,15},{2,0},{3,1},{4,2},{5,3},{6,4},{7,5},{8,6},{9,7},{10,... | collective-permute-start | bytes 393224 | tf_op jit(solution)/shard_map/ppermute | solution.py:402
  6.7 0.9 copy-done
  7.6 0.7 copy-done.1
  8.3 0.7 copy-done.2
  9.4 0.9 collective-permute-done.refs_4_.refs_3_
  10.3 3.2 %collective-permute-start.9 = (bf16[256,256]{1,0:T(8,128)(2,1)S(1)}, bf16[256,256]{1,0:T(8,128)(2,1)S(1)}, u32[]{:S(2)}, u32[]{:S(2)}) collective-permute-start(bf16[256,256]{1,0:T(8,128)(2,1)S(1)} %collective-permute-done.6.refs_3_.refs_2_), channel_id=1, source_target_pairs={{0,14},{1,15},{2,0},{3,1},{4,2},{5,3},{6,4},{7,5},{8,6},{9,7},{10,... | collective-permute-start | bytes 393224 | tf_op jit(solution)/shard_map/ppermute | solution.py:407
  13.5 0.5 collective-permute-start.7
  14.0 2.4 %collective-permute-done.1.refs_8_.refs_7_ = bf16[256,256]{1,0:T(8,128)(2,1)S(1)} collective-permute-done((bf16[256,256]{1,0:T(8,128)(2,1)S(1)}, bf16[256,256]{1,0:T(8,128)(2,1)S(1)}, u32[]{:S(2)}, u32[]{:S(2)}) %collective-permute-start.1) | collective-permute-done | bytes 131104 | tf_op jit(solution)/shard_map/ppermute | solution.py:405
  16.5 3.2 %collective-permute-start.12 = (bf16[256,256]{1,0:T(8,128)(2,1)S(1)}, bf16[256,256]{1,0:T(8,128)(2,1)S(1)}, u32[]{:S(2)}, u32[]{:S(2)}) collective-permute-start(bf16[256,256]{1,0:T(8,128)(2,1)S(1)} %collective-permute-done.9.refs_7_.refs_6_), channel_id=1, source_target_pairs={{0,14},{1,15},{2,0},{3,1},{4,2},{5,3},{6,4},{7,5},{8,6},{9,7},{10,... | collective-permute-start | bytes 393224 | tf_op jit(solution)/shard_map/ppermute | solution.py:407
  20.2 0.7 copy-done.6
  20.9 0.5 spread_mix.1
  21.4 1.2 %collective-permute-done.2.refs_12_.refs_14_.refs_11_ = bf16[256,256]{1,0:T(8,128)(2,1)S(1)} collective-permute-done((bf16[256,256]{1,0:T(8,128)(2,1)S(1)}, bf16[256,256]{1,0:T(8,128)(2,1)S(1)}, u32[]{:S(2)}, u32[]{:S(2)}) %collective-permute-start.2) | collective-permute-done | bytes 131104 | tf_op jit(solution)/shard_map/ppermute | solution.py:405
  22.7 2.4 %pick.3 = (bf16[1024,256]{1,0:T(8,128)(2,1)S(1)}, bf16[256,256]{1,0:T(8,128)(2,1)S(1)}, bf16[256,256]{1,0:T(8,128)(2,1)S(1)}) custom-call(s32[1024,128]{1,0:T(8,128)S(1)} %get-tuple-element.11.refs_0_, bf16[256,256]{1,0:T(8,128)(2,1)S(1)} %get-tuple-element.12.refs_1_.refs_0_, bf16[256,256]{1,0:T(8,128)(2,1)S(1)} %collective-permute-done.5.refs_2_.refs_1_, ...), custom_call_target="tpu_custom_call" | custom-call | flops 1610612736 | bytes 1572864 | tf_op jit(solution)/shard_map/pick/pallas_call | solution.py:103
  25.7 3.1 %collective-permute-done.3.refs_3_.refs_14_ = bf16[256,256]{1,0:T(8,128)(2,1)S(1)} collective-permute-done((bf16[256,256]{1,0:T(8,128)(2,1)S(1)}, bf16[256,256]{1,0:T(8,128)(2,1)S(1)}, u32[]{:S(2)}, u32[]{:S(2)}) %collective-permute-start.3) | collective-permute-done | bytes 131104 | tf_op jit(solution)/shard_map/ppermute | solution.py:405
  28.8 0.6 pick.4.refs_2_
  29.4 0.7 collective-permute-done.4.refs_1_.refs_15_
  30.5 17.6 %all_to_all.20.parts_ref = bf16[16,64,256]{2,1,0:T(8,128)(2,1)S(1)} all-to-all(bf16[16,64,256]{2,1,0:T(8,128)(2,1)S(1)} %bitcast.7), channel_id=1, replica_groups=mesh['tm'=16,'pts'=16] {'tm'}, dimensions={0} | all-to-all | bytes 1048576 | tf_op jit(solution)/shard_map/all_to_all | solution.py:422
  48.2 13.9 %all_to_all.21 = bf16[16,64,256]{2,1,0:T(8,128)(2,1)S(1)} all-to-all(bf16[16,64,256]{2,1,0:T(8,128)(2,1)S(1)} %get-tuple-element.17), channel_id=1, replica_groups=mesh['tm'=16,'pts'=16] {'tm'}, dimensions={0} | all-to-all | bytes 1048576 | tf_op jit(solution)/shard_map/all_to_all | solution.py:424
  62.1 7.0 %match.1 = bf16[1024,256]{1,0:T(8,128)(2,1)S(1)} custom-call(bf16[1024,256]{1,0:T(8,128)(2,1)S(1)} %bitcast.9, bf16[256,256]{1,0:T(8,128)(2,1)S(1)} %get-tuple-element.12.refs_1_.refs_0_, bf16[256,256]{1,0:T(8,128)(2,1)S(1)} %collective-permute-done.5.refs_2_.refs_1_, bf16[256,256]{1,0:T(8,128)(2,1)S(1)} %collective-permute-done.6.refs_3_.refs_2_, ...), custom_call_target="tpu_custom_call" | custom-call | flops 4294967296 | bytes 2097152 | tf_op jit(solution)/shard_map/match/pallas_call | solution.py:179
  69.1 13.3 %all_to_all.22.m_ref = bf16[16,64,256]{2,1,0:T(8,128)(2,1)S(1)} all-to-all(bf16[16,64,256]{2,1,0:T(8,128)(2,1)S(1)} %bitcast.10), channel_id=1, replica_groups=mesh['tm'=16,'pts'=16] {'tm'}, dimensions={0} | all-to-all | bytes 1048576 | tf_op jit(solution)/shard_map/all_to_all | solution.py:426
  82.5 6.5 %mixer.1 = bf16[16,64,256]{2,1,0:T(8,128)(2,1)S(1)} custom-call(bf16[16,64,256]{2,1,0:T(8,128)(2,1)S(1)} %all_to_all.22.m_ref, bf16[64,256]{1,0:T(8,128)(2,1)S(1)} %get-tuple-element.18.q_ref, bf16[2,256,256]{2,1,0:T(8,128)(2,1)S(1)} %get-tuple-element.19.mixes_ref, bf16[512,2048]{1,0:T(8,128)(2,1)S(1)} %copy-done.3, bf16[2048,512]{1,0:T(8,128)(2,1)S(1)} %copy-done.4, ...), custom_call_target="tpu_custom_call" | custom-call | flops 4294967296 | bytes 4194304 | tf_op jit(solution)/shard_map/mixer/pallas_call | solution.py:353
  89.0 13.3 %all_to_all.23 = bf16[16,64,256]{2,1,0:T(8,128)(2,1)S(1)} all-to-all(bf16[16,64,256]{2,1,0:T(8,128)(2,1)S(1)} %mixer.1), channel_id=1, replica_groups=mesh['tm'=16,'pts'=16] {'tm'}, dimensions={0} | all-to-all | bytes 1048576 | tf_op jit(solution)/shard_map/all_to_all | solution.py:428
  102.3 6.2 %rematch.1 = (f32[1,1024]{1,0:T(1,128)}, f32[1,1024]{1,0:T(1,128)}) custom-call(bf16[1024,256]{1,0:T(8,128)(2,1)S(1)} %bitcast.8, bf16[256,256]{1,0:T(8,128)(2,1)S(1)} %get-tuple-element.12.refs_1_.refs_0_, bf16[256,256]{1,0:T(8,128)(2,1)S(1)} %collective-permute-done.5.refs_2_.refs_1_, bf16[256,256]{1,0:T(8,128)(2,1)S(1)} %collective-permute-done.6.refs_3_.refs_2_, ...), custom_call_target="tpu_custom_call" | custom-call | flops 2147483648 | bytes 2097152 | tf_op jit(solution)/shard_map/rematch/pallas_call | solution.py:254
  (33 shorter events, 1.9 us)
Async XLA Ops:
  0.6 9.6 %collective-permute-start = (bf16[256,256]{1,0:T(8,128)(2,1)}, bf16[256,256]{1,0:T(8,128)(2,1)S(1)}, u32[]{:S(2)}, u32[]{:S(2)}) collective-permute-start(bf16[256,256]{1,0:T(8,128)(2,1)} %bitcast.11), channel_id=1, source_target_pairs={{0,2},{1,3},{2,4},{3,5},{4,6},{5,7},{6,8},{7,9},{8,10},{9,11},{10,... | collective-permute-start | bytes 393224 | tf_op jit(solution)/shard_map/ppermute | solution.py:402
  2.6 7.7 %collective-permute-start.6 = (bf16[256,256]{1,0:T(8,128)(2,1)}, bf16[256,256]{1,0:T(8,128)(2,1)S(1)}, u32[]{:S(2)}, u32[]{:S(2)}) collective-permute-start(bf16[256,256]{1,0:T(8,128)(2,1)} %bitcast.12), channel_id=1, source_target_pairs={{0,14},{1,15},{2,0},{3,1},{4,2},{5,3},{6,4},{7,5},{8,6},{9,7},{10,... | collective-permute-start | bytes 393224 | tf_op jit(solution)/shard_map/ppermute | solution.py:402
  6.7 0.9 copy-start
  7.6 0.7 copy-start.1
  8.3 0.7 copy-start.2
  10.3 6.2 %collective-permute-start.1 = (bf16[256,256]{1,0:T(8,128)(2,1)S(1)}, bf16[256,256]{1,0:T(8,128)(2,1)S(1)}, u32[]{:S(2)}, u32[]{:S(2)}) collective-permute-start(bf16[256,256]{1,0:T(8,128)(2,1)S(1)} %collective-permute-done.refs_4_.refs_3_), channel_id=1, source_target_pairs={{0,2},{1,3},{2,4},{3,5},{4,6},{5,7},{6,8},{7,9},{8,10},{9,11},{10,... | collective-permute-start | bytes 393224 | tf_op jit(solution)/shard_map/ppermute | solution.py:405
  10.3 6.2 %collective-permute-start.9 = (bf16[256,256]{1,0:T(8,128)(2,1)S(1)}, bf16[256,256]{1,0:T(8,128)(2,1)S(1)}, u32[]{:S(2)}, u32[]{:S(2)}) collective-permute-start(bf16[256,256]{1,0:T(8,128)(2,1)S(1)} %collective-permute-done.6.refs_3_.refs_2_), channel_id=1, source_target_pairs={{0,14},{1,15},{2,0},{3,1},{4,2},{5,3},{6,4},{7,5},{8,6},{9,7},{10,... | collective-permute-start | bytes 393224 | tf_op jit(solution)/shard_map/ppermute | solution.py:407
  13.5 6.2 %collective-permute-start.5 = (bf16[256,256]{1,0:T(8,128)(2,1)S(1)}, bf16[256,256]{1,0:T(8,128)(2,1)S(1)}, u32[]{:S(2)}, u32[]{:S(2)}) collective-permute-start(bf16[256,256]{1,0:T(8,128)(2,1)S(1)} %get-tuple-element.12.refs_1_.refs_0_), channel_id=1, source_target_pairs={{0,1},{1,0},{2,3},{3,2},{4,5},{5,4},{6,7},{7,6},{8,9},{9,8},{10,11... | collective-permute-start | bytes 393224 | tf_op jit(solution)/shard_map/ppermute | solution.py:398
  13.5 6.2 %collective-permute-start.7 = (bf16[256,256]{1,0:T(8,128)(2,1)S(1)}, bf16[256,256]{1,0:T(8,128)(2,1)S(1)}, u32[]{:S(2)}, u32[]{:S(2)}) collective-permute-start(bf16[256,256]{1,0:T(8,128)(2,1)S(1)} %collective-permute-done.6.refs_3_.refs_2_), channel_id=1, source_target_pairs={{0,1},{1,0},{2,3},{3,2},{4,5},{5,4},{6,7},{7,6},{8,9},{9,8},{10,11... | collective-permute-start | bytes 393224 | tf_op jit(solution)/shard_map/ppermute | solution.py:398
  14.0 8.6 %collective-permute-start.8 = (bf16[256,256]{1,0:T(8,128)(2,1)S(1)}, bf16[256,256]{1,0:T(8,128)(2,1)S(1)}, u32[]{:S(2)}, u32[]{:S(2)}) collective-permute-start(bf16[256,256]{1,0:T(8,128)(2,1)S(1)} %collective-permute-done.refs_4_.refs_3_), channel_id=1, source_target_pairs={{0,1},{1,0},{2,3},{3,2},{4,5},{5,4},{6,7},{7,6},{8,9},{9,8},{10,11... | collective-permute-start | bytes 393224 | tf_op jit(solution)/shard_map/ppermute | solution.py:398
  16.4 6.2 %collective-permute-start.2 = (bf16[256,256]{1,0:T(8,128)(2,1)S(1)}, bf16[256,256]{1,0:T(8,128)(2,1)S(1)}, u32[]{:S(2)}, u32[]{:S(2)}) collective-permute-start(bf16[256,256]{1,0:T(8,128)(2,1)S(1)} %collective-permute-done.1.refs_8_.refs_7_), channel_id=1, source_target_pairs={{0,2},{1,3},{2,4},{3,5},{4,6},{5,7},{6,8},{7,9},{8,10},{9,11},{10,... | collective-permute-start | bytes 393224 | tf_op jit(solution)/shard_map/ppermute | solution.py:405
  16.5 6.2 %collective-permute-start.12 = (bf16[256,256]{1,0:T(8,128)(2,1)S(1)}, bf16[256,256]{1,0:T(8,128)(2,1)S(1)}, u32[]{:S(2)}, u32[]{:S(2)}) collective-permute-start(bf16[256,256]{1,0:T(8,128)(2,1)S(1)} %collective-permute-done.9.refs_7_.refs_6_), channel_id=1, source_target_pairs={{0,14},{1,15},{2,0},{3,1},{4,2},{5,3},{6,4},{7,5},{8,6},{9,7},{10,... | collective-permute-start | bytes 393224 | tf_op jit(solution)/shard_map/ppermute | solution.py:407
  19.7 3.0 %collective-permute-start.10 = (bf16[256,256]{1,0:T(8,128)(2,1)S(1)}, bf16[256,256]{1,0:T(8,128)(2,1)S(1)}, u32[]{:S(2)}, u32[]{:S(2)}) collective-permute-start(bf16[256,256]{1,0:T(8,128)(2,1)S(1)} %collective-permute-done.9.refs_7_.refs_6_), channel_id=1, source_target_pairs={{0,1},{1,0},{2,3},{3,2},{4,5},{5,4},{6,7},{7,6},{8,9},{9,8},{10,11... | collective-permute-start | bytes 393224 | tf_op jit(solution)/shard_map/ppermute | solution.py:398
  19.7 3.0 %collective-permute-start.11 = (bf16[256,256]{1,0:T(8,128)(2,1)S(1)}, bf16[256,256]{1,0:T(8,128)(2,1)S(1)}, u32[]{:S(2)}, u32[]{:S(2)}) collective-permute-start(bf16[256,256]{1,0:T(8,128)(2,1)S(1)} %collective-permute-done.1.refs_8_.refs_7_), channel_id=1, source_target_pairs={{0,1},{1,0},{2,3},{3,2},{4,5},{5,4},{6,7},{7,6},{8,9},{9,8},{10,11... | collective-permute-start | bytes 393224 | tf_op jit(solution)/shard_map/ppermute | solution.py:398
  20.2 0.7 copy-start.6
  22.6 6.2 %collective-permute-start.3 = (bf16[256,256]{1,0:T(8,128)(2,1)S(1)}, bf16[256,256]{1,0:T(8,128)(2,1)S(1)}, u32[]{:S(2)}, u32[]{:S(2)}) collective-permute-start(bf16[256,256]{1,0:T(8,128)(2,1)S(1)} %collective-permute-done.2.refs_12_.refs_14_.refs_11_), channel_id=1, source_target_pairs={{0,2},{1,3},{2,4},{3,5},{4,6},{5,7},{6,8},{7,9},{8,10},{9,11},{10,... | collective-permute-start | bytes 393224 | tf_op jit(solution)/shard_map/ppermute | solution.py:405
  25.1 3.7 %collective-permute-start.13 = (bf16[256,256]{1,0:T(8,128)(2,1)S(1)}, bf16[256,256]{1,0:T(8,128)(2,1)S(1)}, u32[]{:S(2)}, u32[]{:S(2)}) collective-permute-start(bf16[256,256]{1,0:T(8,128)(2,1)S(1)} %get-tuple-element.14), channel_id=1, source_target_pairs={{0,1},{1,0},{2,3},{3,2},{4,5},{5,4},{6,7},{7,6},{8,9},{9,8},{10,11... | collective-permute-start | bytes 393224 | tf_op jit(solution)/shard_map/ppermute | solution.py:398
  25.2 3.6 %collective-permute-start.14 = (bf16[256,256]{1,0:T(8,128)(2,1)S(1)}, bf16[256,256]{1,0:T(8,128)(2,1)S(1)}, u32[]{:S(2)}, u32[]{:S(2)}) collective-permute-start(bf16[256,256]{1,0:T(8,128)(2,1)S(1)} %get-tuple-element.15), channel_id=1, source_target_pairs={{0,1},{1,0},{2,3},{3,2},{4,5},{5,4},{6,7},{7,6},{8,9},{9,8},{10,11... | collective-permute-start | bytes 393224 | tf_op jit(solution)/shard_map/ppermute | solution.py:398
  28.8 1.3 %collective-permute-start.4 = (bf16[256,256]{1,0:T(8,128)(2,1)S(1)}, bf16[256,256]{1,0:T(8,128)(2,1)S(1)}, u32[]{:S(2)}, u32[]{:S(2)}) collective-permute-start(bf16[256,256]{1,0:T(8,128)(2,1)S(1)} %collective-permute-done.3.refs_3_.refs_14_), channel_id=1, source_target_pairs={{0,1},{1,0},{2,3},{3,2},{4,5},{5,4},{6,7},{7,6},{8,9},{9,8},{10,11... | collective-permute-start | bytes 393224 | tf_op jit(solution)/shard_map/ppermute | solution.py:398
  62.1 20.4 %copy-start.3 = (bf16[512,2048]{1,0:T(8,128)(2,1)S(1)}, bf16[512,2048]{1,0:T(8,128)(2,1)}, u32[]{:S(2)}) copy-start(bf16[512,2048]{1,0:T(8,128)(2,1)} %up_ref.1) | copy-start | bytes 6291460
  62.1 20.4 %copy-start.4 = (bf16[2048,512]{1,0:T(8,128)(2,1)S(1)}, bf16[2048,512]{1,0:T(8,128)(2,1)}, u32[]{:S(2)}) copy-start(bf16[2048,512]{1,0:T(8,128)(2,1)} %down_ref.1) | copy-start | bytes 6291460
  62.1 20.4 %copy-start.5 = (bf16[512,256]{1,0:T(8,128)(2,1)S(1)}, bf16[512,256]{1,0:T(8,128)(2,1)}, u32[]{:S(2)}) copy-start(bf16[512,256]{1,0:T(8,128)(2,1)} %tq_ref.1) | copy-start | bytes 786436

commit v6 on v5

--- a/solution.py
+++ b/solution.py
@@ -283,7 +283,7 @@
     token_ref[0, 0] = 0
 
 
-def spread_mix(time_mix, side=256, parts=2):
+def spread_mix(time_mix, side=256, parts=1):
     return pl.pallas_call(
         spread_kernel,
         out_shape=[

time: 109 us -> 108 us (level)
  no operation moved by 1% of the time
where the time goes in v6:
time: 108 us
  blocking collectives  58.2 us (54%)
  Pallas kernels  23.5 us (22%)
  starting transfers between devices  14.1 us (13%)
  waiting for transfers between devices  8.39 us (8%)
  local copies, waits for them, and re-layouts  3.02 us (3%)
    all_to_all x1, blocking collectives, shards(): lax.all_to_all(own[0].reshape(groups, share, width), 'tm', 0, 0, tiled=True)  17.6 us
    all_to_all x1, blocking collectives, shards(): lax.all_to_all(copies, 'tm', 0, 0, tiled=True).reshape(points, width)  13.9 us
    all_to_all x1, blocking collectives, shards(): matched = lax.all_to_all(matched, 'tm', 0, 0, tiled=True)  13.3 us
    all_to_all x1, blocking collectives, shards(): lax.all_to_all(refined, 'tm', 0, 0, tiled=True).reshape(points, width)  13.3 us
    pallas_call x1, Pallas kernels, match(): pl.pallas_call(functools.partial(match_kernel, count, block, LOG2E * widt...  7.04 us
    ppermute x3, waiting for transfers between devices, shards(): below = lax.ppermute(below, 'pts', up)  6.71 us
    ppermute x2, starting transfers between devices, shards(): above = lax.ppermute(above, 'pts', down)  6.47 us
    pallas_call x1, Pallas kernels, rematch(): pl.pallas_call(functools.partial(rematch_kernel, marks, block, LOG2E * wi...  6.2 us
  transfers between devices with their start and end apart: 15, of which 5 were waited for; matrix products, arithmetic and copies ran while one was open for 0% of the time, Pallas kernels for 4%

profile of v6, /device:TPU:8, one launch (start us, length us, event | category | flops | bytes accessed | tf_op | source)
XLA Modules:
  0.0 107.9 jit_solution(11606957722964310)
XLA Ops:
  0.6 2.0 %collective-permute-start = (bf16[256,256]{1,0:T(8,128)(2,1)}, bf16[256,256]{1,0:T(8,128)(2,1)S(1)}, u32[]{:S(2)}, u32[]{:S(2)}) collective-permute-start(bf16[256,256]{1,0:T(8,128)(2,1)} %bitcast.11), channel_id=1, source_target_pairs={{0,2},{1,3},{2,4},{3,5},{4,6},{5,7},{6,8},{7,9},{8,10},{9,11},{10,... | collective-permute-start | bytes 393224 | tf_op jit(solution)/shard_map/ppermute | solution.py:402
  2.6 4.0 %collective-permute-start.6 = (bf16[256,256]{1,0:T(8,128)(2,1)}, bf16[256,256]{1,0:T(8,128)(2,1)S(1)}, u32[]{:S(2)}, u32[]{:S(2)}) collective-permute-start(bf16[256,256]{1,0:T(8,128)(2,1)} %bitcast.12), channel_id=1, source_target_pairs={{0,14},{1,15},{2,0},{3,1},{4,2},{5,3},{6,4},{7,5},{8,6},{9,7},{10,... | collective-permute-start | bytes 393224 | tf_op jit(solution)/shard_map/ppermute | solution.py:402
  6.7 0.9 copy-done
  7.6 0.7 copy-done.1
  8.3 0.7 copy-done.2
  9.4 0.9 collective-permute-done.refs_4_.refs_3_
  10.3 3.2 %collective-permute-start.9 = (bf16[256,256]{1,0:T(8,128)(2,1)S(1)}, bf16[256,256]{1,0:T(8,128)(2,1)S(1)}, u32[]{:S(2)}, u32[]{:S(2)}) collective-permute-start(bf16[256,256]{1,0:T(8,128)(2,1)S(1)} %collective-permute-done.6.refs_3_.refs_2_), channel_id=1, source_target_pairs={{0,14},{1,15},{2,0},{3,1},{4,2},{5,3},{6,4},{7,5},{8,6},{9,7},{10,... | collective-permute-start | bytes 393224 | tf_op jit(solution)/shard_map/ppermute | solution.py:407
  13.5 0.5 collective-permute-start.7
  14.0 2.4 %collective-permute-done.1.refs_8_.refs_7_ = bf16[256,256]{1,0:T(8,128)(2,1)S(1)} collective-permute-done((bf16[256,256]{1,0:T(8,128)(2,1)S(1)}, bf16[256,256]{1,0:T(8,128)(2,1)S(1)}, u32[]{:S(2)}, u32[]{:S(2)}) %collective-permute-start.1) | collective-permute-done | bytes 131104 | tf_op jit(solution)/shard_map/ppermute | solution.py:405
  16.5 3.2 %collective-permute-start.12 = (bf16[256,256]{1,0:T(8,128)(2,1)S(1)}, bf16[256,256]{1,0:T(8,128)(2,1)S(1)}, u32[]{:S(2)}, u32[]{:S(2)}) collective-permute-start(bf16[256,256]{1,0:T(8,128)(2,1)S(1)} %collective-permute-done.9.refs_7_.refs_6_), channel_id=1, source_target_pairs={{0,14},{1,15},{2,0},{3,1},{4,2},{5,3},{6,4},{7,5},{8,6},{9,7},{10,... | collective-permute-start | bytes 393224 | tf_op jit(solution)/shard_map/ppermute | solution.py:407
  20.2 0.7 copy-done.6
  20.9 0.5 spread_mix.1
  21.4 1.2 %collective-permute-done.2.refs_12_.refs_14_.refs_11_ = bf16[256,256]{1,0:T(8,128)(2,1)S(1)} collective-permute-done((bf16[256,256]{1,0:T(8,128)(2,1)S(1)}, bf16[256,256]{1,0:T(8,128)(2,1)S(1)}, u32[]{:S(2)}, u32[]{:S(2)}) %collective-permute-start.2) | collective-permute-done | bytes 131104 | tf_op jit(solution)/shard_map/ppermute | solution.py:405
  22.7 2.4 %pick.3 = (bf16[1024,256]{1,0:T(8,128)(2,1)S(1)}, bf16[256,256]{1,0:T(8,128)(2,1)S(1)}, bf16[256,256]{1,0:T(8,128)(2,1)S(1)}) custom-call(s32[1024,128]{1,0:T(8,128)S(1)} %get-tuple-element.11.refs_0_, bf16[256,256]{1,0:T(8,128)(2,1)S(1)} %get-tuple-element.12.refs_1_.refs_0_, bf16[256,256]{1,0:T(8,128)(2,1)S(1)} %collective-permute-done.5.refs_2_.refs_1_, ...), custom_call_target="tpu_custom_call" | custom-call | flops 1610612736 | bytes 1572864 | tf_op jit(solution)/shard_map/pick/pallas_call | solution.py:103
  25.7 3.1 %collective-permute-done.3.refs_3_.refs_14_ = bf16[256,256]{1,0:T(8,128)(2,1)S(1)} collective-permute-done((bf16[256,256]{1,0:T(8,128)(2,1)S(1)}, bf16[256,256]{1,0:T(8,128)(2,1)S(1)}, u32[]{:S(2)}, u32[]{:S(2)}) %collective-permute-start.3) | collective-permute-done | bytes 131104 | tf_op jit(solution)/shard_map/ppermute | solution.py:405
  28.8 0.6 pick.4.refs_2_
  29.4 0.7 collective-permute-done.4.refs_1_.refs_15_
  30.5 17.6 %all_to_all.20.parts_ref = bf16[16,64,256]{2,1,0:T(8,128)(2,1)S(1)} all-to-all(bf16[16,64,256]{2,1,0:T(8,128)(2,1)S(1)} %bitcast.7), channel_id=1, replica_groups=mesh['tm'=16,'pts'=16] {'tm'}, dimensions={0} | all-to-all | bytes 1048576 | tf_op jit(solution)/shard_map/all_to_all | solution.py:422
  48.2 13.9 %all_to_all.21 = bf16[16,64,256]{2,1,0:T(8,128)(2,1)S(1)} all-to-all(bf16[16,64,256]{2,1,0:T(8,128)(2,1)S(1)} %get-tuple-element.17), channel_id=1, replica_groups=mesh['tm'=16,'pts'=16] {'tm'}, dimensions={0} | all-to-all | bytes 1048576 | tf_op jit(solution)/shard_map/all_to_all | solution.py:424
  62.1 7.0 %match.1 = bf16[1024,256]{1,0:T(8,128)(2,1)S(1)} custom-call(bf16[1024,256]{1,0:T(8,128)(2,1)S(1)} %bitcast.9, bf16[256,256]{1,0:T(8,128)(2,1)S(1)} %get-tuple-element.12.refs_1_.refs_0_, bf16[256,256]{1,0:T(8,128)(2,1)S(1)} %collective-permute-done.5.refs_2_.refs_1_, bf16[256,256]{1,0:T(8,128)(2,1)S(1)} %collective-permute-done.6.refs_3_.refs_2_, ...), custom_call_target="tpu_custom_call" | custom-call | flops 4294967296 | bytes 2097152 | tf_op jit(solution)/shard_map/match/pallas_call | solution.py:179
  69.1 13.3 %all_to_all.22.m_ref = bf16[16,64,256]{2,1,0:T(8,128)(2,1)S(1)} all-to-all(bf16[16,64,256]{2,1,0:T(8,128)(2,1)S(1)} %bitcast.10), channel_id=1, replica_groups=mesh['tm'=16,'pts'=16] {'tm'}, dimensions={0} | all-to-all | bytes 1048576 | tf_op jit(solution)/shard_map/all_to_all | solution.py:426
  82.5 5.9 %mixer.1 = bf16[16,64,256]{2,1,0:T(8,128)(2,1)S(1)} custom-call(bf16[16,64,256]{2,1,0:T(8,128)(2,1)S(1)} %all_to_all.22.m_ref, bf16[64,256]{1,0:T(8,128)(2,1)S(1)} %get-tuple-element.18.q_ref, bf16[1,256,256]{2,1,0:T(8,128)(2,1)S(1)} %get-tuple-element.19.mixes_ref, bf16[512,2048]{1,0:T(8,128)(2,1)S(1)} %copy-done.3, bf16[2048,512]{1,0:T(8,128)(2,1)S(1)} %copy-done.4, ...), custom_call_target="tpu_custom_call" | custom-call | flops 4294967296 | bytes 4194304 | tf_op jit(solution)/shard_map/mixer/pallas_call | solution.py:353
  88.4 13.3 %all_to_all.23 = bf16[16,64,256]{2,1,0:T(8,128)(2,1)S(1)} all-to-all(bf16[16,64,256]{2,1,0:T(8,128)(2,1)S(1)} %mixer.1), channel_id=1, replica_groups=mesh['tm'=16,'pts'=16] {'tm'}, dimensions={0} | all-to-all | bytes 1048576 | tf_op jit(solution)/shard_map/all_to_all | solution.py:428
  101.7 6.2 %rematch.1 = (f32[1,1024]{1,0:T(1,128)}, f32[1,1024]{1,0:T(1,128)}) custom-call(bf16[1024,256]{1,0:T(8,128)(2,1)S(1)} %bitcast.8, bf16[256,256]{1,0:T(8,128)(2,1)S(1)} %get-tuple-element.12.refs_1_.refs_0_, bf16[256,256]{1,0:T(8,128)(2,1)S(1)} %collective-permute-done.5.refs_2_.refs_1_, bf16[256,256]{1,0:T(8,128)(2,1)S(1)} %collective-permute-done.6.refs_3_.refs_2_, ...), custom_call_target="tpu_custom_call" | custom-call | flops 2147483648 | bytes 2097152 | tf_op jit(solution)/shard_map/rematch/pallas_call | solution.py:254
  (33 shorter events, 1.9 us)
Async XLA Ops:
  0.6 9.6 %collective-permute-start = (bf16[256,256]{1,0:T(8,128)(2,1)}, bf16[256,256]{1,0:T(8,128)(2,1)S(1)}, u32[]{:S(2)}, u32[]{:S(2)}) collective-permute-start(bf16[256,256]{1,0:T(8,128)(2,1)} %bitcast.11), channel_id=1, source_target_pairs={{0,2},{1,3},{2,4},{3,5},{4,6},{5,7},{6,8},{7,9},{8,10},{9,11},{10,... | collective-permute-start | bytes 393224 | tf_op jit(solution)/shard_map/ppermute | solution.py:402
  2.6 7.7 %collective-permute-start.6 = (bf16[256,256]{1,0:T(8,128)(2,1)}, bf16[256,256]{1,0:T(8,128)(2,1)S(1)}, u32[]{:S(2)}, u32[]{:S(2)}) collective-permute-start(bf16[256,256]{1,0:T(8,128)(2,1)} %bitcast.12), channel_id=1, source_target_pairs={{0,14},{1,15},{2,0},{3,1},{4,2},{5,3},{6,4},{7,5},{8,6},{9,7},{10,... | collective-permute-start | bytes 393224 | tf_op jit(solution)/shard_map/ppermute | solution.py:402
  6.7 0.9 copy-start
  7.6 0.7 copy-start.1
  8.3 0.7 copy-start.2
  10.3 6.2 %collective-permute-start.1 = (bf16[256,256]{1,0:T(8,128)(2,1)S(1)}, bf16[256,256]{1,0:T(8,128)(2,1)S(1)}, u32[]{:S(2)}, u32[]{:S(2)}) collective-permute-start(bf16[256,256]{1,0:T(8,128)(2,1)S(1)} %collective-permute-done.refs_4_.refs_3_), channel_id=1, source_target_pairs={{0,2},{1,3},{2,4},{3,5},{4,6},{5,7},{6,8},{7,9},{8,10},{9,11},{10,... | collective-permute-start | bytes 393224 | tf_op jit(solution)/shard_map/ppermute | solution.py:405
  10.3 6.2 %collective-permute-start.9 = (bf16[256,256]{1,0:T(8,128)(2,1)S(1)}, bf16[256,256]{1,0:T(8,128)(2,1)S(1)}, u32[]{:S(2)}, u32[]{:S(2)}) collective-permute-start(bf16[256,256]{1,0:T(8,128)(2,1)S(1)} %collective-permute-done.6.refs_3_.refs_2_), channel_id=1, source_target_pairs={{0,14},{1,15},{2,0},{3,1},{4,2},{5,3},{6,4},{7,5},{8,6},{9,7},{10,... | collective-permute-start | bytes 393224 | tf_op jit(solution)/shard_map/ppermute | solution.py:407
  13.5 6.2 %collective-permute-start.5 = (bf16[256,256]{1,0:T(8,128)(2,1)S(1)}, bf16[256,256]{1,0:T(8,128)(2,1)S(1)}, u32[]{:S(2)}, u32[]{:S(2)}) collective-permute-start(bf16[256,256]{1,0:T(8,128)(2,1)S(1)} %get-tuple-element.12.refs_1_.refs_0_), channel_id=1, source_target_pairs={{0,1},{1,0},{2,3},{3,2},{4,5},{5,4},{6,7},{7,6},{8,9},{9,8},{10,11... | collective-permute-start | bytes 393224 | tf_op jit(solution)/shard_map/ppermute | solution.py:398
  13.5 6.2 %collective-permute-start.7 = (bf16[256,256]{1,0:T(8,128)(2,1)S(1)}, bf16[256,256]{1,0:T(8,128)(2,1)S(1)}, u32[]{:S(2)}, u32[]{:S(2)}) collective-permute-start(bf16[256,256]{1,0:T(8,128)(2,1)S(1)} %collective-permute-done.6.refs_3_.refs_2_), channel_id=1, source_target_pairs={{0,1},{1,0},{2,3},{3,2},{4,5},{5,4},{6,7},{7,6},{8,9},{9,8},{10,11... | collective-permute-start | bytes 393224 | tf_op jit(solution)/shard_map/ppermute | solution.py:398
  14.0 8.6 %collective-permute-start.8 = (bf16[256,256]{1,0:T(8,128)(2,1)S(1)}, bf16[256,256]{1,0:T(8,128)(2,1)S(1)}, u32[]{:S(2)}, u32[]{:S(2)}) collective-permute-start(bf16[256,256]{1,0:T(8,128)(2,1)S(1)} %collective-permute-done.refs_4_.refs_3_), channel_id=1, source_target_pairs={{0,1},{1,0},{2,3},{3,2},{4,5},{5,4},{6,7},{7,6},{8,9},{9,8},{10,11... | collective-permute-start | bytes 393224 | tf_op jit(solution)/shard_map/ppermute | solution.py:398
  16.4 6.2 %collective-permute-start.2 = (bf16[256,256]{1,0:T(8,128)(2,1)S(1)}, bf16[256,256]{1,0:T(8,128)(2,1)S(1)}, u32[]{:S(2)}, u32[]{:S(2)}) collective-permute-start(bf16[256,256]{1,0:T(8,128)(2,1)S(1)} %collective-permute-done.1.refs_8_.refs_7_), channel_id=1, source_target_pairs={{0,2},{1,3},{2,4},{3,5},{4,6},{5,7},{6,8},{7,9},{8,10},{9,11},{10,... | collective-permute-start | bytes 393224 | tf_op jit(solution)/shard_map/ppermute | solution.py:405
  16.5 6.2 %collective-permute-start.12 = (bf16[256,256]{1,0:T(8,128)(2,1)S(1)}, bf16[256,256]{1,0:T(8,128)(2,1)S(1)}, u32[]{:S(2)}, u32[]{:S(2)}) collective-permute-start(bf16[256,256]{1,0:T(8,128)(2,1)S(1)} %collective-permute-done.9.refs_7_.refs_6_), channel_id=1, source_target_pairs={{0,14},{1,15},{2,0},{3,1},{4,2},{5,3},{6,4},{7,5},{8,6},{9,7},{10,... | collective-permute-start | bytes 393224 | tf_op jit(solution)/shard_map/ppermute | solution.py:407
  19.7 3.0 %collective-permute-start.10 = (bf16[256,256]{1,0:T(8,128)(2,1)S(1)}, bf16[256,256]{1,0:T(8,128)(2,1)S(1)}, u32[]{:S(2)}, u32[]{:S(2)}) collective-permute-start(bf16[256,256]{1,0:T(8,128)(2,1)S(1)} %collective-permute-done.9.refs_7_.refs_6_), channel_id=1, source_target_pairs={{0,1},{1,0},{2,3},{3,2},{4,5},{5,4},{6,7},{7,6},{8,9},{9,8},{10,11... | collective-permute-start | bytes 393224 | tf_op jit(solution)/shard_map/ppermute | solution.py:398
  19.7 3.0 %collective-permute-start.11 = (bf16[256,256]{1,0:T(8,128)(2,1)S(1)}, bf16[256,256]{1,0:T(8,128)(2,1)S(1)}, u32[]{:S(2)}, u32[]{:S(2)}) collective-permute-start(bf16[256,256]{1,0:T(8,128)(2,1)S(1)} %collective-permute-done.1.refs_8_.refs_7_), channel_id=1, source_target_pairs={{0,1},{1,0},{2,3},{3,2},{4,5},{5,4},{6,7},{7,6},{8,9},{9,8},{10,11... | collective-permute-start | bytes 393224 | tf_op jit(solution)/shard_map/ppermute | solution.py:398
  20.2 0.7 copy-start.6
  22.6 6.2 %collective-permute-start.3 = (bf16[256,256]{1,0:T(8,128)(2,1)S(1)}, bf16[256,256]{1,0:T(8,128)(2,1)S(1)}, u32[]{:S(2)}, u32[]{:S(2)}) collective-permute-start(bf16[256,256]{1,0:T(8,128)(2,1)S(1)} %collective-permute-done.2.refs_12_.refs_14_.refs_11_), channel_id=1, source_target_pairs={{0,2},{1,3},{2,4},{3,5},{4,6},{5,7},{6,8},{7,9},{8,10},{9,11},{10,... | collective-permute-start | bytes 393224 | tf_op jit(solution)/shard_map/ppermute | solution.py:405
  25.1 3.7 %collective-permute-start.13 = (bf16[256,256]{1,0:T(8,128)(2,1)S(1)}, bf16[256,256]{1,0:T(8,128)(2,1)S(1)}, u32[]{:S(2)}, u32[]{:S(2)}) collective-permute-start(bf16[256,256]{1,0:T(8,128)(2,1)S(1)} %get-tuple-element.14), channel_id=1, source_target_pairs={{0,1},{1,0},{2,3},{3,2},{4,5},{5,4},{6,7},{7,6},{8,9},{9,8},{10,11... | collective-permute-start | bytes 393224 | tf_op jit(solution)/shard_map/ppermute | solution.py:398
  25.2 3.6 %collective-permute-start.14 = (bf16[256,256]{1,0:T(8,128)(2,1)S(1)}, bf16[256,256]{1,0:T(8,128)(2,1)S(1)}, u32[]{:S(2)}, u32[]{:S(2)}) collective-permute-start(bf16[256,256]{1,0:T(8,128)(2,1)S(1)} %get-tuple-element.15), channel_id=1, source_target_pairs={{0,1},{1,0},{2,3},{3,2},{4,5},{5,4},{6,7},{7,6},{8,9},{9,8},{10,11... | collective-permute-start | bytes 393224 | tf_op jit(solution)/shard_map/ppermute | solution.py:398
  28.8 1.3 %collective-permute-start.4 = (bf16[256,256]{1,0:T(8,128)(2,1)S(1)}, bf16[256,256]{1,0:T(8,128)(2,1)S(1)}, u32[]{:S(2)}, u32[]{:S(2)}) collective-permute-start(bf16[256,256]{1,0:T(8,128)(2,1)S(1)} %collective-permute-done.3.refs_3_.refs_14_), channel_id=1, source_target_pairs={{0,1},{1,0},{2,3},{3,2},{4,5},{5,4},{6,7},{7,6},{8,9},{9,8},{10,11... | collective-permute-start | bytes 393224 | tf_op jit(solution)/shard_map/ppermute | solution.py:398
  62.1 20.4 %copy-start.3 = (bf16[512,2048]{1,0:T(8,128)(2,1)S(1)}, bf16[512,2048]{1,0:T(8,128)(2,1)}, u32[]{:S(2)}) copy-start(bf16[512,2048]{1,0:T(8,128)(2,1)} %up_ref.1) | copy-start | bytes 6291460
  62.1 20.4 %copy-start.4 = (bf16[2048,512]{1,0:T(8,128)(2,1)S(1)}, bf16[2048,512]{1,0:T(8,128)(2,1)}, u32[]{:S(2)}) copy-start(bf16[2048,512]{1,0:T(8,128)(2,1)} %down_ref.1) | copy-start | bytes 6291460
  62.1 20.4 %copy-start.5 = (bf16[512,256]{1,0:T(8,128)(2,1)S(1)}, bf16[512,256]{1,0:T(8,128)(2,1)}, u32[]{:S(2)}) copy-start(bf16[512,256]{1,0:T(8,128)(2,1)} %tq_ref.1) | copy-start | bytes 786436

commit v7 on v6

--- a/solution.py
+++ b/solution.py
@@ -315,13 +315,12 @@
         scale = lax.rsqrt(power + 1e-06)
         wide = jnp.broadcast_to(scale, (side, 128))
         high = wide.astype(jnp.bfloat16)
-        low = (wide - high.astype(jnp.float32)).astype(jnp.bfloat16)
-        normed = jnp.concatenate([(matched * scale).astype(jnp.bfloat16), high, low], axis=1)
+        normed = jnp.concatenate([(matched * scale).astype(jnp.bfloat16), high], axis=1)
         blend = jnp.dot(mixes_ref[0], normed, preferred_element_type=jnp.float32)
         for part in range(1, mixes_ref.shape[0]):
             blend = blend + jnp.dot(mixes_ref[part], normed, preferred_element_type=jnp.float32)
         section = (matched + blend[:, :width]).astype(jnp.bfloat16).astype(jnp.float32)
-        times = 1.0 + blend[:, width : width + 128] + blend[:, width + 128 :]
+        times = 1.0 + blend[:, width:]
         power = (
             jnp.sum(section * section, axis=1, keepdims=True) + times * times * square
         ) * (0.5 / width)

time: 108 us -> 108 us (level)
  no operation moved by 1% of the time
where the time goes in v7:
time: 108 us
  blocking collectives  58.2 us (54%)
  Pallas kernels  23.4 us (22%)
  starting transfers between devices  14.1 us (13%)
  waiting for transfers between devices  8.39 us (8%)
  local copies, waits for them, and re-layouts  3.02 us (3%)
    all_to_all x1, blocking collectives, shards(): lax.all_to_all(own[0].reshape(groups, share, width), 'tm', 0, 0, tiled=True)  17.6 us
    all_to_all x1, blocking collectives, shards(): lax.all_to_all(copies, 'tm', 0, 0, tiled=True).reshape(points, width)  13.9 us
    all_to_all x1, blocking collectives, shards(): matched = lax.all_to_all(matched, 'tm', 0, 0, tiled=True)  13.3 us
    all_to_all x1, blocking collectives, shards(): lax.all_to_all(refined, 'tm', 0, 0, tiled=True).reshape(points, width)  13.3 us
    pallas_call x1, Pallas kernels, match(): pl.pallas_call(functools.partial(match_kernel, count, block, LOG2E * widt...  7.04 us
    ppermute x3, waiting for transfers between devices, shards(): below = lax.ppermute(below, 'pts', up)  6.71 us
    ppermute x2, starting transfers between devices, shards(): above = lax.ppermute(above, 'pts', down)  6.47 us
    pallas_call x1, Pallas kernels, rematch(): pl.pallas_call(functools.partial(rematch_kernel, marks, block, LOG2E * wi...  6.2 us
  transfers between devices with their start and end apart: 15, of which 5 were waited for; matrix products, arithmetic and copies ran while one was open for 0% of the time, Pallas kernels for 4%

profile of v7, /device:TPU:8, one launch (start us, length us, event | category | flops | bytes accessed | tf_op | source)
XLA Modules:
  0.0 107.9 jit_solution(1339968769958611932)
XLA Ops:
  0.6 2.0 %collective-permute-start = (bf16[256,256]{1,0:T(8,128)(2,1)}, bf16[256,256]{1,0:T(8,128)(2,1)S(1)}, u32[]{:S(2)}, u32[]{:S(2)}) collective-permute-start(bf16[256,256]{1,0:T(8,128)(2,1)} %bitcast.11), channel_id=1, source_target_pairs={{0,2},{1,3},{2,4},{3,5},{4,6},{5,7},{6,8},{7,9},{8,10},{9,11},{10,... | collective-permute-start | bytes 393224 | tf_op jit(solution)/shard_map/ppermute | solution.py:401
  2.6 4.0 %collective-permute-start.6 = (bf16[256,256]{1,0:T(8,128)(2,1)}, bf16[256,256]{1,0:T(8,128)(2,1)S(1)}, u32[]{:S(2)}, u32[]{:S(2)}) collective-permute-start(bf16[256,256]{1,0:T(8,128)(2,1)} %bitcast.12), channel_id=1, source_target_pairs={{0,14},{1,15},{2,0},{3,1},{4,2},{5,3},{6,4},{7,5},{8,6},{9,7},{10,... | collective-permute-start | bytes 393224 | tf_op jit(solution)/shard_map/ppermute | solution.py:401
  6.7 0.9 copy-done
  7.6 0.7 copy-done.1
  8.3 0.7 copy-done.2
  9.4 0.9 collective-permute-done.refs_4_.refs_3_
  10.3 3.2 %collective-permute-start.9 = (bf16[256,256]{1,0:T(8,128)(2,1)S(1)}, bf16[256,256]{1,0:T(8,128)(2,1)S(1)}, u32[]{:S(2)}, u32[]{:S(2)}) collective-permute-start(bf16[256,256]{1,0:T(8,128)(2,1)S(1)} %collective-permute-done.6.refs_3_.refs_2_), channel_id=1, source_target_pairs={{0,14},{1,15},{2,0},{3,1},{4,2},{5,3},{6,4},{7,5},{8,6},{9,7},{10,... | collective-permute-start | bytes 393224 | tf_op jit(solution)/shard_map/ppermute | solution.py:406
  13.5 0.5 collective-permute-start.7
  14.0 2.4 %collective-permute-done.1.refs_8_.refs_7_ = bf16[256,256]{1,0:T(8,128)(2,1)S(1)} collective-permute-done((bf16[256,256]{1,0:T(8,128)(2,1)S(1)}, bf16[256,256]{1,0:T(8,128)(2,1)S(1)}, u32[]{:S(2)}, u32[]{:S(2)}) %collective-permute-start.1) | collective-permute-done | bytes 131104 | tf_op jit(solution)/shard_map/ppermute | solution.py:404
  16.5 3.2 %collective-permute-start.12 = (bf16[256,256]{1,0:T(8,128)(2,1)S(1)}, bf16[256,256]{1,0:T(8,128)(2,1)S(1)}, u32[]{:S(2)}, u32[]{:S(2)}) collective-permute-start(bf16[256,256]{1,0:T(8,128)(2,1)S(1)} %collective-permute-done.9.refs_7_.refs_6_), channel_id=1, source_target_pairs={{0,14},{1,15},{2,0},{3,1},{4,2},{5,3},{6,4},{7,5},{8,6},{9,7},{10,... | collective-permute-start | bytes 393224 | tf_op jit(solution)/shard_map/ppermute | solution.py:406
  20.2 0.7 copy-done.6
  20.9 0.5 spread_mix.1
  21.4 1.2 %collective-permute-done.2.refs_12_.refs_14_.refs_11_ = bf16[256,256]{1,0:T(8,128)(2,1)S(1)} collective-permute-done((bf16[256,256]{1,0:T(8,128)(2,1)S(1)}, bf16[256,256]{1,0:T(8,128)(2,1)S(1)}, u32[]{:S(2)}, u32[]{:S(2)}) %collective-permute-start.2) | collective-permute-done | bytes 131104 | tf_op jit(solution)/shard_map/ppermute | solution.py:404
  22.7 2.4 %pick.3 = (bf16[1024,256]{1,0:T(8,128)(2,1)S(1)}, bf16[256,256]{1,0:T(8,128)(2,1)S(1)}, bf16[256,256]{1,0:T(8,128)(2,1)S(1)}) custom-call(s32[1024,128]{1,0:T(8,128)S(1)} %get-tuple-element.11.refs_0_, bf16[256,256]{1,0:T(8,128)(2,1)S(1)} %get-tuple-element.12.refs_1_.refs_0_, bf16[256,256]{1,0:T(8,128)(2,1)S(1)} %collective-permute-done.5.refs_2_.refs_1_, ...), custom_call_target="tpu_custom_call" | custom-call | flops 1610612736 | bytes 1572864 | tf_op jit(solution)/shard_map/pick/pallas_call | solution.py:103
  25.7 3.1 %collective-permute-done.3.refs_3_.refs_14_ = bf16[256,256]{1,0:T(8,128)(2,1)S(1)} collective-permute-done((bf16[256,256]{1,0:T(8,128)(2,1)S(1)}, bf16[256,256]{1,0:T(8,128)(2,1)S(1)}, u32[]{:S(2)}, u32[]{:S(2)}) %collective-permute-start.3) | collective-permute-done | bytes 131104 | tf_op jit(solution)/shard_map/ppermute | solution.py:404
  28.8 0.6 pick.4.refs_2_
  29.4 0.7 collective-permute-done.4.refs_1_.refs_15_
  30.5 17.6 %all_to_all.20.parts_ref = bf16[16,64,256]{2,1,0:T(8,128)(2,1)S(1)} all-to-all(bf16[16,64,256]{2,1,0:T(8,128)(2,1)S(1)} %bitcast.7), channel_id=1, replica_groups=mesh['tm'=16,'pts'=16] {'tm'}, dimensions={0} | all-to-all | bytes 1048576 | tf_op jit(solution)/shard_map/all_to_all | solution.py:421
  48.2 13.9 %all_to_all.21 = bf16[16,64,256]{2,1,0:T(8,128)(2,1)S(1)} all-to-all(bf16[16,64,256]{2,1,0:T(8,128)(2,1)S(1)} %get-tuple-element.17), channel_id=1, replica_groups=mesh['tm'=16,'pts'=16] {'tm'}, dimensions={0} | all-to-all | bytes 1048576 | tf_op jit(solution)/shard_map/all_to_all | solution.py:423
  62.1 7.0 %match.1 = bf16[1024,256]{1,0:T(8,128)(2,1)S(1)} custom-call(bf16[1024,256]{1,0:T(8,128)(2,1)S(1)} %bitcast.9, bf16[256,256]{1,0:T(8,128)(2,1)S(1)} %get-tuple-element.12.refs_1_.refs_0_, bf16[256,256]{1,0:T(8,128)(2,1)S(1)} %collective-permute-done.5.refs_2_.refs_1_, bf16[256,256]{1,0:T(8,128)(2,1)S(1)} %collective-permute-done.6.refs_3_.refs_2_, ...), custom_call_target="tpu_custom_call" | custom-call | flops 4294967296 | bytes 2097152 | tf_op jit(solution)/shard_map/match/pallas_call | solution.py:179
  69.1 13.3 %all_to_all.22.m_ref = bf16[16,64,256]{2,1,0:T(8,128)(2,1)S(1)} all-to-all(bf16[16,64,256]{2,1,0:T(8,128)(2,1)S(1)} %bitcast.10), channel_id=1, replica_groups=mesh['tm'=16,'pts'=16] {'tm'}, dimensions={0} | all-to-all | bytes 1048576 | tf_op jit(solution)/shard_map/all_to_all | solution.py:425
  82.5 5.9 %mixer.1 = bf16[16,64,256]{2,1,0:T(8,128)(2,1)S(1)} custom-call(bf16[16,64,256]{2,1,0:T(8,128)(2,1)S(1)} %all_to_all.22.m_ref, bf16[64,256]{1,0:T(8,128)(2,1)S(1)} %get-tuple-element.18.q_ref, bf16[1,256,256]{2,1,0:T(8,128)(2,1)S(1)} %get-tuple-element.19.mixes_ref, bf16[512,2048]{1,0:T(8,128)(2,1)S(1)} %copy-done.3, bf16[2048,512]{1,0:T(8,128)(2,1)S(1)} %copy-done.4, ...), custom_call_target="tpu_custom_call" | custom-call | flops 4294967296 | bytes 4194304 | tf_op jit(solution)/shard_map/mixer/pallas_call | solution.py:352
  88.4 13.3 %all_to_all.23 = bf16[16,64,256]{2,1,0:T(8,128)(2,1)S(1)} all-to-all(bf16[16,64,256]{2,1,0:T(8,128)(2,1)S(1)} %mixer.1), channel_id=1, replica_groups=mesh['tm'=16,'pts'=16] {'tm'}, dimensions={0} | all-to-all | bytes 1048576 | tf_op jit(solution)/shard_map/all_to_all | solution.py:427
  101.7 6.2 %rematch.1 = (f32[1,1024]{1,0:T(1,128)}, f32[1,1024]{1,0:T(1,128)}) custom-call(bf16[1024,256]{1,0:T(8,128)(2,1)S(1)} %bitcast.8, bf16[256,256]{1,0:T(8,128)(2,1)S(1)} %get-tuple-element.12.refs_1_.refs_0_, bf16[256,256]{1,0:T(8,128)(2,1)S(1)} %collective-permute-done.5.refs_2_.refs_1_, bf16[256,256]{1,0:T(8,128)(2,1)S(1)} %collective-permute-done.6.refs_3_.refs_2_, ...), custom_call_target="tpu_custom_call" | custom-call | flops 2147483648 | bytes 2097152 | tf_op jit(solution)/shard_map/rematch/pallas_call | solution.py:254
  (33 shorter events, 1.9 us)
Async XLA Ops:
  0.6 9.6 %collective-permute-start = (bf16[256,256]{1,0:T(8,128)(2,1)}, bf16[256,256]{1,0:T(8,128)(2,1)S(1)}, u32[]{:S(2)}, u32[]{:S(2)}) collective-permute-start(bf16[256,256]{1,0:T(8,128)(2,1)} %bitcast.11), channel_id=1, source_target_pairs={{0,2},{1,3},{2,4},{3,5},{4,6},{5,7},{6,8},{7,9},{8,10},{9,11},{10,... | collective-permute-start | bytes 393224 | tf_op jit(solution)/shard_map/ppermute | solution.py:401
  2.6 7.7 %collective-permute-start.6 = (bf16[256,256]{1,0:T(8,128)(2,1)}, bf16[256,256]{1,0:T(8,128)(2,1)S(1)}, u32[]{:S(2)}, u32[]{:S(2)}) collective-permute-start(bf16[256,256]{1,0:T(8,128)(2,1)} %bitcast.12), channel_id=1, source_target_pairs={{0,14},{1,15},{2,0},{3,1},{4,2},{5,3},{6,4},{7,5},{8,6},{9,7},{10,... | collective-permute-start | bytes 393224 | tf_op jit(solution)/shard_map/ppermute | solution.py:401
  6.7 0.9 copy-start
  7.6 0.7 copy-start.1
  8.3 0.7 copy-start.2
  10.3 6.2 %collective-permute-start.1 = (bf16[256,256]{1,0:T(8,128)(2,1)S(1)}, bf16[256,256]{1,0:T(8,128)(2,1)S(1)}, u32[]{:S(2)}, u32[]{:S(2)}) collective-permute-start(bf16[256,256]{1,0:T(8,128)(2,1)S(1)} %collective-permute-done.refs_4_.refs_3_), channel_id=1, source_target_pairs={{0,2},{1,3},{2,4},{3,5},{4,6},{5,7},{6,8},{7,9},{8,10},{9,11},{10,... | collective-permute-start | bytes 393224 | tf_op jit(solution)/shard_map/ppermute | solution.py:404
  10.3 6.2 %collective-permute-start.9 = (bf16[256,256]{1,0:T(8,128)(2,1)S(1)}, bf16[256,256]{1,0:T(8,128)(2,1)S(1)}, u32[]{:S(2)}, u32[]{:S(2)}) collective-permute-start(bf16[256,256]{1,0:T(8,128)(2,1)S(1)} %collective-permute-done.6.refs_3_.refs_2_), channel_id=1, source_target_pairs={{0,14},{1,15},{2,0},{3,1},{4,2},{5,3},{6,4},{7,5},{8,6},{9,7},{10,... | collective-permute-start | bytes 393224 | tf_op jit(solution)/shard_map/ppermute | solution.py:406
  13.5 6.2 %collective-permute-start.5 = (bf16[256,256]{1,0:T(8,128)(2,1)S(1)}, bf16[256,256]{1,0:T(8,128)(2,1)S(1)}, u32[]{:S(2)}, u32[]{:S(2)}) collective-permute-start(bf16[256,256]{1,0:T(8,128)(2,1)S(1)} %get-tuple-element.12.refs_1_.refs_0_), channel_id=1, source_target_pairs={{0,1},{1,0},{2,3},{3,2},{4,5},{5,4},{6,7},{7,6},{8,9},{9,8},{10,11... | collective-permute-start | bytes 393224 | tf_op jit(solution)/shard_map/ppermute | solution.py:397
  13.5 6.2 %collective-permute-start.7 = (bf16[256,256]{1,0:T(8,128)(2,1)S(1)}, bf16[256,256]{1,0:T(8,128)(2,1)S(1)}, u32[]{:S(2)}, u32[]{:S(2)}) collective-permute-start(bf16[256,256]{1,0:T(8,128)(2,1)S(1)} %collective-permute-done.6.refs_3_.refs_2_), channel_id=1, source_target_pairs={{0,1},{1,0},{2,3},{3,2},{4,5},{5,4},{6,7},{7,6},{8,9},{9,8},{10,11... | collective-permute-start | bytes 393224 | tf_op jit(solution)/shard_map/ppermute | solution.py:397
  14.0 8.6 %collective-permute-start.8 = (bf16[256,256]{1,0:T(8,128)(2,1)S(1)}, bf16[256,256]{1,0:T(8,128)(2,1)S(1)}, u32[]{:S(2)}, u32[]{:S(2)}) collective-permute-start(bf16[256,256]{1,0:T(8,128)(2,1)S(1)} %collective-permute-done.refs_4_.refs_3_), channel_id=1, source_target_pairs={{0,1},{1,0},{2,3},{3,2},{4,5},{5,4},{6,7},{7,6},{8,9},{9,8},{10,11... | collective-permute-start | bytes 393224 | tf_op jit(solution)/shard_map/ppermute | solution.py:397
  16.4 6.2 %collective-permute-start.2 = (bf16[256,256]{1,0:T(8,128)(2,1)S(1)}, bf16[256,256]{1,0:T(8,128)(2,1)S(1)}, u32[]{:S(2)}, u32[]{:S(2)}) collective-permute-start(bf16[256,256]{1,0:T(8,128)(2,1)S(1)} %collective-permute-done.1.refs_8_.refs_7_), channel_id=1, source_target_pairs={{0,2},{1,3},{2,4},{3,5},{4,6},{5,7},{6,8},{7,9},{8,10},{9,11},{10,... | collective-permute-start | bytes 393224 | tf_op jit(solution)/shard_map/ppermute | solution.py:404
  16.5 6.2 %collective-permute-start.12 = (bf16[256,256]{1,0:T(8,128)(2,1)S(1)}, bf16[256,256]{1,0:T(8,128)(2,1)S(1)}, u32[]{:S(2)}, u32[]{:S(2)}) collective-permute-start(bf16[256,256]{1,0:T(8,128)(2,1)S(1)} %collective-permute-done.9.refs_7_.refs_6_), channel_id=1, source_target_pairs={{0,14},{1,15},{2,0},{3,1},{4,2},{5,3},{6,4},{7,5},{8,6},{9,7},{10,... | collective-permute-start | bytes 393224 | tf_op jit(solution)/shard_map/ppermute | solution.py:406
  19.7 3.0 %collective-permute-start.10 = (bf16[256,256]{1,0:T(8,128)(2,1)S(1)}, bf16[256,256]{1,0:T(8,128)(2,1)S(1)}, u32[]{:S(2)}, u32[]{:S(2)}) collective-permute-start(bf16[256,256]{1,0:T(8,128)(2,1)S(1)} %collective-permute-done.9.refs_7_.refs_6_), channel_id=1, source_target_pairs={{0,1},{1,0},{2,3},{3,2},{4,5},{5,4},{6,7},{7,6},{8,9},{9,8},{10,11... | collective-permute-start | bytes 393224 | tf_op jit(solution)/shard_map/ppermute | solution.py:397
  19.7 3.0 %collective-permute-start.11 = (bf16[256,256]{1,0:T(8,128)(2,1)S(1)}, bf16[256,256]{1,0:T(8,128)(2,1)S(1)}, u32[]{:S(2)}, u32[]{:S(2)}) collective-permute-start(bf16[256,256]{1,0:T(8,128)(2,1)S(1)} %collective-permute-done.1.refs_8_.refs_7_), channel_id=1, source_target_pairs={{0,1},{1,0},{2,3},{3,2},{4,5},{5,4},{6,7},{7,6},{8,9},{9,8},{10,11... | collective-permute-start | bytes 393224 | tf_op jit(solution)/shard_map/ppermute | solution.py:397
  20.2 0.7 copy-start.6
  22.6 6.2 %collective-permute-start.3 = (bf16[256,256]{1,0:T(8,128)(2,1)S(1)}, bf16[256,256]{1,0:T(8,128)(2,1)S(1)}, u32[]{:S(2)}, u32[]{:S(2)}) collective-permute-start(bf16[256,256]{1,0:T(8,128)(2,1)S(1)} %collective-permute-done.2.refs_12_.refs_14_.refs_11_), channel_id=1, source_target_pairs={{0,2},{1,3},{2,4},{3,5},{4,6},{5,7},{6,8},{7,9},{8,10},{9,11},{10,... | collective-permute-start | bytes 393224 | tf_op jit(solution)/shard_map/ppermute | solution.py:404
  25.1 3.7 %collective-permute-start.13 = (bf16[256,256]{1,0:T(8,128)(2,1)S(1)}, bf16[256,256]{1,0:T(8,128)(2,1)S(1)}, u32[]{:S(2)}, u32[]{:S(2)}) collective-permute-start(bf16[256,256]{1,0:T(8,128)(2,1)S(1)} %get-tuple-element.14), channel_id=1, source_target_pairs={{0,1},{1,0},{2,3},{3,2},{4,5},{5,4},{6,7},{7,6},{8,9},{9,8},{10,11... | collective-permute-start | bytes 393224 | tf_op jit(solution)/shard_map/ppermute | solution.py:397
  25.2 3.6 %collective-permute-start.14 = (bf16[256,256]{1,0:T(8,128)(2,1)S(1)}, bf16[256,256]{1,0:T(8,128)(2,1)S(1)}, u32[]{:S(2)}, u32[]{:S(2)}) collective-permute-start(bf16[256,256]{1,0:T(8,128)(2,1)S(1)} %get-tuple-element.15), channel_id=1, source_target_pairs={{0,1},{1,0},{2,3},{3,2},{4,5},{5,4},{6,7},{7,6},{8,9},{9,8},{10,11... | collective-permute-start | bytes 393224 | tf_op jit(solution)/shard_map/ppermute | solution.py:397
  28.8 1.3 %collective-permute-start.4 = (bf16[256,256]{1,0:T(8,128)(2,1)S(1)}, bf16[256,256]{1,0:T(8,128)(2,1)S(1)}, u32[]{:S(2)}, u32[]{:S(2)}) collective-permute-start(bf16[256,256]{1,0:T(8,128)(2,1)S(1)} %collective-permute-done.3.refs_3_.refs_14_), channel_id=1, source_target_pairs={{0,1},{1,0},{2,3},{3,2},{4,5},{5,4},{6,7},{7,6},{8,9},{9,8},{10,11... | collective-permute-start | bytes 393224 | tf_op jit(solution)/shard_map/ppermute | solution.py:397
  62.1 20.4 %copy-start.3 = (bf16[512,2048]{1,0:T(8,128)(2,1)S(1)}, bf16[512,2048]{1,0:T(8,128)(2,1)}, u32[]{:S(2)}) copy-start(bf16[512,2048]{1,0:T(8,128)(2,1)} %up_ref.1) | copy-start | bytes 6291460
  62.1 20.4 %copy-start.4 = (bf16[2048,512]{1,0:T(8,128)(2,1)S(1)}, bf16[2048,512]{1,0:T(8,128)(2,1)}, u32[]{:S(2)}) copy-start(bf16[2048,512]{1,0:T(8,128)(2,1)} %down_ref.1) | copy-start | bytes 6291460
  62.1 20.4 %copy-start.5 = (bf16[512,256]{1,0:T(8,128)(2,1)S(1)}, bf16[512,256]{1,0:T(8,128)(2,1)}, u32[]{:S(2)}) copy-start(bf16[512,256]{1,0:T(8,128)(2,1)} %tq_ref.1) | copy-start | bytes 786436
